TPU v7x, 256 devices: a whole 4x4x8 slice. The times are simulated.
256 devices in a mesh: rep: 32 (over x_lo, z, core), fsdp: 8 (over y, x_hi).
Axes of the slice: x: 4 (x_hi: 2, x_lo: 2; x = x_hi * 2 + x_lo), y: 4, z: 8, core: 2. Of those that a mesh axis runs over, the one named last changes fastest.
Arguments:
- activations: bfloat16 [32, 3072, 8192], P('rep', 'fsdp'), may hold values from -6 to 6
- norm_gain: float32 [8192], replicated, may hold values from 0.1 to 1.9
- key_weight: bfloat16 [32, 8192, 512], P('rep', 'fsdp'), may hold values from -0.03125 to 0.03125
- key_target: bfloat16 [32, 3072, 512], P('rep', 'fsdp'), may hold values from -1.5 to 1.5
- replica_frag: bfloat16 [32, 8192, 1024], P('rep', 'fsdp'), may hold values from -1.5 to 1.5
- outer_params: float32 [8192, 1024], P(('fsdp', 'rep')), may hold values from -1.5 to 1.5
- outer_moment: float32 [8192, 1024], P(('fsdp', 'rep')), may hold values from -0.6 to 0.6
Outputs:
- new_params: float32 [8192, 1024], P(('fsdp', 'rep'))
- new_moment: float32 [8192, 1024], P(('fsdp', 'rep'))
- fresh_frag: bfloat16 [8192, 1024], P('fsdp')
- weight_grad: bfloat16 [32, 8192, 512], P('rep', 'fsdp')
All inputs are finite; a program needn't handle non-finite values.
Results may differ from a plain program's by a relative error of at most 0.015.
Values may be sent and summed in bfloat16 or wider, within the bound.
No kernel may reach another device: no remote copies, remote signals or barrier semaphores. Data moves between devices by JAX's collectives and lax.ppermute only.
A program may use at most 128 MiB of HBM per device.

v0:
```python
import jax
import jax.numpy as jnp
from jax import lax
from jax.sharding import PartitionSpec as P

BLOCK = 128


def encode_blocks(deltas):
    shaped = deltas.reshape(deltas.shape[:-1] + (deltas.shape[-1] // BLOCK, BLOCK))
    needed = (jnp.max(jnp.abs(shaped), axis=-1, keepdims=True) + 1e-06) / 448.0
    scales = jnp.full(needed.shape, 2.0**9, needed.dtype)
    for exponent in range(8, -31, -1):
        scales = jnp.where(needed <= 2.0**exponent, 2.0**exponent, scales)
    magnitude = jnp.abs(shaped) / scales
    spacing = jnp.full(magnitude.shape, 2.0 ** (-9), magnitude.dtype)
    for exponent in range(-5, 9):
        spacing = jnp.where(magnitude >= 2.0**exponent, 2.0 ** (exponent - 3), spacing)
    levels = jnp.floor(magnitude / spacing + 0.5) * spacing
    encoded = jnp.where(shaped < 0, -levels, levels).astype(jnp.bfloat16)
    return (encoded, scales)


def decode_rows(deltas):
    encoded, scales = encode_blocks(deltas)
    return (encoded.astype(jnp.float32) * scales).reshape(deltas.shape)


def per_device(
    activations, norm_gain, key_weight, key_target, replica_frag, outer_params, outer_moment
):
    wide = activations[0].astype(jnp.float32)
    inv_rms = lax.rsqrt(jnp.mean(wide * wide, axis=1, keepdims=True) + 1e-05)
    normed = (wide * inv_rms * norm_gain[None, :]).astype(jnp.bfloat16)
    tok_rows = normed.shape[0]
    token_count = tok_rows * lax.axis_size("fsdp")
    columns = normed
    keys = jnp.dot(
        columns,
        lax.all_gather(key_weight[0], "fsdp", axis=0, tiled=True),
        preferred_element_type=jnp.float32,
    )
    key_cot = (
        (keys - key_target[0].astype(jnp.float32)) / jnp.sqrt(jnp.float32(token_count))
    ).astype(jnp.bfloat16)
    columns = normed
    grad_rows = lax.psum_scatter(
        lax.dot_general(
            columns, key_cot, (((0,), (0,)), ((), ())), preferred_element_type=jnp.float32
        ).astype(jnp.bfloat16),
        "fsdp",
        scatter_dimension=0,
        tiled=True,
    )
    weight_grad = grad_rows[None]
    replicas = lax.axis_size("rep")
    anchor = lax.all_gather(outer_params, "rep", axis=0, tiled=True)
    decoded = decode_rows(anchor - replica_frag[0].astype(jnp.float32))
    totals = lax.psum_scatter(decoded, "rep", scatter_dimension=0, tiled=True)
    mean_delta = totals / jnp.float32(replicas)
    new_moment = 0.9 * outer_moment + mean_delta
    new_params = outer_params - 0.7 * (mean_delta + 0.9 * new_moment)
    fresh_frag = lax.all_gather(new_params.astype(jnp.bfloat16), "rep", axis=0, tiled=True)
    return (new_params, new_moment, fresh_frag, weight_grad)


def solution(mesh):
    placed = (
        P("rep", "fsdp", None),
        P(),
        P("rep", "fsdp", None),
        P("rep", "fsdp", None),
        P("rep", "fsdp", None),
        P(("fsdp", "rep"), None),
        P(("fsdp", "rep"), None),
    )
    return jax.shard_map(
        per_device,
        mesh=mesh,
        in_specs=placed,
        out_specs=(
            P(("fsdp", "rep"), None),
            P(("fsdp", "rep"), None),
            P("fsdp", None),
            P("rep", "fsdp", None),
        ),
        check_vma=False,
    )
```

profile of v0, /device:TPU:32, one launch (start us, length us, event | category | flops | bytes accessed | tf_op | source)
XLA Modules:
  0.0 422.1 jit_solution(6391743536804445477)
XLA Ops:
  8.0 0.0 all-gather.5.cloned.1.call-start
  8.0 0.7 all-gather.5.cloned.1.call-update
  8.7 0.0 reduce-scatter.3.cloned.1.call-start
  8.8 70.5 %all-gather.5.cloned.1.call-done = f32[1024,1024]{1,0:T(8,128)} async-done(((f32[32,1024]{1,0:T(8,128)}), f32[1024,1024]{1,0:T(8,128)}) %all-gather.5.cloned.1.call-update) | async-done | bytes 4194320 | tf_op jit(solution)/shard_map/all_gather | solution.py:57
  79.2 3.6 abs_bitcast_fusion
  82.8 3.0 copy.11
  85.8 0.0 copy-start.1
  85.8 3.5 reduce_max.9
  89.3 0.0 copy-start
  89.3 1.4 select_select_fusion
  90.7 1.1 div.41
  91.8 0.0 copy-done.1
  91.8 0.0 copy-done
  91.8 7.1 %bitcast_multiply_fusion = f32[1024,1024]{1,0:T(8,128)} fusion(f32[128,8,8,128]{3,2,1,0:T(8,128)S(1)} %bitcast.52, f32[1024,1024]{1,0:T(8,128)S(1)} %copy-done, bf16[1,1024,1024]{2,1,0:T(8,128)(2,1)S(1)} %copy-done.1), kind=kLoop, calls=%fused_computation.10 | loop fusion | flops 45088768 | bytes 14680064 | tf_op jit(solution)/shard_map/mul | solution.py:26
  99.0 0.0 copy-start.2
  99.0 0.0 copy-start.3
  99.0 0.0 reduce-scatter.3.cloned.1.call-update
  99.0 0.0 copy-start.4
  99.0 0.0 copy-start.5
  99.0 0.0 all-gather.9.cloned.1.call-start
  99.1 0.5 all-gather.9.cloned.1.call-update
  99.6 0.0 all-gather.7.cloned.1.call-start
  99.6 119.8 %reduce-scatter.3.cloned.1.call-done = f32[32,1024]{1,0:T(8,128)} async-done(((f32[1024,1024]{1,0:T(8,128)}), f32[32,1024]{1,0:T(8,128)}) %reduce-scatter.3.cloned.1.call-update) | async-done | bytes 131088 | tf_op jit(solution)/shard_map/reduce_scatter | solution.py:59
  219.4 0.0 copy-done.2
  219.5 0.0 copy-done.3
  219.5 1.7 fusion.27
  221.1 0.0 all-gather.7.cloned.1.call-update
  221.1 0.2 reduce-scatter.5.cloned.1.call-start
  221.4 4.1 fusion
  225.5 0.0 all-gather.9.cloned.1.call-done
  225.5 0.0 copy-done.4
  225.5 0.0 copy-done.5
  225.5 8.7 %fusion.22 = bf16[384,512]{1,0:T(8,128)(2,1)S(1)} fusion(bf16[1,8192,512]{2,1,0:T(8,128)(2,1)} %all-gather.9.cloned.1.call-done, bf16[1,384,8192]{2,1,0:T(8,128)(2,1)} %param.7, f32[8192]{0:T(1024)S(1)} %copy-done.5, f32[384]{0:T(512)S(1)} %add_rsqrt_fusion, bf16[1,384,512]{2,1,0:T(8,128)(2,1)S(1)} %copy-done.4), kind=kOutput, calls=%fused_computation.21 | convolution fusion | flops 3234594816 | bytes 15500800 | tf_op jit(solution)/shard_map/dot_general | solution.py:38
  234.2 10.7 %convolution_convert_fusion = bf16[8192,512]{1,0:T(8,128)(2,1)} fusion(bf16[384,512]{1,0:T(8,128)(2,1)S(1)} %fusion.22, bf16[1,384,8192]{2,1,0:T(8,128)(2,1)} %param.7, f32[8192]{0:T(1024)S(1)} %copy-done.5, f32[384]{0:T(512)S(1)} %add_rsqrt_fusion), kind=kOutput, calls=%fused_computation.5 | convolution fusion | flops 3238002688 | bytes 15107584 | tf_op jit(solution)/shard_map/dot_general | solution.py:48
  244.9 0.0 reduce-scatter.5.cloned.1.call-update
  244.9 42.9 %all-gather.7.cloned.1.call-done = bf16[1024,1024]{1,0:T(8,128)(2,1)} async-done(((bf16[32,1024]{1,0:T(8,128)(2,1)}), bf16[1024,1024]{1,0:T(8,128)(2,1)}) %all-gather.7.cloned.1.call-update) | async-done | bytes 2097168 | tf_op jit(solution)/shard_map/all_gather | solution.py:63
  287.8 123.6 %reduce-scatter.5.cloned.1.call-done = bf16[1024,512]{1,0:T(8,128)(2,1)} async-done(((bf16[8192,512]{1,0:T(8,128)(2,1)}), bf16[1024,512]{1,0:T(8,128)(2,1)}) %reduce-scatter.5.cloned.1.call-update) | async-done | bytes 1048592 | tf_op jit(solution)/shard_map/reduce_scatter | solution.py:47
  411.4 3.1 copy.15
  (1 shorter events, 0.0 us)
Async XLA Ops:
  8.0 71.2 %all-gather.5.cloned.1.call-start = ((), (), s32[]{:S(2)}) async-start(), calls=%async_computation.2 | async-start | bytes 4325376 | tf_op jit(solution)/shard_map/all_gather | solution.py:57
  8.7 210.7 %reduce-scatter.3.cloned.1.call-start = ((), (), s32[]{:S(2)}) async-start(), calls=%async_computation.3 | async-start | bytes 4325376 | tf_op jit(solution)/shard_map/reduce_scatter | solution.py:59
  85.8 6.0 %copy-start.1 = (bf16[1,1024,1024]{2,1,0:T(8,128)(2,1)S(1)}, bf16[1,1024,1024]{2,1,0:T(8,128)(2,1)}, u32[]{:S(2)}) copy-start(bf16[1,1024,1024]{2,1,0:T(8,128)(2,1)} %param.11) | copy-start | bytes 6291460
  89.3 2.5 copy-start
  99.0 120.5 %copy-start.2 = (f32[32,1024]{1,0:T(8,128)S(1)}, f32[32,1024]{1,0:T(8,128)}, u32[]{:S(2)}) copy-start(f32[32,1024]{1,0:T(8,128)} %param.12) | copy-start | bytes 393220
  99.0 120.5 %copy-start.3 = (f32[32,1024]{1,0:T(8,128)S(1)}, f32[32,1024]{1,0:T(8,128)}, u32[]{:S(2)}) copy-start(f32[32,1024]{1,0:T(8,128)} %param.13) | copy-start | bytes 393220
  99.0 126.5 %copy-start.4 = (bf16[1,384,512]{2,1,0:T(8,128)(2,1)S(1)}, bf16[1,384,512]{2,1,0:T(8,128)(2,1)}, u32[]{:S(2)}) copy-start(bf16[1,384,512]{2,1,0:T(8,128)(2,1)} %param.10) | copy-start | bytes 1179652
  99.0 126.5 %copy-start.5 = (f32[8192]{0:T(1024)S(1)}, f32[8192]{0:T(1024)}, u32[]{:S(2)}) copy-start(f32[8192]{0:T(1024)} %param.8) | copy-start | bytes 98308
  99.0 126.5 %all-gather.9.cloned.1.call-start = ((), (), s32[]{:S(2)}) async-start(), calls=%async_computation.6 | async-start | bytes 9437184 | tf_op jit(solution)/shard_map/all_gather | solution.py:40
  99.6 188.2 %all-gather.7.cloned.1.call-start = ((), (), s32[]{:S(2)}) async-start(), calls=%async_computation.4 | async-start | bytes 2162688 | tf_op jit(solution)/shard_map/all_gather | solution.py:63
  221.1 190.3 %reduce-scatter.5.cloned.1.call-start = ((), (), s32[]{:S(2)}) async-start(), calls=%async_computation.5 | async-start | bytes 9437184 | tf_op jit(solution)/shard_map/reduce_scatter | solution.py:47
Sparse Core Ops, SparseCore 0:
  10.7 68.5 all-gather.4
  99.1 120.2 reduce-scatter.2
Sparse Core Ops, SparseCore 1:
  102.1 112.3 all-gather.8
  221.2 66.5 all-gather.6
  292.3 119.0 reduce-scatter.4
where the time goes:
time: 423 us; the launch traced here: 422 us
  waiting for transfers between devices  358 us (85%)
  other arithmetic  21.3 us (5%)
  matrix products  19.3 us (5%)
  between operations  15.8 us (4%)
  local copies, waits for them, and re-layouts  7.22 us (2%)
    reduce_scatter x1, waiting for transfers between devices, per_device(): lax.psum_scatter(lax.dot_general(columns, key_cot, (((0,), (0,)), ((), ()...  124 us
    reduce_scatter x1, waiting for transfers between devices, per_device(): totals = lax.psum_scatter(decoded, 'rep', scatter_dimension=0, tiled=True)  120 us
    all_gather x1, waiting for transfers between devices, per_device(): anchor = lax.all_gather(outer_params, 'rep', axis=0, tiled=True)  70.5 us
    all_gather x1, waiting for transfers between devices, per_device(): lax.all_gather(new_params.astype(jnp.bfloat16), 'rep', axis=0, tiled=True)  42.9 us
    dot_general x1, matrix products, per_device(): lax.dot_general(columns, key_cot, (((0,), (0,)), ((), ())), preferred_ele...  10.7 us
    dot_general x1, matrix products, per_device(): jnp.dot(columns, lax.all_gather(key_weight[0], 'fsdp', axis=0, tiled=True...  8.66 us
  transfers between devices with their start and end apart: 5, of which 4 were waited for; matrix products, arithmetic and copies ran while one was open for 6% of the time, Pallas kernels for 0%

commit v1 on v0

v1 whole, which is shorter than its diff:
```python
import functools

import jax
import jax.numpy as jnp
from jax import lax
from jax.experimental import pallas as pl
from jax.experimental.pallas import tpu as pltpu
from jax.sharding import PartitionSpec as P

BLOCK = 128
N_Y = 4
N_X = 2
PER_STEP = 4


def y_shift(step):
    return [
        (y * N_X + x, ((y + step) % N_Y) * N_X + x) for y in range(N_Y) for x in range(N_X)
    ]


X_SWAP = [(y * N_X + x, y * N_X + 1 - x) for y in range(N_Y) for x in range(N_X)]


def send_y(block, step):
    return lax.ppermute(block, "fsdp", y_shift(step))


def power_not_below(needed):
    scale = jnp.full(needed.shape, 2.0**-30, jnp.float32)
    inverse = jnp.full(needed.shape, 2.0**30, jnp.float32)
    rest = needed
    for step in (32, 16, 8, 4, 2, 1):
        above = rest > 2.0 ** (step - 31)
        scale = jnp.where(above, scale * 2.0**step, scale)
        inverse = jnp.where(above, inverse * 2.0**-step, inverse)
        rest = jnp.where(above, rest * 2.0**-step, rest)
    return scale, inverse


def round_to_grid(magnitude):
    rest = magnitude
    spacing = jnp.full(magnitude.shape, 2.0**-9, jnp.float32)
    for step in (8, 4, 2, 1):
        above = rest >= 2.0 ** (step - 6)
        spacing = jnp.where(above, spacing * 2.0**step, spacing)
        rest = jnp.where(above, rest * 2.0**-step, rest)
    return jnp.floor(rest * 512.0 + 0.5) * spacing


def outer_kernel(replicas, frag_ref, params_ref, moment_ref, new_params_ref, new_moment_ref, fresh_ref, total):
    step = pl.program_id(0)

    @pl.when(step == 0)
    def start():
        total[...] = jnp.zeros_like(total)

    rows, cols = params_ref.shape
    blocks = cols // BLOCK
    lane = lax.broadcasted_iota(jnp.int32, (rows, BLOCK), 1)

    def delta(replica, block):
        at = pl.ds(block * BLOCK, BLOCK)
        return params_ref[:, at] - frag_ref[replica, :, at].astype(jnp.float32)

    largest = jnp.zeros((rows, BLOCK), jnp.float32)
    for replica in range(PER_STEP):
        for block in range(blocks):
            peak = jnp.max(jnp.abs(delta(replica, block)), axis=1, keepdims=True)
            largest = jnp.where(lane == replica * blocks + block, peak, largest)
    scales, inverses = power_not_below((largest + 1e-06) / 448.0)
    for block in range(blocks):
        at = pl.ds(block * BLOCK, BLOCK)
        term = total[:, at]
        for replica in range(PER_STEP):
            slot = replica * blocks + block
            diff = delta(replica, block)
            level = round_to_grid(jnp.abs(diff) * inverses[:, slot : slot + 1])
            decoded = level * scales[:, slot : slot + 1]
            term = term + jnp.where(diff < 0, -decoded, decoded)
        total[:, at] = term

    @pl.when(step == pl.num_programs(0) - 1)
    def finish():
        mean_delta = total[...] / jnp.float32(replicas)
        new_moment = 0.9 * moment_ref[...] + mean_delta
        new_params = params_ref[...] - 0.7 * (mean_delta + 0.9 * new_moment)
        new_moment_ref[...] = new_moment
        new_params_ref[...] = new_params
        fresh_ref[...] = new_params.astype(jnp.bfloat16)


def outer_step(frags, outer_params, outer_moment):
    replicas, rows, cols = frags.shape
    whole = pl.BlockSpec((rows, cols), lambda i: (0, 0))
    return pl.pallas_call(
        functools.partial(outer_kernel, replicas),
        grid=(replicas // PER_STEP,),
        in_specs=[pl.BlockSpec((PER_STEP, rows, cols), lambda i: (i, 0, 0)), whole, whole],
        out_specs=[whole, whole, whole],
        out_shape=[
            jax.ShapeDtypeStruct((rows, cols), jnp.float32),
            jax.ShapeDtypeStruct((rows, cols), jnp.float32),
            jax.ShapeDtypeStruct((rows, cols), jnp.bfloat16),
        ],
        scratch_shapes=[pltpu.VMEM((rows, cols), jnp.float32)],
        cost_estimate=pl.CostEstimate(
            flops=40 * replicas * rows * cols, bytes_accessed=3 * replicas * rows * cols, transcendentals=0
        ),
    )(frags, outer_params, outer_moment)


def per_device(
    activations, norm_gain, key_weight, key_target, replica_frag, outer_params, outer_moment
):
    place = lax.axis_index("fsdp")
    y = place // N_X
    x = place % N_X
    tokens = activations[0]
    quarter = tokens.shape[1] // N_Y
    rows = quarter // N_X
    token_count = tokens.shape[0] * lax.axis_size("fsdp")

    fragment = replica_frag[0]
    frags = lax.all_to_all(fragment, "rep", 0, 0, tiled=True)
    frags = frags.reshape(lax.axis_size("rep"), -1, fragment.shape[1])
    new_params, new_moment, fresh = outer_step(frags, outer_params, outer_moment)
    fresh_frag = lax.all_gather(fresh, "rep", axis=0, tiled=True)

    def columns(step):
        return lax.dynamic_slice(tokens, (0, lax.rem(y + step, N_Y) * quarter), (tokens.shape[0], quarter))

    weight = key_weight[0]
    held = [columns(0), send_y(columns(1), 1), send_y(columns(2), 2), send_y(columns(3), 3)]
    other = lax.ppermute(weight, "fsdp", X_SWAP)
    gain = lax.dynamic_slice(norm_gain, (y * quarter,), (quarter,))
    pair = jnp.where(
        x == 0, jnp.concatenate([weight, other]), jnp.concatenate([other, weight])
    )
    pair = (pair.astype(jnp.float32) * gain[:, None]).astype(jnp.bfloat16)
    wide = tokens.astype(jnp.float32)
    inv_rms = lax.rsqrt(jnp.mean(wide * wide, axis=1, keepdims=True) + 1e-05)
    keys = jnp.dot(held[0], pair, preferred_element_type=jnp.float32)
    for step in (1, 2, 3):
        part = jnp.dot(held[step], pair, preferred_element_type=jnp.float32)
        keys = keys + send_y(part.astype(jnp.bfloat16), N_Y - step).astype(jnp.float32)
    key_cot = (keys * inv_rms - key_target[0].astype(jnp.float32)) / jnp.sqrt(jnp.float32(token_count))
    key_cot = (key_cot * inv_rms).astype(jnp.bfloat16)
    cots = [key_cot] + [send_y(key_cot, step) for step in (1, 2, 3)]

    def grad(at):
        total = None
        for block, cot in zip(held, cots):
            part = lax.dot_general(
                lax.dynamic_slice(block, (0, at * rows), (block.shape[0], rows)),
                cot,
                (((0,), (0,)), ((), ())),
                preferred_element_type=jnp.float32,
            )
            total = part if total is None else total + part
        return total

    theirs = lax.ppermute(grad(1 - x).astype(jnp.bfloat16), "fsdp", X_SWAP)
    own_gain = lax.dynamic_slice(norm_gain, (place * rows,), (rows,))
    weight_grad = ((grad(x) + theirs.astype(jnp.float32)) * own_gain[:, None]).astype(jnp.bfloat16)
    return (new_params, new_moment, fresh_frag, weight_grad[None])


def solution(mesh):
    placed = (
        P("rep", "fsdp", None),
        P(),
        P("rep", "fsdp", None),
        P("rep", "fsdp", None),
        P("rep", "fsdp", None),
        P(("fsdp", "rep"), None),
        P(("fsdp", "rep"), None),
    )
    return jax.shard_map(
        per_device,
        mesh=mesh,
        in_specs=placed,
        out_specs=(
            P(("fsdp", "rep"), None),
            P(("fsdp", "rep"), None),
            P("fsdp", None),
            P("rep", "fsdp", None),
        ),
        check_vma=False,
    )
```

time: 423 us -> 195 us (0.46)
  waiting for transfers between devices: 358 us -> 92.5 us
  starting transfers between devices: 0.38 us -> 30 us
  other arithmetic: 21.3 us -> 8.84 us
  Pallas kernels: 0 us -> 9.14 us
  matrix products: 19.3 us -> 28 us
    reduce_scatter x2 -> x0, waiting for transfers between devices: 243 us -> none  [the longest x1 124 us: per_device(): lax.psum_scatter(lax.dot_general(columns, key_cot, (((0,), (0,)), ((), ()...]
    all_gather x3 -> x1, waiting for transfers between devices: 113 us -> 5.03 us  [per_device(): fresh_frag = lax.all_gather(fresh, 'rep', axis=0, tiled=True)]
    ppermute x0 -> x11, waiting for transfers between devices: none -> 87.4 us  [the longest x1 37.8 us: per_device(): other = lax.ppermute(weight, 'fsdp', X_SWAP)]
    ppermute x0 -> x11, starting transfers between devices: none -> 20.3 us  [the longest x9 14.7 us: send_y(): return lax.ppermute(block, 'fsdp', y_shift(step))]
    all_to_all x0 -> x1, starting transfers between devices: none -> 9.67 us  [per_device(): frags = lax.all_to_all(fragment, 'rep', 0, 0, tiled=True)]
    pallas_call x0 -> x1, Pallas kernels: none -> 9.14 us  [outer_step(): pl.pallas_call(functools.partial(outer_kernel, replicas), grid=(replicas...]
    dot_general x2 -> x12, matrix products: 19.3 us -> 28 us  [the longest x8 15.7 us: grad(): lax.dot_general(lax.dynamic_slice(block, (0, at * rows), (block.shape[0],...]
    mul x1 -> x0, other arithmetic: 7.12 us -> none  [decode_rows(): return (encoded.astype(jnp.float32) * scales).reshape(deltas.shape)]
  transfers between devices with their start and end apart: 5 -> 13, of which waited for: 4 -> 6; matrix products, arithmetic and copies ran while one was open for 6% -> 22% of each run, Pallas kernels for 0% -> 5%
where the time goes in v1:
time: 195 us; the launch traced here: 192 us
  waiting for transfers between devices  92.5 us (47%)
  starting transfers between devices  30 us (15%)
  matrix products  28 us (14%)
  between operations  14.3 us (7%)
  local copies, waits for them, and re-layouts  9.25 us (5%)
  Pallas kernels  9.14 us (5%)
  other arithmetic  8.84 us (5%)
    ppermute x1, waiting for transfers between devices, per_device(): other = lax.ppermute(weight, 'fsdp', X_SWAP)  37.8 us
    ppermute x9, waiting for transfers between devices, send_y(): return lax.ppermute(block, 'fsdp', y_shift(step))  33.7 us
    ppermute x1, waiting for transfers between devices, per_device(): theirs = lax.ppermute(grad(1 - x).astype(jnp.bfloat16), 'fsdp', X_SWAP)  16 us
    dot_general x8, matrix products, grad(): lax.dot_general(lax.dynamic_slice(block, (0, at * rows), (block.shape[0],...  15.7 us
    ppermute x9, starting transfers between devices, send_y(): return lax.ppermute(block, 'fsdp', y_shift(step))  14.7 us
    all_to_all x1, starting transfers between devices, per_device(): frags = lax.all_to_all(fragment, 'rep', 0, 0, tiled=True)  9.67 us
    dot_general x3, matrix products, per_device(): part = jnp.dot(held[step], pair, preferred_element_type=jnp.float32)  9.49 us
    pallas_call x1, Pallas kernels, outer_step(): pl.pallas_call(functools.partial(outer_kernel, replicas), grid=(replicas...  9.14 us
  transfers between devices with their start and end apart: 13, of which 6 were waited for; matrix products, arithmetic and copies ran while one was open for 22% of the time, Pallas kernels for 5%

profile of v1, /device:TPU:32, one launch (start us, length us, event | category | flops | bytes accessed | tf_op | source)
XLA Modules:
  0.0 192.0 jit_solution(10890159648019063749)
XLA Ops:
  7.2 9.7 %all-to-all-start = ((bf16[32,32,1024]{2,1,0:T(8,128)(2,1)}), bf16[32,32,1024]{2,1,0:T(8,128)(2,1)S(1)}, u32[]{:S(2)}, u32[]{:S(2)}) async-start(bf16[32,32,1024]{2,1,0:T(8,128)(2,1)} %bitcast.51), calls=%async_computation | async-start | bytes 4194304 | tf_op jit(solution)/shard_map/all_to_all | solution.py:125
  16.8 0.0 all-gather.2.cloned.1.call-start
  16.9 0.0 copy-start.3
  17.0 0.0 copy-start.4
  17.0 4.8 %dynamic-slice_bitcast_fusion.2 = (bf16[384,2048]{1,0:T(8,128)(2,1)}, bf16[384,2048]{1,0:T(8,128)(2,1)}, bf16[384,2048]{1,0:T(8,128)(2,1)}) fusion(bf16[1,384,8192]{2,1,0:T(8,128)(2,1)} %param.7, s32[]{:T(128)S(6)} %select_n.64, s32[]{:T(128)S(6)} %select_n.66, s32[]{:T(128)S(6)} %select_n.65), kind=kLoop, calls=%fused_computation.9 | loop fusion | bytes 9437196 | tf_op jit(solution)/shard_map/dynamic_slice | solution.py:131
  21.8 3.0 %collective-permute-start.5 = (bf16[384,2048]{1,0:T(8,128)(2,1)}, bf16[384,2048]{1,0:T(8,128)(2,1)}, u32[]{:S(2)}, u32[]{:S(2)}) collective-permute-start(bf16[384,2048]{1,0:T(8,128)(2,1)} %get-tuple-element.11), channel_id=1, source_target_pairs={{0,6},{1,7},{2,0},{3,1},{4,2},{5,3},{6,4},{7,5},{8,14},{9,15},{10,... | collective-permute-start | bytes 4718600 | tf_op jit(solution)/shard_map/ppermute | solution.py:26
  24.8 2.7 %collective-permute-start = (bf16[1024,512]{1,0:T(8,128)(2,1)S(1)}, bf16[1024,512]{1,0:T(8,128)(2,1)}, u32[]{:S(2)}, u32[]{:S(2)}) collective-permute-start(bf16[1024,512]{1,0:T(8,128)(2,1)S(1)} %bitcast.52), channel_id=1, source_target_pairs={{0,1},{1,0},{2,3},{3,2},{4,5},{5,4},{6,7},{7,6},{8,9},{9,8},{10,11... | collective-permute-start | bytes 3145736 | tf_op jit(solution)/shard_map/ppermute | solution.py:135
  27.5 0.6 collective-permute-start.3
  28.2 1.0 collective-permute-start.1
  29.1 37.8 %collective-permute-done = bf16[1024,512]{1,0:T(8,128)(2,1)} collective-permute-done((bf16[1024,512]{1,0:T(8,128)(2,1)S(1)}, bf16[1024,512]{1,0:T(8,128)(2,1)}, u32[]{:S(2)}, u32[]{:S(2)}) %collective-permute-start) | collective-permute-done | bytes 1048608 | tf_op jit(solution)/shard_map/ppermute | solution.py:135
  66.9 3.1 %multiply_convert_fusion = bf16[2048,512]{1,0:T(8,128)(2,1)S(1)} fusion(bf16[1024,512]{1,0:T(8,128)(2,1)} %collective-permute-done, bf16[1024,512]{1,0:T(8,128)(2,1)S(1)} %bitcast.53, f32[2048]{0:T(1024)S(1)} %dynamic_slice.63, pred[]{:T(512)S(6)} %eq.5), kind=kLoop, calls=%fused_computation.1 | loop fusion | flops 12582912 | bytes 4202497 | tf_op jit(solution)/shard_map/convert_element_type | solution.py:140
  70.0 22.7 %collective-permute-done.5 = bf16[384,2048]{1,0:T(8,128)(2,1)} collective-permute-done((bf16[384,2048]{1,0:T(8,128)(2,1)}, bf16[384,2048]{1,0:T(8,128)(2,1)}, u32[]{:S(2)}, u32[]{:S(2)}) %collective-permute-start.5) | collective-permute-done | bytes 1572896 | tf_op jit(solution)/shard_map/ppermute | solution.py:26
  92.8 3.2 %convolution_convert_fusion = bf16[384,512]{1,0:T(8,128)(2,1)} fusion(bf16[384,2048]{1,0:T(8,128)(2,1)} %collective-permute-done.5, bf16[2048,512]{1,0:T(8,128)(2,1)S(1)} %multiply_convert_fusion), kind=kOutput, calls=%fused_computation.18 | convolution fusion | flops 805502976 | bytes 4063232 | tf_op jit(solution)/shard_map/dot_general | solution.py:145
  95.9 0.0 collective-permute-start.6
  95.9 0.0 collective-permute-done.3
  95.9 3.2 %convolution_convert_fusion.1 = bf16[384,512]{1,0:T(8,128)(2,1)} fusion(bf16[384,2048]{1,0:T(8,128)(2,1)} %collective-permute-done.3, bf16[2048,512]{1,0:T(8,128)(2,1)S(1)} %multiply_convert_fusion), kind=kOutput, calls=%fused_computation.19 | convolution fusion | flops 805502976 | bytes 4063232 | tf_op jit(solution)/shard_map/dot_general | solution.py:145
  99.1 5.2 %collective-permute-start.4 = (bf16[384,512]{1,0:T(8,128)(2,1)}, bf16[384,512]{1,0:T(8,128)(2,1)}, u32[]{:S(2)}, u32[]{:S(2)}) collective-permute-start(bf16[384,512]{1,0:T(8,128)(2,1)} %convolution_convert_fusion.1), channel_id=1, source_target_pairs={{0,4},{1,5},{2,6},{3,7},{4,0},{5,1},{6,2},{7,3},{8,12},{9,13},{10,... | collective-permute-start | bytes 1179656 | tf_op jit(solution)/shard_map/ppermute | solution.py:26
  104.3 0.0 collective-permute-done.1
  104.3 3.2 %convolution_convert_fusion.2 = bf16[384,512]{1,0:T(8,128)(2,1)} fusion(bf16[384,2048]{1,0:T(8,128)(2,1)} %collective-permute-done.1, bf16[2048,512]{1,0:T(8,128)(2,1)S(1)} %multiply_convert_fusion), kind=kOutput, calls=%fused_computation.20 | convolution fusion | flops 805502976 | bytes 4063232 | tf_op jit(solution)/shard_map/dot_general | solution.py:145
  107.4 0.0 collective-permute-start.2
  107.4 0.0 all-to-all-done.frag_ref
  107.5 1.3 copy-done
  108.8 9.1 %shard_map.102 = (f32[32,1024]{1,0:T(8,128)}, f32[32,1024]{1,0:T(8,128)}, bf16[32,1024]{1,0:T(8,128)(2,1)}) custom-call(bf16[32,32,1024]{2,1,0:T(8,128)(2,1)} %copy-done, f32[32,1024]{1,0:T(8,128)} %params_ref.1, f32[32,1024]{1,0:T(8,128)} %moment_ref.1), custom_call_target="tpu_custom_call" | custom-call | flops 41943040 | bytes 3145728 | tf_op jit(solution)/shard_map/pallas_call | solution.py:96
  117.9 0.0 all-gather.2.cloned.1.call-update
  117.9 0.0 copy-start.5
  118.0 4.3 %multiply_reduce_fusion = f32[384]{0:T(512)S(1)} fusion(bf16[1,384,8192]{2,1,0:T(8,128)(2,1)} %param.7), kind=kLoop, calls=%fused_computation | loop fusion | flops 9436800 | bytes 6292992 | tf_op jit(solution)/shard_map/reduce_sum | solution.py:142
  122.2 0.0 collective-permute-done.6
  122.2 0.0 collective-permute-done.4
  122.3 2.9 %fusion.21 = bf16[384,512]{1,0:T(8,128)(2,1)S(1)} fusion(bf16[2048,512]{1,0:T(8,128)(2,1)S(1)} %copy-done.2, bf16[1,384,8192]{2,1,0:T(8,128)(2,1)} %param.7, s32[]{:T(128)S(6)} %select_n.59, bf16[384,512]{1,0:T(8,128)(2,1)} %collective-permute-done.6, bf16[384,512]{1,0:T(8,128)(2,1)} %collective-permute-done.4, ...), kind=kOutput, calls=%fused_computation.17 | convolution fusion | flops 807469056 | bytes 5639172 | tf_op jit(solution)/shard_map/dot_general | solution.py:143
  125.2 1.7 collective-permute-start.8
  126.9 0.7 collective-permute-start.7
  127.6 2.6 %collective-permute-start.9 = (bf16[384,512]{1,0:T(8,128)(2,1)S(1)}, bf16[384,512]{1,0:T(8,128)(2,1)S(1)}, u32[]{:S(2)}, u32[]{:S(2)}) collective-permute-start(bf16[384,512]{1,0:T(8,128)(2,1)S(1)} %fusion.21), channel_id=1, source_target_pairs={{0,6},{1,7},{2,0},{3,1},{4,2},{5,3},{6,4},{7,5},{8,14},{9,15},{10,... | collective-permute-start | bytes 1179656 | tf_op jit(solution)/shard_map/ppermute | solution.py:26
  130.1 2.2 %fusion.25 = f32[1024,512]{1,0:T(8,128)S(1)} fusion(bf16[384,512]{1,0:T(8,128)(2,1)S(1)} %fusion.21, bf16[1,384,8192]{2,1,0:T(8,128)(2,1)} %param.7, s32[]{:T(128)S(6)} %dynamic_slice.73), kind=kOutput, calls=%fused_computation.22 | convolution fusion | flops 402653184 | bytes 3276804 | tf_op jit(solution)/shard_map/dot_general | solution.py:154
  132.3 6.7 %collective-permute-done.8 = bf16[384,512]{1,0:T(8,128)(2,1)S(1)} collective-permute-done((bf16[384,512]{1,0:T(8,128)(2,1)S(1)}, bf16[384,512]{1,0:T(8,128)(2,1)S(1)}, u32[]{:S(2)}, u32[]{:S(2)}) %collective-permute-start.8) | collective-permute-done | bytes 393248 | tf_op jit(solution)/shard_map/ppermute | solution.py:26
  139.0 1.9 fusion.33
  140.9 4.2 %collective-permute-done.7 = bf16[384,512]{1,0:T(8,128)(2,1)S(1)} collective-permute-done((bf16[384,512]{1,0:T(8,128)(2,1)S(1)}, bf16[384,512]{1,0:T(8,128)(2,1)S(1)}, u32[]{:S(2)}, u32[]{:S(2)}) %collective-permute-start.7) | collective-permute-done | bytes 393248 | tf_op jit(solution)/shard_map/ppermute | solution.py:26
  145.1 1.9 fusion.35
  147.0 1.9 add_convert_fusion
  148.9 2.8 %collective-permute-start.10 = (bf16[1024,512]{1,0:T(8,128)(2,1)S(1)}, bf16[1024,512]{1,0:T(8,128)(2,1)S(1)}, u32[]{:S(2)}, u32[]{:S(2)}) collective-permute-start(bf16[1024,512]{1,0:T(8,128)(2,1)S(1)} %add_convert_fusion), channel_id=1, source_target_pairs={{0,1},{1,0},{2,3},{3,2},{4,5},{5,4},{6,7},{7,6},{8,9},{9,8},{10,11... | collective-permute-start | bytes 3145736 | tf_op jit(solution)/shard_map/ppermute | solution.py:163
  151.7 2.2 %fusion.27 = f32[1024,512]{1,0:T(8,128)S(1)} fusion(bf16[384,512]{1,0:T(8,128)(2,1)S(1)} %fusion.21, bf16[1,384,8192]{2,1,0:T(8,128)(2,1)} %param.7, s32[]{:T(128)S(6)} %dynamic_slice.58), kind=kOutput, calls=%fused_computation.24 | convolution fusion | flops 402653184 | bytes 3276804 | tf_op jit(solution)/shard_map/dot_general | solution.py:154
  153.9 1.9 fusion.38
  155.8 1.9 fusion.40
  157.7 0.0 dynamic-slice-start
  157.7 1.9 fusion.42
  159.6 16.0 %collective-permute-done.10 = bf16[1024,512]{1,0:T(8,128)(2,1)S(1)} collective-permute-done((bf16[1024,512]{1,0:T(8,128)(2,1)S(1)}, bf16[1024,512]{1,0:T(8,128)(2,1)S(1)}, u32[]{:S(2)}, u32[]{:S(2)}) %collective-permute-start.10) | collective-permute-done | bytes 1048608 | tf_op jit(solution)/shard_map/ppermute | solution.py:163
  175.6 1.4 fusion.24
  177.1 5.0 %all-gather.2.cloned.1.call-done = bf16[1024,1024]{1,0:T(8,128)(2,1)} async-done(((bf16[32,1024]{1,0:T(8,128)(2,1)}), bf16[1024,1024]{1,0:T(8,128)(2,1)}) %all-gather.2.cloned.1.call-update) | async-done | bytes 2097168 | tf_op jit(solution)/shard_map/all_gather | solution.py:128
  182.1 3.1 %copy.12 = bf16[1024,1024]{1,0:T(8,128)(2,1)} copy(bf16[1024,1024]{1,0:T(8,128)(2,1)} %all-gather.2.cloned.1.call-done) | data formatting | bytes 4194304
  (13 shorter events, 0.0 us)
Async XLA Ops:
  7.2 100.3 %all-to-all-start = ((bf16[32,32,1024]{2,1,0:T(8,128)(2,1)}), bf16[32,32,1024]{2,1,0:T(8,128)(2,1)S(1)}, u32[]{:S(2)}, u32[]{:S(2)}) async-start(bf16[32,32,1024]{2,1,0:T(8,128)(2,1)} %bitcast.51), calls=%async_computation | async-start | bytes 4194304 | tf_op jit(solution)/shard_map/all_to_all | solution.py:125
  16.8 165.2 %all-gather.2.cloned.1.call-start = ((), (), s32[]{:S(2)}) async-start(), calls=%async_computation.1 | async-start | bytes 2162688 | tf_op jit(solution)/shard_map/all_gather | solution.py:128
  16.9 7.9 %copy-start.3 = (bf16[1,1024,512]{2,1,0:T(8,128)(2,1)S(1)}, bf16[1,1024,512]{2,1,0:T(8,128)(2,1)}, u32[]{:S(2)}) copy-start(bf16[1,1024,512]{2,1,0:T(8,128)(2,1)} %param.9) | copy-start | bytes 3145732
  17.0 12.2 %copy-start.4 = (f32[8192]{0:T(1024)S(1)}, f32[8192]{0:T(1024)}, u32[]{:S(2)}) copy-start(f32[8192]{0:T(1024)} %param.8) | copy-start | bytes 98308
  21.8 71.0 %collective-permute-start.5 = (bf16[384,2048]{1,0:T(8,128)(2,1)}, bf16[384,2048]{1,0:T(8,128)(2,1)}, u32[]{:S(2)}, u32[]{:S(2)}) collective-permute-start(bf16[384,2048]{1,0:T(8,128)(2,1)} %get-tuple-element.11), channel_id=1, source_target_pairs={{0,6},{1,7},{2,0},{3,1},{4,2},{5,3},{6,4},{7,5},{8,14},{9,15},{10,... | collective-permute-start | bytes 4718600 | tf_op jit(solution)/shard_map/ppermute | solution.py:26
  24.8 42.1 %collective-permute-start = (bf16[1024,512]{1,0:T(8,128)(2,1)S(1)}, bf16[1024,512]{1,0:T(8,128)(2,1)}, u32[]{:S(2)}, u32[]{:S(2)}) collective-permute-start(bf16[1024,512]{1,0:T(8,128)(2,1)S(1)} %bitcast.52), channel_id=1, source_target_pairs={{0,1},{1,0},{2,3},{3,2},{4,5},{5,4},{6,7},{7,6},{8,9},{9,8},{10,11... | collective-permute-start | bytes 3145736 | tf_op jit(solution)/shard_map/ppermute | solution.py:135
  27.5 68.4 %collective-permute-start.3 = (bf16[384,2048]{1,0:T(8,128)(2,1)}, bf16[384,2048]{1,0:T(8,128)(2,1)}, u32[]{:S(2)}, u32[]{:S(2)}) collective-permute-start(bf16[384,2048]{1,0:T(8,128)(2,1)} %get-tuple-element.12), channel_id=1, source_target_pairs={{0,4},{1,5},{2,6},{3,7},{4,0},{5,1},{6,2},{7,3},{8,12},{9,13},{10,... | collective-permute-start | bytes 4718600 | tf_op jit(solution)/shard_map/ppermute | solution.py:26
  28.2 76.1 %collective-permute-start.1 = (bf16[384,2048]{1,0:T(8,128)(2,1)}, bf16[384,2048]{1,0:T(8,128)(2,1)}, u32[]{:S(2)}, u32[]{:S(2)}) collective-permute-start(bf16[384,2048]{1,0:T(8,128)(2,1)} %get-tuple-element.10), channel_id=1, source_target_pairs={{0,2},{1,3},{2,4},{3,5},{4,6},{5,7},{6,0},{7,1},{8,10},{9,11},{10,... | collective-permute-start | bytes 4718600 | tf_op jit(solution)/shard_map/ppermute | solution.py:26
  70.0 34.2 %copy-start.1 = (bf16[2048,512]{1,0:T(8,128)(2,1)}, bf16[2048,512]{1,0:T(8,128)(2,1)S(1)}, u32[]{:S(2)}) copy-start(bf16[2048,512]{1,0:T(8,128)(2,1)S(1)} %multiply_convert_fusion) | copy-start | bytes 6291460
  95.9 26.3 %collective-permute-start.6 = (bf16[384,512]{1,0:T(8,128)(2,1)}, bf16[384,512]{1,0:T(8,128)(2,1)}, u32[]{:S(2)}, u32[]{:S(2)}) collective-permute-start(bf16[384,512]{1,0:T(8,128)(2,1)} %convolution_convert_fusion), channel_id=1, source_target_pairs={{0,2},{1,3},{2,4},{3,5},{4,6},{5,7},{6,0},{7,1},{8,10},{9,11},{10,... | collective-permute-start | bytes 1179656 | tf_op jit(solution)/shard_map/ppermute | solution.py:26
  99.1 23.1 %collective-permute-start.4 = (bf16[384,512]{1,0:T(8,128)(2,1)}, bf16[384,512]{1,0:T(8,128)(2,1)}, u32[]{:S(2)}, u32[]{:S(2)}) collective-permute-start(bf16[384,512]{1,0:T(8,128)(2,1)} %convolution_convert_fusion.1), channel_id=1, source_target_pairs={{0,4},{1,5},{2,6},{3,7},{4,0},{5,1},{6,2},{7,3},{8,12},{9,13},{10,... | collective-permute-start | bytes 1179656 | tf_op jit(solution)/shard_map/ppermute | solution.py:26
  107.4 14.8 %collective-permute-start.2 = (bf16[384,512]{1,0:T(8,128)(2,1)}, bf16[384,512]{1,0:T(8,128)(2,1)}, u32[]{:S(2)}, u32[]{:S(2)}) collective-permute-start(bf16[384,512]{1,0:T(8,128)(2,1)} %convolution_convert_fusion.2), channel_id=1, source_target_pairs={{0,6},{1,7},{2,0},{3,1},{4,2},{5,3},{6,4},{7,5},{8,14},{9,15},{10,... | collective-permute-start | bytes 1179656 | tf_op jit(solution)/shard_map/ppermute | solution.py:26
  107.4 1.3 copy-start
  117.9 4.3 %copy-start.2 = (bf16[2048,512]{1,0:T(8,128)(2,1)S(1)}, bf16[2048,512]{1,0:T(8,128)(2,1)}, u32[]{:S(2)}) copy-start(bf16[2048,512]{1,0:T(8,128)(2,1)} %copy-done.1) | copy-start | bytes 6291460
  117.9 4.3 %copy-start.5 = (bf16[1,384,512]{2,1,0:T(8,128)(2,1)S(1)}, bf16[1,384,512]{2,1,0:T(8,128)(2,1)}, u32[]{:S(2)}) copy-start(bf16[1,384,512]{2,1,0:T(8,128)(2,1)} %param.10) | copy-start | bytes 1179652
  125.2 13.9 %collective-permute-start.8 = (bf16[384,512]{1,0:T(8,128)(2,1)S(1)}, bf16[384,512]{1,0:T(8,128)(2,1)S(1)}, u32[]{:S(2)}, u32[]{:S(2)}) collective-permute-start(bf16[384,512]{1,0:T(8,128)(2,1)S(1)} %fusion.21), channel_id=1, source_target_pairs={{0,4},{1,5},{2,6},{3,7},{4,0},{5,1},{6,2},{7,3},{8,12},{9,13},{10,... | collective-permute-start | bytes 1179656 | tf_op jit(solution)/shard_map/ppermute | solution.py:26
  126.9 18.3 %collective-permute-start.7 = (bf16[384,512]{1,0:T(8,128)(2,1)S(1)}, bf16[384,512]{1,0:T(8,128)(2,1)S(1)}, u32[]{:S(2)}, u32[]{:S(2)}) collective-permute-start(bf16[384,512]{1,0:T(8,128)(2,1)S(1)} %fusion.21), channel_id=1, source_target_pairs={{0,2},{1,3},{2,4},{3,5},{4,6},{5,7},{6,0},{7,1},{8,10},{9,11},{10,... | collective-permute-start | bytes 1179656 | tf_op jit(solution)/shard_map/ppermute | solution.py:26
  127.6 19.4 %collective-permute-start.9 = (bf16[384,512]{1,0:T(8,128)(2,1)S(1)}, bf16[384,512]{1,0:T(8,128)(2,1)S(1)}, u32[]{:S(2)}, u32[]{:S(2)}) collective-permute-start(bf16[384,512]{1,0:T(8,128)(2,1)S(1)} %fusion.21), channel_id=1, source_target_pairs={{0,6},{1,7},{2,0},{3,1},{4,2},{5,3},{6,4},{7,5},{8,14},{9,15},{10,... | collective-permute-start | bytes 1179656 | tf_op jit(solution)/shard_map/ppermute | solution.py:26
  148.9 26.7 %collective-permute-start.10 = (bf16[1024,512]{1,0:T(8,128)(2,1)S(1)}, bf16[1024,512]{1,0:T(8,128)(2,1)S(1)}, u32[]{:S(2)}, u32[]{:S(2)}) collective-permute-start(bf16[1024,512]{1,0:T(8,128)(2,1)S(1)} %add_convert_fusion), channel_id=1, source_target_pairs={{0,1},{1,0},{2,3},{3,2},{4,5},{5,4},{6,7},{7,6},{8,9},{9,8},{10,11... | collective-permute-start | bytes 3145736 | tf_op jit(solution)/shard_map/ppermute | solution.py:163
  157.7 17.9 %dynamic-slice-start = ((f32[8192]{0:T(1024)}, s32[]{:T(128)}), f32[1024]{0:T(1024)S(1)}, s32[]{:S(2)}) async-start(f32[8192]{0:T(1024)} %param.8, s32[]{:T(128)} %select_n.69), calls=%async_computation.2 | async-start | bytes 8704 | tf_op jit(solution)/shard_map/dynamic_slice | solution.py:164
Sparse Core Ops, SparseCore 0:
  118.1 63.9 all-gather.1

commit v2 on v1

v2 whole, which is shorter than its diff:
```python
import functools

import jax
import jax.numpy as jnp
from jax import lax
from jax.experimental import pallas as pl
from jax.experimental.pallas import tpu as pltpu
from jax.sharding import PartitionSpec as P

BLOCK = 128
N_Y = 4
N_X = 2
PER_STEP = 8
N_CORE = 2
ANY = pl.BlockSpec(memory_space=pl.ANY)
HBM = pl.BlockSpec(memory_space=pltpu.HBM)
VMEM = pl.BlockSpec(memory_space=pltpu.VMEM)
SMEM = pl.BlockSpec(memory_space=pltpu.SMEM)
PARAMS = pltpu.CompilerParams(vmem_limit_bytes=24 * 2**20)
COST = pl.CostEstimate(flops=10**12, bytes_accessed=10**9, transcendentals=10**9)
SHORT = pl.CostEstimate(flops=2 * 10**10, bytes_accessed=10**6, transcendentals=0)


def in_hbm(array):
    return pltpu.with_memory_space_constraint(array, pltpu.HBM)


def y_shift(step):
    return [
        (y * N_X + x, ((y + step) % N_Y) * N_X + x) for y in range(N_Y) for x in range(N_X)
    ]


X_SWAP = [(y * N_X + x, y * N_X + 1 - x) for y in range(N_Y) for x in range(N_X)]


def send_y(block, step):
    return lax.ppermute(block, "fsdp", y_shift(step))


def power_not_below(needed):
    scale = jnp.full(needed.shape, 2.0**-30, jnp.float32)
    inverse = jnp.full(needed.shape, 2.0**30, jnp.float32)
    rest = needed
    for step in (32, 16, 8, 4, 2, 1):
        above = rest > 2.0 ** (step - 31)
        scale = jnp.where(above, scale * 2.0**step, scale)
        inverse = jnp.where(above, inverse * 2.0**-step, inverse)
        rest = jnp.where(above, rest * 2.0**-step, rest)
    return scale, inverse


def grid_spacing(magnitude):
    whole = jnp.maximum((magnitude * 64.0).astype(jnp.int32), 1)
    power = 31 - lax.clz(whole)
    one = jnp.ones_like(whole)
    spacing = lax.shift_left(one, power).astype(jnp.float32)
    inverse = lax.shift_left(one, 15 - power).astype(jnp.float32) * 2.0**-15
    return spacing, inverse


def outer_kernel(
    replicas, frag_ref, params_ref, moment_ref, *refs
):
    new_params_ref, new_moment_ref, fresh_ref, total = refs[-4:]
    step = pl.program_id(0)

    @pl.when(step == 0)
    def start():
        total[...] = jnp.zeros_like(total)

    rows, cols = params_ref.shape
    blocks = cols // BLOCK
    lane = lax.broadcasted_iota(jnp.int32, (rows, BLOCK), 1)

    def delta(replica, block):
        at = pl.ds(block * BLOCK, BLOCK)
        return params_ref[:, at] - frag_ref[replica, :, at].astype(jnp.float32)

    largest = jnp.zeros((rows, BLOCK), jnp.float32)
    for replica in range(PER_STEP):
        for block in range(blocks):
            peak = jnp.max(jnp.abs(delta(replica, block)), axis=1, keepdims=True)
            largest = jnp.where(lane == replica * blocks + block, peak, largest)
    scales, inverses = power_not_below((largest + 1e-06) / 448.0)
    for block in range(blocks):
        at = pl.ds(block * BLOCK, BLOCK)
        term = total[:, at]
        for replica in range(PER_STEP):
            slot = replica * blocks + block
            diff = delta(replica, block)
            magnitude = jnp.abs(diff) * inverses[:, slot : slot + 1]
            spacing, inverse = grid_spacing(magnitude)
            level = jnp.floor(magnitude * (inverse * 512.0) + 0.5)
            decoded = level * (spacing * (scales[:, slot : slot + 1] * 2.0**-9))
            term = term + jnp.where(diff < 0, -decoded, decoded)
        total[:, at] = term

    @pl.when(step == pl.num_programs(0) - 1)
    def finish():
        mean_delta = total[...] / jnp.float32(replicas)
        new_moment = 0.9 * moment_ref[...] + mean_delta
        new_params = params_ref[...] - 0.7 * (mean_delta + 0.9 * new_moment)
        new_moment_ref[...] = new_moment
        new_params_ref[...] = new_params
        fresh_ref[...] = new_params.astype(jnp.bfloat16)


def outer_step(frags, outer_params, outer_moment, *after):
    replicas, rows, cols = frags.shape
    whole = pl.BlockSpec((rows, cols), lambda i: (0, 0))
    return pl.pallas_call(
        functools.partial(outer_kernel, replicas),
        grid=(replicas // PER_STEP,),
        in_specs=[pl.BlockSpec((PER_STEP, rows, cols), lambda i: (i, 0, 0)), whole, whole] + [ANY] * len(after),
        out_specs=[whole, whole, whole],
        out_shape=[
            jax.ShapeDtypeStruct((rows, cols), jnp.float32),
            jax.ShapeDtypeStruct((rows, cols), jnp.float32),
            jax.ShapeDtypeStruct((rows, cols), jnp.bfloat16),
        ],
        scratch_shapes=[pltpu.VMEM((rows, cols), jnp.float32)],
        compiler_params=PARAMS,
        cost_estimate=COST,
        name="outer",
    )(frags, outer_params, outer_moment, *after)


def spread_kernel(source_ref, *refs):
    target_ref = refs[-1]
    for copy in range(target_ref.shape[0]):
        target_ref[copy] = source_ref[...]


def spread(source, copies, *after):
    shape = (copies,) + source.shape
    return pl.pallas_call(
        spread_kernel,
        in_specs=[VMEM] + [ANY] * len(after),
        out_specs=VMEM,
        out_shape=pltpu.VMEM(shape, source.dtype),
        compiler_params=PARAMS,
        cost_estimate=COST,
        name="spread",
    )(source, *after)


PIECES = 4


def merge_kernel(core_ref, mine_ref, theirs_ref, out_ref, held, in_sems, out_sems):
    core = core_ref[0]
    chips = held.shape[1] // PIECES
    reads, writes = [], []
    for piece in range(PIECES):
        at = pl.ds(piece * chips, chips)
        for which, (source, slot) in enumerate(((mine_ref, core), (theirs_ref, 1 - core))):
            sem = which * PIECES + piece
            reads.append(pltpu.make_async_copy(source.at[at], held.at[which, at], in_sems.at[sem]))
            writes.append(
                pltpu.make_async_copy(held.at[which, at], out_ref.at[at, slot], out_sems.at[sem])
            )
    for read in reads:
        read.start()
    for read, write in zip(reads, writes):
        read.wait()
        write.start()
    for write in writes:
        write.wait()


def merge_cores(core, mine, theirs):
    chips, rows, cols = mine.shape
    return pl.pallas_call(
        merge_kernel,
        in_specs=[SMEM, HBM, HBM],
        out_specs=HBM,
        out_shape=jax.ShapeDtypeStruct((chips, N_CORE, rows, cols), mine.dtype),
        scratch_shapes=[
            pltpu.VMEM((N_CORE,) + mine.shape, mine.dtype),
            pltpu.SemaphoreType.DMA((N_CORE * PIECES,)),
            pltpu.SemaphoreType.DMA((N_CORE * PIECES,)),
        ],
        compiler_params=PARAMS,
        name="merge",
    )(core.reshape(1), in_hbm(mine), in_hbm(theirs))


def cut_kernel(count, kept, at_ref, source_ref, *refs):
    targets, (buffer, in_sems, out_sems) = refs[-3 - count : -3], refs[-3:]
    width = buffer.shape[3]
    reads, writes = [], []
    for which in range(count):
        for half in range(N_X):
            columns = pl.ds(pl.multiple_of((at_ref[which] * N_X + half) * width, width), width)
            slot = which * N_X + half
            held = buffer.at[which, half] if which < count - kept else targets[which].at[half]
            reads.append(pltpu.make_async_copy(source_ref.at[:, columns], held, in_sems.at[slot]))
            if which < count - kept:
                writes.append(pltpu.make_async_copy(held, targets[which].at[half], out_sems.at[slot]))
    for read in reads:
        read.start()
    for slot, read in enumerate(reads):
        read.wait()
        if slot < len(writes):
            writes[slot].start()
    for write in writes:
        write.wait()


def cut_columns(tokens, places, width, kept, *after):
    rows = tokens.shape[0]
    count = len(places)
    moved = count - kept
    shape = (N_X, rows, width // N_X)
    return pl.pallas_call(
        functools.partial(cut_kernel, count, kept),
        in_specs=[SMEM, HBM] + [ANY] * len(after),
        out_specs=[HBM] * moved + [VMEM] * kept,
        out_shape=[jax.ShapeDtypeStruct(shape, tokens.dtype)] * moved + [pltpu.VMEM(shape, tokens.dtype)] * kept,
        scratch_shapes=[
            pltpu.VMEM((moved,) + shape, tokens.dtype),
            pltpu.SemaphoreType.DMA((count * N_X,)),
            pltpu.SemaphoreType.DMA((moved * N_X,)),
        ],
        compiler_params=PARAMS,
        cost_estimate=COST,
        name="cut",
    )(jnp.stack(places), in_hbm(tokens), *(in_hbm(one) for one in after))


def behind_kernel(source_ref, *refs):
    target_ref, buffer, in_sems, out_sems = refs[-4:]
    rows = source_ref.shape[0] // 4
    reads, writes = [], []
    for part in range(4):
        at = pl.ds(part * rows, rows)
        reads.append(pltpu.make_async_copy(source_ref.at[at], buffer.at[at], in_sems.at[part]))
        writes.append(pltpu.make_async_copy(buffer.at[at], target_ref.at[at], out_sems.at[part]))
    for read in reads:
        read.start()
    for read, write in zip(reads, writes):
        read.wait()
        write.start()
    for write in writes:
        write.wait()


def behind(source, *after):
    return pl.pallas_call(
        behind_kernel,
        in_specs=[ANY] * (1 + len(after)),
        out_specs=ANY,
        out_shape=jax.ShapeDtypeStruct(source.shape, source.dtype),
        scratch_shapes=[
            pltpu.VMEM(source.shape, source.dtype),
            pltpu.SemaphoreType.DMA((4,)),
            pltpu.SemaphoreType.DMA((4,)),
        ],
        compiler_params=PARAMS,
        cost_estimate=COST,
        name="behind",
    )(in_hbm(source), *(in_hbm(one) for one in after))


def pair_kernel(x_ref, weight_ref, other_ref, gain_ref, pair_ref):
    x = x_ref[0]
    width = weight_ref.shape[1]
    for which, source in enumerate((weight_ref, other_ref)):
        at = x if which == 0 else 1 - x
        factor = jnp.concatenate([gain_ref[at]] * (width // BLOCK), axis=1)
        pair_ref[at] = (source[...].astype(jnp.float32) * factor).astype(jnp.bfloat16)


def scaled_pair(x, weight, other, gain):
    return pl.pallas_call(
        pair_kernel,
        in_specs=[SMEM] + [VMEM] * 3,
        out_specs=VMEM,
        out_shape=pltpu.VMEM((N_X,) + weight.shape, weight.dtype),
        compiler_params=PARAMS,
        cost_estimate=COST,
        name="pair",
    )(x.reshape(1), weight, other, gain)


def own_kernel(token_count, tokens_ref, block_ref, weight_ref, key_target_ref, base_ref, factor_ref):
    wide = tokens_ref[...].astype(jnp.float32)
    inv_rms = lax.rsqrt(jnp.mean(wide * wide, axis=1, keepdims=True) + 1e-05)
    rows = tokens_ref.shape[0]
    at = pl.ds(pl.multiple_of(pl.program_id(0) * rows, rows), rows)
    keys = sum(
        jnp.dot(block_ref[half, at, :], weight_ref[half], preferred_element_type=jnp.float32)
        for half in range(N_X)
    )
    root = jnp.sqrt(jnp.float32(token_count))
    base_ref[...] = (keys * inv_rms - key_target_ref[...].astype(jnp.float32)) / root * inv_rms
    factor_ref[...] = jnp.broadcast_to(inv_rms * inv_rms / root, factor_ref.shape)


def own_part(tokens, block, weight, key_target, token_count):
    rows, depth = tokens.shape
    width = weight.shape[2]
    part = rows // 3
    return pl.pallas_call(
        functools.partial(own_kernel, token_count),
        grid=(3,),
        in_specs=[
            pl.BlockSpec((part, depth), lambda i: (i, 0)),
            VMEM,
            VMEM,
            pl.BlockSpec((part, width), lambda i: (i, 0)),
        ],
        out_specs=[pl.BlockSpec((part, wide), lambda i: (i, 0)) for wide in (width, BLOCK)],
        out_shape=[jax.ShapeDtypeStruct((rows, wide), jnp.float32) for wide in (width, BLOCK)],
        compiler_params=PARAMS,
        cost_estimate=COST,
        name="own",
    )(in_hbm(tokens), block, weight, in_hbm(key_target))


SPLIT = 4


def part_kernel(block_ref, weight_ref, *refs):
    part_ref, kept_ref, sems = refs[-3:]
    rows = kept_ref.shape[1] // SPLIT
    reads = []
    for half in range(N_X):
        for piece in range(SPLIT):
            at = pl.ds(piece * rows, rows)
            reads.append(
                pltpu.make_async_copy(
                    block_ref.at[half, at], kept_ref.at[half, at], sems.at[half * SPLIT + piece]
                )
            )
    for read in reads:
        read.start()
    total = None
    for half in range(N_X):
        for read in reads[half * SPLIT : (half + 1) * SPLIT]:
            read.wait()
        term = jnp.dot(kept_ref[half], weight_ref[half], preferred_element_type=jnp.float32)
        total = term if total is None else total + term
    part_ref[...] = total.astype(jnp.bfloat16)


def key_part(block, weight, *after):
    return pl.pallas_call(
        part_kernel,
        in_specs=[HBM, VMEM] + [ANY] * len(after),
        out_specs=VMEM,
        out_shape=jax.ShapeDtypeStruct((block.shape[1], weight.shape[2]), jnp.bfloat16),
        scratch_shapes=[pltpu.VMEM(block.shape, block.dtype), pltpu.SemaphoreType.DMA((N_X * SPLIT,))],
        compiler_params=PARAMS,
        cost_estimate=COST,
        name="part",
    )(in_hbm(block), weight, *after)


HALVES = 2


def cot_kernel(*refs):
    sources, halves, held, sems = refs[:5], refs[-6 - HALVES : -6], refs[-6:-1], refs[-1]
    reads = [pltpu.make_async_copy(source, target, sems.at[i]) for i, (source, target) in enumerate(zip(sources, held))]
    for read in reads:
        read.start()
    for read in reads:
        read.wait()
    base, factor, first, second, third = held
    width = halves[0].shape[0]
    wide = jnp.concatenate([factor[...]] * (width // BLOCK), axis=1)
    for half, out_ref in enumerate(halves):
        at = pl.ds(half * width, width)
        others = (
            first[:, at].astype(jnp.float32)
            + second[:, at].astype(jnp.float32)
            + third[:, at].astype(jnp.float32)
        )
        out_ref[...] = (base[:, at] + wide * others).T.astype(jnp.bfloat16)


def cotangent(base, factor, parts, *after):
    rows, width = base.shape
    sources = [base, factor, *parts]
    return pl.pallas_call(
        cot_kernel,
        in_specs=[HBM] * 5 + [ANY] * len(after),
        out_specs=[VMEM] * HALVES,
        out_shape=[jax.ShapeDtypeStruct((width // HALVES, rows), jnp.bfloat16)] * HALVES,
        scratch_shapes=[pltpu.VMEM(one.shape, one.dtype) for one in sources] + [pltpu.SemaphoreType.DMA((5,))],
        compiler_params=PARAMS,
        cost_estimate=COST,
        name="cot",
    )(*(in_hbm(one) for one in sources), *after)


def add_kernel(half, own_ref, theirs_ref, *refs):
    out_ref, held, total, in_sems, out_sems = refs[-5:]
    rows, width = theirs_ref.shape
    piece = rows // PIECES
    columns = pl.ds(half * width, width)
    reads, writes = [], []
    for which in range(PIECES):
        at = pl.ds(which * piece, piece)
        reads.append(pltpu.make_async_copy(theirs_ref.at[at], held.at[at], in_sems.at[which]))
        writes.append(pltpu.make_async_copy(total.at[at], out_ref.at[at, columns], out_sems.at[which]))
    for read in reads:
        read.start()
    for which in range(PIECES):
        at = pl.ds(which * piece, piece)
        reads[which].wait()
        total[at, :] = (own_ref[at, columns] + held[at, :].astype(jnp.float32)).astype(jnp.bfloat16)
        writes[which].start()
    for write in writes:
        write.wait()


def add_half(half, own, theirs, before, *after):
    rows, width = theirs.shape
    return pl.pallas_call(
        functools.partial(add_kernel, half),
        in_specs=[VMEM, HBM] + [HBM] * (before is not None) + [ANY] * len(after),
        out_specs=HBM,
        out_shape=jax.ShapeDtypeStruct(own.shape, jnp.bfloat16),
        input_output_aliases={} if before is None else {2: 0},
        scratch_shapes=[
            pltpu.VMEM(theirs.shape, jnp.bfloat16),
            pltpu.VMEM(theirs.shape, jnp.bfloat16),
            pltpu.SemaphoreType.DMA((PIECES,)),
            pltpu.SemaphoreType.DMA((PIECES,)),
        ],
        compiler_params=PARAMS,
        name="add",
    )(own, in_hbm(theirs), *(() if before is None else (before,)), *(in_hbm(one) for one in after))


TILES = 2


def load_kernel(count, *refs):
    sources, gain_ref, targets, gain, sems = refs[:count], refs[count], refs[-2 - count : -2], refs[-2], refs[-1]
    reads = [pltpu.make_async_copy(gain_ref, gain, sems.at[2 * count])]
    for which in range(count):
        for half in range(N_X):
            reads.append(
                pltpu.make_async_copy(
                    sources[which].at[half], targets[which].at[half], sems.at[which * N_X + half]
                )
            )
    for read in reads:
        read.start()
    for read in reads:
        read.wait()


def load_blocks(blocks, gain, *after):
    count = len(blocks)
    kept = [pltpu.VMEM(one.shape, one.dtype) for one in (*blocks, gain)]
    *loaded, gain = pl.pallas_call(
        functools.partial(load_kernel, count),
        in_specs=[HBM] * (count + 1) + [ANY] * len(after),
        out_specs=[VMEM] * (count + 1),
        out_shape=kept,
        scratch_shapes=[pltpu.SemaphoreType.DMA((2 * count + 1,))],
        compiler_params=PARAMS,
        name="load",
    )(*(in_hbm(one) for one in (*blocks, gain)), *after)
    return loaded, gain


def grad_kernel(count, half_ref, *refs):
    blocks, gain_ref, cots, out_ref = refs[:count], refs[count], refs[count + 1 : -1], refs[-1]
    half = half_ref[0]
    width = cots[0].shape[0]
    tile = out_ref.shape[0] // TILES
    for part in range(TILES):
        at = pl.ds(part * tile, tile)
        block = jnp.concatenate([ref[half, :, at] for ref in blocks], axis=0)
        factor = jnp.concatenate([gain_ref[half, at, :]] * (width // BLOCK), axis=1)
        for group in range(len(cots) // count):
            cot = jnp.concatenate([ref[...] for ref in cots[group * count : (group + 1) * count]], axis=1)
            total = jnp.dot(cot, block, preferred_element_type=jnp.float32).T * factor
            out_ref[at, pl.ds(group * width, width)] = total.astype(out_ref.dtype)


def grad_rows(blocks, half, cots, gain, out, cost):
    count = len(blocks)
    return pl.pallas_call(
        functools.partial(grad_kernel, count),
        in_specs=[SMEM] + [VMEM] * (count + 1 + len(cots)),
        out_specs=VMEM,
        out_shape=out,
        compiler_params=PARAMS,
        cost_estimate=cost,
        name="grad",
    )(half.reshape(1), *blocks, gain, *cots)


def per_device(
    activations, norm_gain, key_weight, key_target, replica_frag, outer_params, outer_moment
):
    place = lax.axis_index("fsdp")
    y = place // N_X
    x = place % N_X
    tokens = activations[0]
    quarter = tokens.shape[1] // N_Y
    rows = quarter // N_X
    token_count = tokens.shape[0] * lax.axis_size("fsdp")

    places = {step: lax.rem(y + step, N_Y) for step in (2, 1, 3)}
    sent = {}
    (sent[2],) = cut_columns(tokens, [places[2]], quarter, 0)
    held = {2: send_y(sent[2], 2)}

    fragment = behind(replica_frag[0], sent[2])
    frags = lax.all_to_all(fragment, "rep", 0, 0, tiled=True)
    frags = frags.reshape(lax.axis_size("rep"), -1, fragment.shape[1])

    sent[1], sent[3], own = cut_columns(
        tokens, [places[1], places[3], y], quarter, 0, fragment
    )
    held[1], held[3] = send_y(sent[1], 1), send_y(sent[3], 3)
    weight = key_weight[0]
    other = lax.ppermute(weight, "fsdp", X_SWAP)

    gain = lax.dynamic_slice(norm_gain, (y * quarter,), (quarter,))
    wide_gain = jnp.broadcast_to(gain.reshape(N_X, rows, 1), (N_X, rows, BLOCK))
    pair = scaled_pair(x, weight, other, wide_gain)
    base, factor = own_part(tokens, own, pair, key_target[0], token_count)
    parts = {}
    parts[2] = key_part(held[2], pair, base)
    new_params, new_moment, fresh = outer_step(frags, outer_params, outer_moment, parts[2])
    parts[1] = key_part(held[1], pair, fresh)
    parts[3] = key_part(held[3], pair, parts[1])
    chips = lax.axis_size("rep") // N_CORE
    many = spread(fresh, chips, parts[3])
    others = [send_y(parts[step], N_Y - step) for step in (2, 1, 3)]
    cot = cotangent(base, factor, others, many)
    cots = [[part] + [send_y(part, step) for step in (2, 1, 3)] for part in cot]

    cores = [[chip * N_CORE + core for chip in range(chips)] for core in range(N_CORE)]
    own_rows, cols = fresh.shape
    mine = lax.all_to_all(
        many.reshape(chips * own_rows, cols),
        "rep",
        0,
        0,
        axis_index_groups=cores,
        tiled=True,
    ).reshape(chips, own_rows, cols)
    theirs = lax.ppermute(mine, "rep", [(i, i ^ 1) for i in range(chips * N_CORE)])
    fresh_frag = merge_cores(lax.axis_index("rep") % N_CORE, mine, theirs).reshape(-1, cols)

    blocks, wide_gain = load_blocks([own, held[2], held[1], held[3]], wide_gain, cot[0])
    width = cot[0].shape[0]
    theirs = []
    for half in range(HALVES):
        out = jax.ShapeDtypeStruct((rows, width), jnp.bfloat16)
        part = grad_rows(blocks, 1 - x, cots[half], wide_gain, out, None)
        theirs.append(lax.ppermute(part, "fsdp", X_SWAP))
    out = pltpu.VMEM((rows, HALVES * width), jnp.float32)
    mine_grad = grad_rows(blocks, x, cots[0] + cots[1], wide_gain, out, SHORT)
    weight_grad = add_half(0, mine_grad, theirs[0], None)
    weight_grad = add_half(1, mine_grad, theirs[1], weight_grad, fresh_frag)
    return (new_params, new_moment, fresh_frag, weight_grad[None])


def solution(mesh):
    placed = (
        P("rep", "fsdp", None),
        P(),
        P("rep", "fsdp", None),
        P("rep", "fsdp", None),
        P("rep", "fsdp", None),
        P(("fsdp", "rep"), None),
        P(("fsdp", "rep"), None),
    )
    return jax.shard_map(
        per_device,
        mesh=mesh,
        in_specs=placed,
        out_specs=(
            P(("fsdp", "rep"), None),
            P(("fsdp", "rep"), None),
            P("fsdp", None),
            P("rep", "fsdp", None),
        ),
        check_vma=False,
    )
```

time: 195 us -> 149 us (0.76)
  waiting for transfers between devices: 92.5 us -> 38.9 us
  Pallas kernels: 9.14 us -> 55.6 us
  matrix products: 28 us -> 0 us
  starting transfers between devices: 30 us -> 43.7 us
  between operations: 14.3 us -> 1.11 us
  other arithmetic: 8.84 us -> 0.08 us
    pallas_call x0 -> x17, Pallas kernels: none -> 48 us  [the longest x3 9.82 us: key_part(): pl.pallas_call(part_kernel, in_specs=[HBM, VMEM] + [ANY] * len(after), ou...]
    ppermute x1, waiting for transfers between devices: 37.8 us -> 3.66 us  [per_device(): other = lax.ppermute(weight, 'fsdp', X_SWAP)]
    dot_general x12 -> x0, matrix products: 28 us -> none  [the longest x8 15.7 us: grad(): lax.dot_general(lax.dynamic_slice(block, (0, at * rows), (block.shape[0],...]
    ppermute x9 -> x12, waiting for transfers between devices: 33.7 us -> 10.1 us  [send_y(): return lax.ppermute(block, 'fsdp', y_shift(step))]
    all_to_all x1, waiting for transfers between devices: 0.01 us -> 20.2 us  [per_device(): frags = lax.all_to_all(fragment, 'rep', 0, 0, tiled=True)]
    ppermute x1 -> x3, waiting for transfers between devices: 16 us -> 5 us  [the longest x2 4.99 us: per_device(): theirs.append(lax.ppermute(part, 'fsdp', X_SWAP))]
    all_to_all x0 -> x1, starting transfers between devices: none -> 7.74 us  [per_device(): lax.all_to_all(many.reshape(chips * own_rows, cols), 'rep', 0, 0, axis_in...]
    ppermute x9 -> x12, starting transfers between devices: 14.7 us -> 20.9 us  [send_y(): return lax.ppermute(block, 'fsdp', y_shift(step))]
  transfers between devices with their start and end apart: 13 -> 18, of which waited for: 6 -> 9; matrix products, arithmetic and copies ran while one was open for 22% -> 1% of each run, Pallas kernels for 5% -> 37%
where the time goes in v2:
time: 149 us; the launch traced here: 147 us
  Pallas kernels  55.6 us (37%)
  starting transfers between devices  43.7 us (29%)
  waiting for transfers between devices  38.9 us (26%)
  local copies, waits for them, and re-layouts  7.73 us (5%)
    ppermute x12, starting transfers between devices, send_y(): return lax.ppermute(block, 'fsdp', y_shift(step))  20.9 us
    all_to_all x1, waiting for transfers between devices, per_device(): frags = lax.all_to_all(fragment, 'rep', 0, 0, tiled=True)  20.2 us
    ppermute x12, waiting for transfers between devices, send_y(): return lax.ppermute(block, 'fsdp', y_shift(step))  10.1 us
    pallas_call x3, Pallas kernels, key_part(): pl.pallas_call(part_kernel, in_specs=[HBM, VMEM] + [ANY] * len(after), ou...  9.82 us
    pallas_call x3, Pallas kernels, grad_rows(): pl.pallas_call(functools.partial(grad_kernel, count), in_specs=[SMEM] + [...  9.72 us
    all_to_all x1, starting transfers between devices, per_device(): frags = lax.all_to_all(fragment, 'rep', 0, 0, tiled=True)  8.83 us
    all_to_all x1, starting transfers between devices, per_device(): lax.all_to_all(many.reshape(chips * own_rows, cols), 'rep', 0, 0, axis_in...  7.74 us
    pallas_call x1, Pallas kernels, outer_step(): pl.pallas_call(functools.partial(outer_kernel, replicas), grid=(replicas...  7.67 us
  transfers between devices with their start and end apart: 18, of which 9 were waited for; matrix products, arithmetic and copies ran while one was open for 1% of the time, Pallas kernels for 37%

profile of v2, /device:TPU:32, one launch (start us, length us, event | category | flops | bytes accessed | tf_op | source)
XLA Modules:
  0.0 147.2 jit_solution(6622969834915315006)
XLA Ops:
  0.6 3.1 %collective-permute-start.1 = (bf16[1024,512]{1,0:T(8,128)(2,1)}, bf16[1024,512]{1,0:T(8,128)(2,1)}, u32[]{:S(2)}, u32[]{:S(2)}) collective-permute-start(bf16[1024,512]{1,0:T(8,128)(2,1)} %bitcast.14), channel_id=1, source_target_pairs={{0,1},{1,0},{2,3},{3,2},{4,5},{5,4},{6,7},{7,6},{8,9},{9,8},{10,11... | collective-permute-start | bytes 3145736 | tf_op jit(solution)/shard_map/ppermute | solution.py:526
  3.7 2.3 %cut.2.refs_0_ = bf16[2,384,1024]{2,1,0:T(8,128)(2,1)} custom-call(s32[1]{0:T(128)} %bitcast.1.at_ref, bf16[384,8192]{1,0:T(8,128)(2,1)} %bitcast.19), custom_call_target="tpu_custom_call" | custom-call | flops 999999995904 | bytes 1000000000 | tf_op jit(solution)/shard_map/cut/pallas_call | solution.py:216
  6.1 3.3 %collective-permute-start = (bf16[2,384,1024]{2,1,0:T(8,128)(2,1)}, bf16[2,384,1024]{2,1,0:T(8,128)(2,1)}, u32[]{:S(2)}, u32[]{:S(2)}) collective-permute-start(bf16[2,384,1024]{2,1,0:T(8,128)(2,1)} %cut.2.refs_0_), channel_id=1, source_target_pairs={{0,4},{1,5},{2,6},{3,7},{4,0},{5,1},{6,2},{7,3},{8,12},{9,13},{10,... | collective-permute-start | bytes 4718600 | tf_op jit(solution)/shard_map/ppermute | solution.py:38
  9.3 2.4 %behind.1.refs_0_ = bf16[1024,1024]{1,0:T(8,128)(2,1)} custom-call(bf16[1024,1024]{1,0:T(8,128)(2,1)} %bitcast.22, bf16[2,384,1024]{2,1,0:T(8,128)(2,1)} %cut.2.refs_0_), custom_call_target="tpu_custom_call" | custom-call | flops 999999995904 | bytes 1000000000 | tf_op jit(solution)/shard_map/behind/pallas_call | solution.py:250
  11.8 8.8 %all-to-all-start = ((bf16[32,32,1024]{2,1,0:T(8,128)(2,1)}), bf16[32,32,1024]{2,1,0:T(8,128)(2,1)}, u32[]{:S(2)}, u32[]{:S(2)}) async-start(bf16[32,32,1024]{2,1,0:T(8,128)(2,1)} %bitcast.3), calls=%async_computation | async-start | bytes 4194304 | tf_op jit(solution)/shard_map/all_to_all | solution.py:518
  20.7 3.8 %cut.3 = (bf16[2,384,1024]{2,1,0:T(8,128)(2,1)}, bf16[2,384,1024]{2,1,0:T(8,128)(2,1)}, bf16[2,384,1024]{2,1,0:T(8,128)(2,1)S(1)}) custom-call(s32[3]{0:T(128)S(1)} %pad_add_fusion.at_ref, bf16[384,8192]{1,0:T(8,128)(2,1)} %bitcast.20, bf16[1024,1024]{1,0:T(8,128)(2,1)} %behind.1.refs_0_), custom_call_target="tpu_custom_call" | custom-call | flops 999999995904 | bytes 1000000000 | tf_op jit(solution)/shard_map/cut/pallas_call | solution.py:216
  24.5 0.8 collective-permute-start.3
  25.2 2.6 %collective-permute-start.2 = (bf16[2,384,1024]{2,1,0:T(8,128)(2,1)}, bf16[2,384,1024]{2,1,0:T(8,128)(2,1)}, u32[]{:S(2)}, u32[]{:S(2)}) collective-permute-start(bf16[2,384,1024]{2,1,0:T(8,128)(2,1)} %get-tuple-element.24), channel_id=1, source_target_pairs={{0,6},{1,7},{2,0},{3,1},{4,2},{5,3},{6,4},{7,5},{8,14},{9,15},{10,... | collective-permute-start | bytes 4718600 | tf_op jit(solution)/shard_map/ppermute | solution.py:38
  27.8 0.7 dynamic_slice.3
  28.5 3.7 %collective-permute-done.1.other_ref = bf16[1024,512]{1,0:T(8,128)(2,1)} collective-permute-done((bf16[1024,512]{1,0:T(8,128)(2,1)}, bf16[1024,512]{1,0:T(8,128)(2,1)}, u32[]{:S(2)}, u32[]{:S(2)}) %collective-permute-start.1) | collective-permute-done | bytes 1048608 | tf_op jit(solution)/shard_map/ppermute | solution.py:526
  32.5 2.0 %pair.1.weight_ref = bf16[2,1024,512]{2,1,0:T(8,128)(2,1)S(1)} custom-call(s32[1]{0:T(128)} %bitcast.4.x_ref.half_ref, bf16[1024,512]{1,0:T(8,128)(2,1)S(1)} %bitcast.15, bf16[1024,512]{1,0:T(8,128)(2,1)} %collective-permute-done.1.other_ref, f32[2,1024,128]{2,1,0:T(8,128)S(1)} %broadcast_in_dim.11.gain_ref.refs_4_), custom_call_target="tpu_custom_call" | custom-call | flops 999999995904 | bytes 1000000000 | tf_op jit(solution)/shard_map/pair/pallas_call | solution.py:276
  34.6 5.8 %own.1 = (f32[384,512]{1,0:T(8,128)S(1)}, f32[384,128]{1,0:T(8,128)S(1)}) custom-call(bf16[384,8192]{1,0:T(8,128)(2,1)} %bitcast.21, bf16[2,384,1024]{2,1,0:T(8,128)(2,1)S(1)} %get-tuple-element.19.block_ref.refs_0_, bf16[2,1024,512]{2,1,0:T(8,128)(2,1)S(1)} %pair.1.weight_ref, bf16[384,512]{1,0:T(8,128)(2,1)} %bitcast.23), custom_call_target="tpu_custom_call" | custom-call | flops 999999995904 | bytes 1000000000 | tf_op jit(solution)/shard_map/own/pallas_call | solution.py:305
  40.3 5.0 %collective-permute-done.block_ref.refs_1_ = bf16[2,384,1024]{2,1,0:T(8,128)(2,1)} collective-permute-done((bf16[2,384,1024]{2,1,0:T(8,128)(2,1)}, bf16[2,384,1024]{2,1,0:T(8,128)(2,1)}, u32[]{:S(2)}, u32[]{:S(2)}) %collective-permute-start) | collective-permute-done | bytes 1572896 | tf_op jit(solution)/shard_map/ppermute | solution.py:38
  45.3 3.3 %part.3.refs_0_ = bf16[384,512]{1,0:T(8,128)(2,1)} custom-call(bf16[2,384,1024]{2,1,0:T(8,128)(2,1)} %collective-permute-done.block_ref.refs_1_, bf16[2,1024,512]{2,1,0:T(8,128)(2,1)S(1)} %pair.1.weight_ref, f32[384,512]{1,0:T(8,128)S(1)} %get-tuple-element.20.refs_0_), custom_call_target="tpu_custom_call" | custom-call | flops 999999995904 | bytes 1000000000 | tf_op jit(solution)/shard_map/part/pallas_call | solution.py:349
  48.7 3.3 %collective-permute-start.5 = (bf16[384,512]{1,0:T(8,128)(2,1)}, bf16[384,512]{1,0:T(8,128)(2,1)}, u32[]{:S(2)}, u32[]{:S(2)}) collective-permute-start(bf16[384,512]{1,0:T(8,128)(2,1)} %part.3.refs_0_), channel_id=1, source_target_pairs={{0,4},{1,5},{2,6},{3,7},{4,0},{5,1},{6,2},{7,3},{8,12},{9,13},{10,... | collective-permute-start | bytes 1179656 | tf_op jit(solution)/shard_map/ppermute | solution.py:38
  51.9 20.2 %all-to-all-done.frag_ref = bf16[32,32,1024]{2,1,0:T(8,128)(2,1)} async-done(((bf16[32,32,1024]{2,1,0:T(8,128)(2,1)}), bf16[32,32,1024]{2,1,0:T(8,128)(2,1)}, u32[]{:S(2)}, u32[]{:S(2)}) %all-to-all-start) | async-done | bytes 2097184 | tf_op jit(solution)/shard_map/all_to_all | solution.py:518
  72.1 7.7 %outer.1 = (f32[32,1024]{1,0:T(8,128)}, f32[32,1024]{1,0:T(8,128)}, bf16[32,1024]{1,0:T(8,128)(2,1)S(1)}) custom-call(bf16[32,32,1024]{2,1,0:T(8,128)(2,1)} %all-to-all-done.frag_ref, f32[32,1024]{1,0:T(8,128)S(1)} %copy-done.12, f32[32,1024]{1,0:T(8,128)S(1)} %copy-done.13, bf16[384,512]{1,0:T(8,128)(2,1)} %part.3.refs_0_), custom_call_target="tpu_custom_call" | custom-call | flops 999999995904 | bytes 1000000000 | tf_op jit(solution)/shard_map/outer/pallas_call | solution.py:112
  79.8 3.3 %part.4.refs_0_ = bf16[384,512]{1,0:T(8,128)(2,1)} custom-call(bf16[2,384,1024]{2,1,0:T(8,128)(2,1)} %collective-permute-done.3.block_ref.refs_2_, bf16[2,1024,512]{2,1,0:T(8,128)(2,1)S(1)} %copy-done.15, bf16[32,1024]{1,0:T(8,128)(2,1)S(1)} %get-tuple-element.23.refs_0_.source_ref), custom_call_target="tpu_custom_call" | custom-call | flops 999999995904 | bytes 1000000000 | tf_op jit(solution)/shard_map/part/pallas_call | solution.py:349
  83.1 1.1 collective-permute-start.6
  84.2 3.3 %part.5.refs_0_ = bf16[384,512]{1,0:T(8,128)(2,1)} custom-call(bf16[2,384,1024]{2,1,0:T(8,128)(2,1)} %collective-permute-done.2.block_ref.refs_3_, bf16[2,1024,512]{2,1,0:T(8,128)(2,1)S(1)} %copy-done.15, bf16[384,512]{1,0:T(8,128)(2,1)} %part.4.refs_0_), custom_call_target="tpu_custom_call" | custom-call | flops 999999995904 | bytes 1000000000 | tf_op jit(solution)/shard_map/part/pallas_call | solution.py:349
  87.5 1.0 collective-permute-start.7
  88.5 1.0 spread.1.refs_5_
  89.6 7.7 %all-to-all-start.1 = ((bf16[16,32,1024]{2,1,0:T(8,128)(2,1)}), bf16[16,32,1024]{2,1,0:T(8,128)(2,1)}, u32[]{:S(2)}, u32[]{:S(2)}) async-start(bf16[16,32,1024]{2,1,0:T(8,128)(2,1)} %spread.1.refs_5_), calls=%async_computation.1 | async-start | bytes 2097152 | tf_op jit(solution)/shard_map/all_to_all | solution.py:545
  97.3 2.1 %collective-permute-done.7.refs_4_ = bf16[384,512]{1,0:T(8,128)(2,1)} collective-permute-done((bf16[384,512]{1,0:T(8,128)(2,1)}, bf16[384,512]{1,0:T(8,128)(2,1)}, u32[]{:S(2)}, u32[]{:S(2)}) %collective-permute-start.7) | collective-permute-done | bytes 393248 | tf_op jit(solution)/shard_map/ppermute | solution.py:38
  99.5 1.8 %cot.1 = (bf16[256,384]{1,0:T(8,128)(2,1)S(1)}, bf16[256,384]{1,0:T(8,128)(2,1)S(1)}) custom-call(f32[384,512]{1,0:T(8,128)} %copy-done.16, f32[384,128]{1,0:T(8,128)} %copy-done.17, bf16[384,512]{1,0:T(8,128)(2,1)} %collective-permute-done.5.refs_2_, bf16[384,512]{1,0:T(8,128)(2,1)} %collective-permute-done.6.refs_3_, ...), custom_call_target="tpu_custom_call" | custom-call | flops 999999995904 | bytes 1000000000 | tf_op jit(solution)/shard_map/cot/pallas_call | solution.py:387
  101.3 1.1 collective-permute-start.10
  102.4 0.8 collective-permute-start.8
  103.9 3.7 %collective-permute-start.11 = (bf16[256,384]{1,0:T(8,128)(2,1)S(1)}, bf16[256,384]{1,0:T(8,128)(2,1)}, u32[]{:S(2)}, u32[]{:S(2)}) collective-permute-start(bf16[256,384]{1,0:T(8,128)(2,1)S(1)} %get-tuple-element.33.refs_9_.refs_5_), channel_id=1, source_target_pairs={{0,4},{1,5},{2,6},{3,7},{4,0},{5,1},{6,2},{7,3},{8,12},{9,13},{10,... | collective-permute-start | bytes 589832 | tf_op jit(solution)/shard_map/ppermute | solution.py:38
  107.6 1.7 %collective-permute-done.10.refs_8_ = bf16[256,384]{1,0:T(8,128)(2,1)S(1)} collective-permute-done((bf16[256,384]{1,0:T(8,128)(2,1)S(1)}, bf16[256,384]{1,0:T(8,128)(2,1)S(1)}, u32[]{:S(2)}, u32[]{:S(2)}) %collective-permute-start.10) | collective-permute-done | bytes 196640 | tf_op jit(solution)/shard_map/ppermute | solution.py:38
  109.3 0.7 copy-done.8
  109.9 2.6 %collective-permute-start.13 = (bf16[256,384]{1,0:T(8,128)(2,1)S(1)}, bf16[256,384]{1,0:T(8,128)(2,1)}, u32[]{:S(2)}, u32[]{:S(2)}) collective-permute-start(bf16[256,384]{1,0:T(8,128)(2,1)S(1)} %get-tuple-element.33.refs_9_.refs_5_), channel_id=1, source_target_pairs={{0,6},{1,7},{2,0},{3,1},{4,2},{5,3},{6,4},{7,5},{8,14},{9,15},{10,... | collective-permute-start | bytes 589832 | tf_op jit(solution)/shard_map/ppermute | solution.py:38
  112.5 3.2 %load.1 = (bf16[2,384,1024]{2,1,0:T(8,128)(2,1)S(1)}, bf16[2,384,1024]{2,1,0:T(8,128)(2,1)S(1)}, bf16[2,384,1024]{2,1,0:T(8,128)(2,1)S(1)}, bf16[2,384,1024]{2,1,0:T(8,128)(2,1)S(1)}, f32[2,1024,128]{2,1,0:T(8,128)S(1)}) custom-call(bf16[2,384,1024]{2,1,0:T(8,128)(2,1)} %copy-done.7, bf16[2,384,1024]{2,1,0:T(8,128)(2,1)} %collective-permute-done.block_ref.refs_1_, ...), custom_call_target="tpu_custom_call" | custom-call | tf_op jit(solution)/shard_map/load/pallas_call | solution.py:461
  115.8 0.9 collective-permute-done.9.refs_7_
  116.7 3.4 %grad.5 = bf16[1024,256]{1,0:T(8,128)(2,1)} custom-call(s32[1]{0:T(128)} %bitcast.12.half_ref, bf16[2,384,1024]{2,1,0:T(8,128)(2,1)S(1)} %get-tuple-element.28.refs_0_, bf16[2,384,1024]{2,1,0:T(8,128)(2,1)S(1)} %get-tuple-element.29.refs_1_, bf16[2,384,1024]{2,1,0:T(8,128)(2,1)S(1)} %get-tuple-element.30.refs_2_, ...), custom_call_target="tpu_custom_call" | custom-call | tf_op jit(solution)/shard_map/grad/pallas_call | solution.py:490
  120.1 1.6 %collective-permute-start.15 = (bf16[1024,256]{1,0:T(8,128)(2,1)}, bf16[1024,256]{1,0:T(8,128)(2,1)}, u32[]{:S(2)}, u32[]{:S(2)}) collective-permute-start(bf16[1024,256]{1,0:T(8,128)(2,1)} %grad.5), channel_id=1, source_target_pairs={{0,1},{1,0},{2,3},{3,2},{4,5},{5,4},{6,7},{7,6},{8,9},{9,8},{10,11... | collective-permute-start | bytes 1572872 | tf_op jit(solution)/shard_map/ppermute | solution.py:562
  122.1 3.0 %grad.4 = bf16[1024,256]{1,0:T(8,128)(2,1)} custom-call(s32[1]{0:T(128)} %bitcast.12.half_ref, bf16[2,384,1024]{2,1,0:T(8,128)(2,1)S(1)} %get-tuple-element.28.refs_0_, bf16[2,384,1024]{2,1,0:T(8,128)(2,1)S(1)} %get-tuple-element.29.refs_1_, bf16[2,384,1024]{2,1,0:T(8,128)(2,1)S(1)} %get-tuple-element.30.refs_2_, ...), custom_call_target="tpu_custom_call" | custom-call | tf_op jit(solution)/shard_map/grad/pallas_call | solution.py:490
  125.1 1.6 %collective-permute-start.14 = (bf16[1024,256]{1,0:T(8,128)(2,1)}, bf16[1024,256]{1,0:T(8,128)(2,1)}, u32[]{:S(2)}, u32[]{:S(2)}) collective-permute-start(bf16[1024,256]{1,0:T(8,128)(2,1)} %grad.4), channel_id=1, source_target_pairs={{0,1},{1,0},{2,3},{3,2},{4,5},{5,4},{6,7},{7,6},{8,9},{9,8},{10,11... | collective-permute-start | bytes 1572872 | tf_op jit(solution)/shard_map/ppermute | solution.py:562
  126.7 1.4 copy-done.1
  128.1 1.4 copy-done.3
  129.5 1.2 copy-done.5
  130.8 0.9 copy-done.10
  131.7 3.2 %grad.3.own_ref = f32[1024,512]{1,0:T(8,128)S(1)} custom-call(s32[1]{0:T(128)} %bitcast.4.x_ref.half_ref, bf16[2,384,1024]{2,1,0:T(8,128)(2,1)S(1)} %get-tuple-element.28.refs_0_, bf16[2,384,1024]{2,1,0:T(8,128)(2,1)S(1)} %get-tuple-element.29.refs_1_, bf16[2,384,1024]{2,1,0:T(8,128)(2,1)S(1)} %copy-done.1, bf16[2,384,1024]{2,1,0:T(8,128)(2,1)S(1)} %copy-done.3, ...), custom_call_target="tpu_custom_call" | custom-call | flops 20000000000 | bytes 1000000 | tf_op jit(solution)/shard_map/grad/pallas_call | solution.py:490
  134.9 1.8 %collective-permute-done.15.theirs_ref = bf16[1024,256]{1,0:T(8,128)(2,1)} collective-permute-done((bf16[1024,256]{1,0:T(8,128)(2,1)}, bf16[1024,256]{1,0:T(8,128)(2,1)}, u32[]{:S(2)}, u32[]{:S(2)}) %collective-permute-start.15) | collective-permute-done | bytes 524320 | tf_op jit(solution)/shard_map/ppermute | solution.py:562
  136.8 1.8 %add.32.refs_0_ = bf16[1024,512]{1,0:T(8,128)(2,1)} custom-call(f32[1024,512]{1,0:T(8,128)S(1)} %grad.3.own_ref, bf16[1024,256]{1,0:T(8,128)(2,1)} %collective-permute-done.15.theirs_ref), custom_call_target="tpu_custom_call" | custom-call | tf_op jit(solution)/shard_map/add/pallas_call | solution.py:422
  138.7 1.0 copy-done.20
  139.7 2.4 %merge.1 = bf16[16,2,32,1024]{3,2,1,0:T(8,128)(2,1)} custom-call(s32[1]{0:T(128)} %bitcast.10.core_ref, bf16[16,32,1024]{2,1,0:T(8,128)(2,1)} %all-to-all-done.1.mine_ref, bf16[16,32,1024]{2,1,0:T(8,128)(2,1)} %copy-done.20), custom_call_target="tpu_custom_call" | custom-call | tf_op jit(solution)/shard_map/merge/pallas_call | solution.py:174
  142.1 3.1 %collective-permute-done.14.theirs_ref = bf16[1024,256]{1,0:T(8,128)(2,1)} collective-permute-done((bf16[1024,256]{1,0:T(8,128)(2,1)}, bf16[1024,256]{1,0:T(8,128)(2,1)}, u32[]{:S(2)}, u32[]{:S(2)}) %collective-permute-start.14) | collective-permute-done | bytes 524320 | tf_op jit(solution)/shard_map/ppermute | solution.py:562
  145.2 1.8 %add.33 = bf16[1024,512]{1,0:T(8,128)(2,1)} custom-call(f32[1024,512]{1,0:T(8,128)S(1)} %grad.3.own_ref, bf16[1024,256]{1,0:T(8,128)(2,1)} %collective-permute-done.14.theirs_ref, bf16[1024,512]{1,0:T(8,128)(2,1)} %add.32.refs_0_, bf16[1024,1024]{1,0:T(8,128)(2,1)} %bitcast.16), custom_call_target="tpu_custom_call", output_to_operand_aliasing={{}: (2, {})} | custom-call | tf_op jit(solution)/shard_map/add/pallas_call | solution.py:422
  (52 shorter events, 1.5 us)
Async XLA Ops:
  0.6 31.5 %collective-permute-start.1 = (bf16[1024,512]{1,0:T(8,128)(2,1)}, bf16[1024,512]{1,0:T(8,128)(2,1)}, u32[]{:S(2)}, u32[]{:S(2)}) collective-permute-start(bf16[1024,512]{1,0:T(8,128)(2,1)} %bitcast.14), channel_id=1, source_target_pairs={{0,1},{1,0},{2,3},{3,2},{4,5},{5,4},{6,7},{7,6},{8,9},{9,8},{10,11... | collective-permute-start | bytes 3145736 | tf_op jit(solution)/shard_map/ppermute | solution.py:526
  6.1 39.3 %collective-permute-start = (bf16[2,384,1024]{2,1,0:T(8,128)(2,1)}, bf16[2,384,1024]{2,1,0:T(8,128)(2,1)}, u32[]{:S(2)}, u32[]{:S(2)}) collective-permute-start(bf16[2,384,1024]{2,1,0:T(8,128)(2,1)} %cut.2.refs_0_), channel_id=1, source_target_pairs={{0,4},{1,5},{2,6},{3,7},{4,0},{5,1},{6,2},{7,3},{8,12},{9,13},{10,... | collective-permute-start | bytes 4718600 | tf_op jit(solution)/shard_map/ppermute | solution.py:38
  11.8 60.3 %all-to-all-start = ((bf16[32,32,1024]{2,1,0:T(8,128)(2,1)}), bf16[32,32,1024]{2,1,0:T(8,128)(2,1)}, u32[]{:S(2)}, u32[]{:S(2)}) async-start(bf16[32,32,1024]{2,1,0:T(8,128)(2,1)} %bitcast.3), calls=%async_computation | async-start | bytes 4194304 | tf_op jit(solution)/shard_map/all_to_all | solution.py:518
  20.7 11.8 %copy-start.11 = (bf16[1,1024,512]{2,1,0:T(8,128)(2,1)S(1)}, bf16[1,1024,512]{2,1,0:T(8,128)(2,1)}, u32[]{:S(2)}) copy-start(bf16[1,1024,512]{2,1,0:T(8,128)(2,1)} %param.9) | copy-start | bytes 3145732
  24.5 10.1 %copy-start.7 = (bf16[2,384,1024]{2,1,0:T(8,128)(2,1)}, bf16[2,384,1024]{2,1,0:T(8,128)(2,1)S(1)}, u32[]{:S(2)}) copy-start(bf16[2,384,1024]{2,1,0:T(8,128)(2,1)S(1)} %get-tuple-element.19.block_ref.refs_0_) | copy-start | bytes 4718596
  24.5 55.3 %collective-permute-start.3 = (bf16[2,384,1024]{2,1,0:T(8,128)(2,1)}, bf16[2,384,1024]{2,1,0:T(8,128)(2,1)}, u32[]{:S(2)}, u32[]{:S(2)}) collective-permute-start(bf16[2,384,1024]{2,1,0:T(8,128)(2,1)} %get-tuple-element.25), channel_id=1, source_target_pairs={{0,2},{1,3},{2,4},{3,5},{4,6},{5,7},{6,0},{7,1},{8,10},{9,11},{10,... | collective-permute-start | bytes 4718600 | tf_op jit(solution)/shard_map/ppermute | solution.py:38
  25.2 59.0 %collective-permute-start.2 = (bf16[2,384,1024]{2,1,0:T(8,128)(2,1)}, bf16[2,384,1024]{2,1,0:T(8,128)(2,1)}, u32[]{:S(2)}, u32[]{:S(2)}) collective-permute-start(bf16[2,384,1024]{2,1,0:T(8,128)(2,1)} %get-tuple-element.24), channel_id=1, source_target_pairs={{0,6},{1,7},{2,0},{3,1},{4,2},{5,3},{6,4},{7,5},{8,14},{9,15},{10,... | collective-permute-start | bytes 4718600 | tf_op jit(solution)/shard_map/ppermute | solution.py:38
  32.5 2.0 %copy-start.6 = (f32[2,1024,128]{2,1,0:T(8,128)}, f32[2,1024,128]{2,1,0:T(8,128)S(1)}, u32[]{:S(2)}) copy-start(f32[2,1024,128]{2,1,0:T(8,128)S(1)} %broadcast_in_dim.11.gain_ref.refs_4_) | copy-start | bytes 3145732
  34.5 10.8 %copy-start.14 = (bf16[2,1024,512]{2,1,0:T(8,128)(2,1)}, bf16[2,1024,512]{2,1,0:T(8,128)(2,1)S(1)}, u32[]{:S(2)}) copy-start(bf16[2,1024,512]{2,1,0:T(8,128)(2,1)S(1)} %pair.1.weight_ref) | copy-start | bytes 6291460
  40.3 8.3 %copy-start.16 = (f32[384,512]{1,0:T(8,128)}, f32[384,512]{1,0:T(8,128)S(1)}, u32[]{:S(2)}) copy-start(f32[384,512]{1,0:T(8,128)S(1)} %get-tuple-element.20.refs_0_) | copy-start | bytes 2359300
  40.3 8.3 %copy-start.17 = (f32[384,128]{1,0:T(8,128)}, f32[384,128]{1,0:T(8,128)S(1)}, u32[]{:S(2)}) copy-start(f32[384,128]{1,0:T(8,128)S(1)} %get-tuple-element.26.refs_1_) | copy-start | bytes 589828
  45.3 26.8 %copy-start.12 = (f32[32,1024]{1,0:T(8,128)S(1)}, f32[32,1024]{1,0:T(8,128)}, u32[]{:S(2)}) copy-start(f32[32,1024]{1,0:T(8,128)} %params_ref.1) | copy-start | bytes 393220
  45.3 26.8 %copy-start.13 = (f32[32,1024]{1,0:T(8,128)S(1)}, f32[32,1024]{1,0:T(8,128)}, u32[]{:S(2)}) copy-start(f32[32,1024]{1,0:T(8,128)} %moment_ref.1) | copy-start | bytes 393220
  48.7 48.7 %collective-permute-start.5 = (bf16[384,512]{1,0:T(8,128)(2,1)}, bf16[384,512]{1,0:T(8,128)(2,1)}, u32[]{:S(2)}, u32[]{:S(2)}) collective-permute-start(bf16[384,512]{1,0:T(8,128)(2,1)} %part.3.refs_0_), channel_id=1, source_target_pairs={{0,4},{1,5},{2,6},{3,7},{4,0},{5,1},{6,2},{7,3},{8,12},{9,13},{10,... | collective-permute-start | bytes 1179656 | tf_op jit(solution)/shard_map/ppermute | solution.py:38
  72.1 7.7 %copy-start.15 = (bf16[2,1024,512]{2,1,0:T(8,128)(2,1)S(1)}, bf16[2,1024,512]{2,1,0:T(8,128)(2,1)}, u32[]{:S(2)}) copy-start(bf16[2,1024,512]{2,1,0:T(8,128)(2,1)} %copy-done.14) | copy-start | bytes 6291460
  79.8 3.3 %copy-start.18 = (bf16[32,1024]{1,0:T(8,128)(2,1)}, bf16[32,1024]{1,0:T(8,128)(2,1)S(1)}, u32[]{:S(2)}) copy-start(bf16[32,1024]{1,0:T(8,128)(2,1)S(1)} %get-tuple-element.23.refs_0_.source_ref) | copy-start | bytes 196612
  83.1 16.4 %collective-permute-start.6 = (bf16[384,512]{1,0:T(8,128)(2,1)}, bf16[384,512]{1,0:T(8,128)(2,1)}, u32[]{:S(2)}, u32[]{:S(2)}) collective-permute-start(bf16[384,512]{1,0:T(8,128)(2,1)} %part.4.refs_0_), channel_id=1, source_target_pairs={{0,6},{1,7},{2,0},{3,1},{4,2},{5,3},{6,4},{7,5},{8,14},{9,15},{10,... | collective-permute-start | bytes 1179656 | tf_op jit(solution)/shard_map/ppermute | solution.py:38
  84.2 4.3 %copy-start.19 = (bf16[32,1024]{1,0:T(8,128)(2,1)S(1)}, bf16[32,1024]{1,0:T(8,128)(2,1)}, u32[]{:S(2)}) copy-start(bf16[32,1024]{1,0:T(8,128)(2,1)} %copy-done.18) | copy-start | bytes 196612
  87.5 12.0 %collective-permute-start.7 = (bf16[384,512]{1,0:T(8,128)(2,1)}, bf16[384,512]{1,0:T(8,128)(2,1)}, u32[]{:S(2)}, u32[]{:S(2)}) collective-permute-start(bf16[384,512]{1,0:T(8,128)(2,1)} %part.5.refs_0_), channel_id=1, source_target_pairs={{0,2},{1,3},{2,4},{3,5},{4,6},{5,7},{6,0},{7,1},{8,10},{9,11},{10,... | collective-permute-start | bytes 1179656 | tf_op jit(solution)/shard_map/ppermute | solution.py:38
  89.6 37.1 %all-to-all-start.1 = ((bf16[16,32,1024]{2,1,0:T(8,128)(2,1)}), bf16[16,32,1024]{2,1,0:T(8,128)(2,1)}, u32[]{:S(2)}, u32[]{:S(2)}) async-start(bf16[16,32,1024]{2,1,0:T(8,128)(2,1)} %spread.1.refs_5_), calls=%async_computation.1 | async-start | bytes 2097152 | tf_op jit(solution)/shard_map/all_to_all | solution.py:545
  101.3 7.9 %collective-permute-start.10 = (bf16[256,384]{1,0:T(8,128)(2,1)S(1)}, bf16[256,384]{1,0:T(8,128)(2,1)S(1)}, u32[]{:S(2)}, u32[]{:S(2)}) collective-permute-start(bf16[256,384]{1,0:T(8,128)(2,1)S(1)} %get-tuple-element.27.refs_5_), channel_id=1, source_target_pairs={{0,6},{1,7},{2,0},{3,1},{4,2},{5,3},{6,4},{7,5},{8,14},{9,15},{10,... | collective-permute-start | bytes 589832 | tf_op jit(solution)/shard_map/ppermute | solution.py:38
  102.4 13.4 %collective-permute-start.8 = (bf16[256,384]{1,0:T(8,128)(2,1)S(1)}, bf16[256,384]{1,0:T(8,128)(2,1)}, u32[]{:S(2)}, u32[]{:S(2)}) collective-permute-start(bf16[256,384]{1,0:T(8,128)(2,1)S(1)} %get-tuple-element.27.refs_5_), channel_id=1, source_target_pairs={{0,4},{1,5},{2,6},{3,7},{4,0},{5,1},{6,2},{7,3},{8,12},{9,13},{10,... | collective-permute-start | bytes 589832 | tf_op jit(solution)/shard_map/ppermute | solution.py:38
  103.2 13.4 %collective-permute-start.9 = (bf16[256,384]{1,0:T(8,128)(2,1)S(1)}, bf16[256,384]{1,0:T(8,128)(2,1)}, u32[]{:S(2)}, u32[]{:S(2)}) collective-permute-start(bf16[256,384]{1,0:T(8,128)(2,1)S(1)} %get-tuple-element.27.refs_5_), channel_id=1, source_target_pairs={{0,2},{1,3},{2,4},{3,5},{4,6},{5,7},{6,0},{7,1},{8,10},{9,11},{10,... | collective-permute-start | bytes 589832 | tf_op jit(solution)/shard_map/ppermute | solution.py:38
  103.9 17.8 %collective-permute-start.11 = (bf16[256,384]{1,0:T(8,128)(2,1)S(1)}, bf16[256,384]{1,0:T(8,128)(2,1)}, u32[]{:S(2)}, u32[]{:S(2)}) collective-permute-start(bf16[256,384]{1,0:T(8,128)(2,1)S(1)} %get-tuple-element.33.refs_9_.refs_5_), channel_id=1, source_target_pairs={{0,4},{1,5},{2,6},{3,7},{4,0},{5,1},{6,2},{7,3},{8,12},{9,13},{10,... | collective-permute-start | bytes 589832 | tf_op jit(solution)/shard_map/ppermute | solution.py:38
  107.6 14.5 %collective-permute-start.12 = (bf16[256,384]{1,0:T(8,128)(2,1)S(1)}, bf16[256,384]{1,0:T(8,128)(2,1)}, u32[]{:S(2)}, u32[]{:S(2)}) collective-permute-start(bf16[256,384]{1,0:T(8,128)(2,1)S(1)} %get-tuple-element.33.refs_9_.refs_5_), channel_id=1, source_target_pairs={{0,2},{1,3},{2,4},{3,5},{4,6},{5,7},{6,0},{7,1},{8,10},{9,11},{10,... | collective-permute-start | bytes 589832 | tf_op jit(solution)/shard_map/ppermute | solution.py:38
  109.3 0.7 copy-start.8
  109.9 12.1 %collective-permute-start.13 = (bf16[256,384]{1,0:T(8,128)(2,1)S(1)}, bf16[256,384]{1,0:T(8,128)(2,1)}, u32[]{:S(2)}, u32[]{:S(2)}) collective-permute-start(bf16[256,384]{1,0:T(8,128)(2,1)S(1)} %get-tuple-element.33.refs_9_.refs_5_), channel_id=1, source_target_pairs={{0,6},{1,7},{2,0},{3,1},{4,2},{5,3},{6,4},{7,5},{8,14},{9,15},{10,... | collective-permute-start | bytes 589832 | tf_op jit(solution)/shard_map/ppermute | solution.py:38
  112.5 4.2 %copy-start.9 = (bf16[256,384]{1,0:T(8,128)(2,1)S(1)}, bf16[256,384]{1,0:T(8,128)(2,1)}, u32[]{:S(2)}) copy-start(bf16[256,384]{1,0:T(8,128)(2,1)} %copy-done.8) | copy-start | bytes 589828
  115.7 6.3 %copy-start = (bf16[2,384,1024]{2,1,0:T(8,128)(2,1)}, bf16[2,384,1024]{2,1,0:T(8,128)(2,1)S(1)}, u32[]{:S(2)}) copy-start(bf16[2,384,1024]{2,1,0:T(8,128)(2,1)S(1)} %get-tuple-element.30.refs_2_) | copy-start | bytes 4718596
  115.7 6.3 %copy-start.2 = (bf16[2,384,1024]{2,1,0:T(8,128)(2,1)}, bf16[2,384,1024]{2,1,0:T(8,128)(2,1)S(1)}, u32[]{:S(2)}) copy-start(bf16[2,384,1024]{2,1,0:T(8,128)(2,1)S(1)} %get-tuple-element.31.refs_3_) | copy-start | bytes 4718596
  115.7 6.3 %copy-start.4 = (f32[2,1024,128]{2,1,0:T(8,128)}, f32[2,1024,128]{2,1,0:T(8,128)S(1)}, u32[]{:S(2)}) copy-start(f32[2,1024,128]{2,1,0:T(8,128)S(1)} %get-tuple-element.32.refs_4_) | copy-start | bytes 3145732
  120.1 16.7 %collective-permute-start.15 = (bf16[1024,256]{1,0:T(8,128)(2,1)}, bf16[1024,256]{1,0:T(8,128)(2,1)}, u32[]{:S(2)}, u32[]{:S(2)}) collective-permute-start(bf16[1024,256]{1,0:T(8,128)(2,1)} %grad.5), channel_id=1, source_target_pairs={{0,1},{1,0},{2,3},{3,2},{4,5},{5,4},{6,7},{7,6},{8,9},{9,8},{10,11... | collective-permute-start | bytes 1572872 | tf_op jit(solution)/shard_map/ppermute | solution.py:562
  125.1 20.1 %collective-permute-start.14 = (bf16[1024,256]{1,0:T(8,128)(2,1)}, bf16[1024,256]{1,0:T(8,128)(2,1)}, u32[]{:S(2)}, u32[]{:S(2)}) collective-permute-start(bf16[1024,256]{1,0:T(8,128)(2,1)} %grad.4), channel_id=1, source_target_pairs={{0,1},{1,0},{2,3},{3,2},{4,5},{5,4},{6,7},{7,6},{8,9},{9,8},{10,11... | collective-permute-start | bytes 1572872 | tf_op jit(solution)/shard_map/ppermute | solution.py:562
  126.7 11.9 %collective-permute-start.4 = (bf16[16,32,1024]{2,1,0:T(8,128)(2,1)}, bf16[16,32,1024]{2,1,0:T(8,128)(2,1)S(1)}, u32[]{:S(2)}, u32[]{:S(2)}) collective-permute-start(bf16[16,32,1024]{2,1,0:T(8,128)(2,1)} %all-to-all-done.1.mine_ref), channel_id=1, source_target_pairs={{0,8},{8,0},{16,24},{24,16},{32,40},{40,32},{48,56},{56,48},{64,72... | collective-permute-start | bytes 3145736 | tf_op jit(solution)/shard_map/ppermute | solution.py:553
  126.7 1.4 copy-start.1
  128.1 1.4 copy-start.3
  129.5 1.2 copy-start.5
  130.8 0.9 copy-start.10
  138.7 1.0 copy-start.20

commit v3 on v2

--- a/solution.py
+++ b/solution.py
@@ -173,7 +173,7 @@
     chips, rows, cols = mine.shape
     return pl.pallas_call(
         merge_kernel,
-        in_specs=[SMEM, HBM, HBM],
+        in_specs=[SMEM, ANY, ANY],
         out_specs=HBM,
         out_shape=jax.ShapeDtypeStruct((chips, N_CORE, rows, cols), mine.dtype),
         scratch_shapes=[
@@ -183,7 +183,7 @@
         ],
         compiler_params=PARAMS,
         name="merge",
-    )(core.reshape(1), in_hbm(mine), in_hbm(theirs))
+    )(core.reshape(1), mine, theirs)
 
 
 def cut_kernel(count, kept, at_ref, source_ref, *refs):
@@ -229,14 +229,18 @@
     )(jnp.stack(places), in_hbm(tokens), *(in_hbm(one) for one in after))
 
 
-def behind_kernel(source_ref, *refs):
-    target_ref, buffer, in_sems, out_sems = refs[-4:]
-    rows = source_ref.shape[0] // 4
+def behind_kernel(count, *refs):
+    sources, refs = refs[:count], refs[-2 * count - 2 :]
+    targets, buffers, (in_sems, out_sems) = refs[:count], refs[count : 2 * count], refs[2 * count :]
     reads, writes = [], []
-    for part in range(4):
-        at = pl.ds(part * rows, rows)
-        reads.append(pltpu.make_async_copy(source_ref.at[at], buffer.at[at], in_sems.at[part]))
-        writes.append(pltpu.make_async_copy(buffer.at[at], target_ref.at[at], out_sems.at[part]))
+    for which in range(count):
+        rows = sources[which].shape[0] // PIECES
+        for piece in range(PIECES):
+            at = pl.ds(piece * rows, rows)
+            held = buffers[which].at[at]
+            slot = which * PIECES + piece
+            reads.append(pltpu.make_async_copy(sources[which].at[at], held, in_sems.at[slot]))
+            writes.append(pltpu.make_async_copy(held, targets[which].at[at], out_sems.at[slot]))
     for read in reads:
         read.start()
     for read, write in zip(reads, writes):
@@ -246,21 +250,19 @@
         write.wait()
 
 
-def behind(source, *after):
-    return pl.pallas_call(
-        behind_kernel,
-        in_specs=[ANY] * (1 + len(after)),
-        out_specs=ANY,
-        out_shape=jax.ShapeDtypeStruct(source.shape, source.dtype),
-        scratch_shapes=[
-            pltpu.VMEM(source.shape, source.dtype),
-            pltpu.SemaphoreType.DMA((4,)),
-            pltpu.SemaphoreType.DMA((4,)),
-        ],
+def behind(sources, *after):
+    count = len(sources)
+    return pl.pallas_call(
+        functools.partial(behind_kernel, count),
+        in_specs=[HBM] * count + [ANY] * len(after),
+        out_specs=[HBM] * count,
+        out_shape=[jax.ShapeDtypeStruct(one.shape, one.dtype) for one in sources],
+        scratch_shapes=[pltpu.VMEM(one.shape, one.dtype) for one in sources]
+        + [pltpu.SemaphoreType.DMA((count * PIECES,))] * 2,
         compiler_params=PARAMS,
         cost_estimate=COST,
         name="behind",
-    )(in_hbm(source), *(in_hbm(one) for one in after))
+    )(*(in_hbm(one) for one in sources), *(in_hbm(one) for one in after))
 
 
 def pair_kernel(x_ref, weight_ref, other_ref, gain_ref, pair_ref):
@@ -322,40 +324,49 @@
 SPLIT = 4
 
 
-def part_kernel(block_ref, weight_ref, *refs):
-    part_ref, kept_ref, sems = refs[-3:]
-    rows = kept_ref.shape[1] // SPLIT
+def part_kernel(count, *refs):
+    blocks, weight_ref = refs[:count], refs[count]
+    parts, (held, sems) = refs[-2 - count : -2], refs[-2:]
+    rows = held.shape[2] // SPLIT
     reads = []
-    for half in range(N_X):
-        for piece in range(SPLIT):
-            at = pl.ds(piece * rows, rows)
-            reads.append(
-                pltpu.make_async_copy(
-                    block_ref.at[half, at], kept_ref.at[half, at], sems.at[half * SPLIT + piece]
+    for which in range(count):
+        for half in range(N_X):
+            for piece in range(SPLIT):
+                at = pl.ds(piece * rows, rows)
+                reads.append(
+                    pltpu.make_async_copy(
+                        blocks[which].at[half, at], held.at[which, half, at], sems.at[len(reads)]
+                    )
                 )
-            )
     for read in reads:
         read.start()
-    total = None
-    for half in range(N_X):
-        for read in reads[half * SPLIT : (half + 1) * SPLIT]:
-            read.wait()
-        term = jnp.dot(kept_ref[half], weight_ref[half], preferred_element_type=jnp.float32)
-        total = term if total is None else total + term
-    part_ref[...] = total.astype(jnp.bfloat16)
-
-
-def key_part(block, weight, *after):
-    return pl.pallas_call(
-        part_kernel,
-        in_specs=[HBM, VMEM] + [ANY] * len(after),
-        out_specs=VMEM,
-        out_shape=jax.ShapeDtypeStruct((block.shape[1], weight.shape[2]), jnp.bfloat16),
-        scratch_shapes=[pltpu.VMEM(block.shape, block.dtype), pltpu.SemaphoreType.DMA((N_X * SPLIT,))],
+    for which in range(count):
+        total = None
+        for half in range(N_X):
+            slot = (which * N_X + half) * SPLIT
+            for read in reads[slot : slot + SPLIT]:
+                read.wait()
+            term = jnp.dot(held[which, half], weight_ref[half], preferred_element_type=jnp.float32)
+            total = term if total is None else total + term
+        parts[which][...] = total.astype(jnp.bfloat16)
+
+
+def key_parts(blocks, weight, *after):
+    count = len(blocks)
+    rows = blocks[0].shape[1]
+    return pl.pallas_call(
+        functools.partial(part_kernel, count),
+        in_specs=[HBM] * count + [VMEM] + [ANY] * len(after),
+        out_specs=[VMEM] * count,
+        out_shape=[jax.ShapeDtypeStruct((rows, weight.shape[2]), jnp.bfloat16)] * count,
+        scratch_shapes=[
+            pltpu.VMEM((count,) + blocks[0].shape, jnp.bfloat16),
+            pltpu.SemaphoreType.DMA((count * N_X * SPLIT,)),
+        ],
         compiler_params=PARAMS,
         cost_estimate=COST,
         name="part",
-    )(in_hbm(block), weight, *after)
+    )(*(in_hbm(one) for one in blocks), weight, *after)
 
 
 HALVES = 2
@@ -421,7 +432,7 @@
     rows, width = theirs.shape
     return pl.pallas_call(
         functools.partial(add_kernel, half),
-        in_specs=[VMEM, HBM] + [HBM] * (before is not None) + [ANY] * len(after),
+        in_specs=[VMEM, ANY] + [HBM] * (before is not None) + [ANY] * len(after),
         out_specs=HBM,
         out_shape=jax.ShapeDtypeStruct(own.shape, jnp.bfloat16),
         input_output_aliases={} if before is None else {2: 0},
@@ -433,69 +444,92 @@
         ],
         compiler_params=PARAMS,
         name="add",
-    )(own, in_hbm(theirs), *(() if before is None else (before,)), *(in_hbm(one) for one in after))
+    )(own, theirs, *(() if before is None else (before,)), *(in_hbm(one) for one in after))
 
 
 TILES = 2
 
 
-def load_kernel(count, *refs):
-    sources, gain_ref, targets, gain, sems = refs[:count], refs[count], refs[-2 - count : -2], refs[-2], refs[-1]
-    reads = [pltpu.make_async_copy(gain_ref, gain, sems.at[2 * count])]
+def load_kernel(count, half_ref, *refs):
+    sources, gain_ref, (held, gain, sems) = refs[:count], refs[count], refs[-3:]
+    half = half_ref[0]
+    tokens = sources[0].shape[1]
+    reads = [pltpu.make_async_copy(gain_ref.at[half], gain, sems.at[count])]
     for which in range(count):
-        for half in range(N_X):
-            reads.append(
-                pltpu.make_async_copy(
-                    sources[which].at[half], targets[which].at[half], sems.at[which * N_X + half]
-                )
-            )
+        at = pl.ds(which * tokens, tokens)
+        reads.append(pltpu.make_async_copy(sources[which].at[half], held.at[at], sems.at[which]))
     for read in reads:
         read.start()
     for read in reads:
         read.wait()
 
 
-def load_blocks(blocks, gain, *after):
+def load_half(blocks, gain, half, *after):
     count = len(blocks)
-    kept = [pltpu.VMEM(one.shape, one.dtype) for one in (*blocks, gain)]
-    *loaded, gain = pl.pallas_call(
+    _, tokens, rows = blocks[0].shape
+    return pl.pallas_call(
         functools.partial(load_kernel, count),
-        in_specs=[HBM] * (count + 1) + [ANY] * len(after),
-        out_specs=[VMEM] * (count + 1),
-        out_shape=kept,
-        scratch_shapes=[pltpu.SemaphoreType.DMA((2 * count + 1,))],
+        in_specs=[SMEM] + [HBM] * (count + 1) + [ANY] * len(after),
+        out_specs=[VMEM] * 2,
+        out_shape=[pltpu.VMEM((count * tokens, rows), jnp.bfloat16), pltpu.VMEM(gain.shape[1:], gain.dtype)],
+        scratch_shapes=[pltpu.SemaphoreType.DMA((count + 1,))],
         compiler_params=PARAMS,
         name="load",
-    )(*(in_hbm(one) for one in (*blocks, gain)), *after)
-    return loaded, gain
-
-
-def grad_kernel(count, half_ref, *refs):
-    blocks, gain_ref, cots, out_ref = refs[:count], refs[count], refs[count + 1 : -1], refs[-1]
-    half = half_ref[0]
+    )(half.reshape(1), *(in_hbm(one) for one in (*blocks, gain)), *after)
+
+
+def grad_tiles(block_ref, gain_ref, cots, out_ref, group):
     width = cots[0].shape[0]
     tile = out_ref.shape[0] // TILES
+    cot = jnp.concatenate([ref[...] for ref in cots], axis=1)
     for part in range(TILES):
         at = pl.ds(part * tile, tile)
-        block = jnp.concatenate([ref[half, :, at] for ref in blocks], axis=0)
-        factor = jnp.concatenate([gain_ref[half, at, :]] * (width // BLOCK), axis=1)
-        for group in range(len(cots) // count):
-            cot = jnp.concatenate([ref[...] for ref in cots[group * count : (group + 1) * count]], axis=1)
-            total = jnp.dot(cot, block, preferred_element_type=jnp.float32).T * factor
-            out_ref[at, pl.ds(group * width, width)] = total.astype(out_ref.dtype)
-
-
-def grad_rows(blocks, half, cots, gain, out, cost):
+        factor = jnp.concatenate([gain_ref[at, :]] * (width // BLOCK), axis=1)
+        total = jnp.dot(cot, block_ref[:, at], preferred_element_type=jnp.float32).T * factor
+        out_ref[at, pl.ds(group * width, width)] = total.astype(out_ref.dtype)
+
+
+def grad_kernel(block_ref, gain_ref, *refs):
+    grad_tiles(block_ref, gain_ref, refs[:-1], refs[-1], 0)
+
+
+def sent_grad(block, gain, cots):
+    return pl.pallas_call(
+        grad_kernel,
+        in_specs=[VMEM] * (2 + len(cots)),
+        out_specs=VMEM,
+        out_shape=jax.ShapeDtypeStruct((block.shape[1], cots[0].shape[0]), jnp.bfloat16),
+        compiler_params=PARAMS,
+        name="grad",
+    )(block, gain, *cots)
+
+
+def kept_kernel(count, half_ref, *refs):
+    sources, gain_ref, refs = refs[:count], refs[count], refs[count + 1 :]
+    cots, (out_ref, held, gain, sems) = refs[: HALVES * count], refs[-4:]
+    load_kernel(count, half_ref, *sources, gain_ref, held, gain, sems)
+    for group in range(HALVES):
+        grad_tiles(held, gain, cots[group * count : (group + 1) * count], out_ref, group)
+
+
+def kept_grad(blocks, gain, half, cots, *after):
     count = len(blocks)
-    return pl.pallas_call(
-        functools.partial(grad_kernel, count),
-        in_specs=[SMEM] + [VMEM] * (count + 1 + len(cots)),
+    _, tokens, rows = blocks[0].shape
+    width = cots[0][0].shape[0]
+    return pl.pallas_call(
+        functools.partial(kept_kernel, count),
+        in_specs=[SMEM] + [HBM] * (count + 1) + [VMEM] * (HALVES * count) + [ANY] * len(after),
         out_specs=VMEM,
-        out_shape=out,
-        compiler_params=PARAMS,
-        cost_estimate=cost,
-        name="grad",
-    )(half.reshape(1), *blocks, gain, *cots)
+        out_shape=pltpu.VMEM((rows, HALVES * width), jnp.float32),
+        scratch_shapes=[
+            pltpu.VMEM((count * tokens, rows), jnp.bfloat16),
+            pltpu.VMEM(gain.shape[1:], gain.dtype),
+            pltpu.SemaphoreType.DMA((count + 1,)),
+        ],
+        compiler_params=PARAMS,
+        cost_estimate=SHORT,
+        name="kept",
+    )(half.reshape(1), *(in_hbm(one) for one in (*blocks, gain)), *(one for part in cots for one in part), *after)
 
 
 def per_device(
@@ -514,7 +548,7 @@
     (sent[2],) = cut_columns(tokens, [places[2]], quarter, 0)
     held = {2: send_y(sent[2], 2)}
 
-    fragment = behind(replica_frag[0], sent[2])
+    fragment, weight = behind([replica_frag[0], key_weight[0]], sent[2])
     frags = lax.all_to_all(fragment, "rep", 0, 0, tiled=True)
     frags = frags.reshape(lax.axis_size("rep"), -1, fragment.shape[1])
 
@@ -522,7 +556,6 @@
         tokens, [places[1], places[3], y], quarter, 0, fragment
     )
     held[1], held[3] = send_y(sent[1], 1), send_y(sent[3], 3)
-    weight = key_weight[0]
     other = lax.ppermute(weight, "fsdp", X_SWAP)
 
     gain = lax.dynamic_slice(norm_gain, (y * quarter,), (quarter,))
@@ -530,10 +563,9 @@
     pair = scaled_pair(x, weight, other, wide_gain)
     base, factor = own_part(tokens, own, pair, key_target[0], token_count)
     parts = {}
-    parts[2] = key_part(held[2], pair, base)
+    (parts[2],) = key_parts([held[2]], pair, base)
     new_params, new_moment, fresh = outer_step(frags, outer_params, outer_moment, parts[2])
-    parts[1] = key_part(held[1], pair, fresh)
-    parts[3] = key_part(held[3], pair, parts[1])
+    parts[1], parts[3] = key_parts([held[1], held[3]], pair, fresh)
     chips = lax.axis_size("rep") // N_CORE
     many = spread(fresh, chips, parts[3])
     others = [send_y(parts[step], N_Y - step) for step in (2, 1, 3)]
@@ -553,15 +585,13 @@
     theirs = lax.ppermute(mine, "rep", [(i, i ^ 1) for i in range(chips * N_CORE)])
     fresh_frag = merge_cores(lax.axis_index("rep") % N_CORE, mine, theirs).reshape(-1, cols)
 
-    blocks, wide_gain = load_blocks([own, held[2], held[1], held[3]], wide_gain, cot[0])
-    width = cot[0].shape[0]
-    theirs = []
+    blocks = [own, held[2], held[1], held[3]]
+    theirs, last = [], None
+    loaded = load_half(blocks, wide_gain, 1 - x, cot[0])
     for half in range(HALVES):
-        out = jax.ShapeDtypeStruct((rows, width), jnp.bfloat16)
-        part = grad_rows(blocks, 1 - x, cots[half], wide_gain, out, None)
-        theirs.append(lax.ppermute(part, "fsdp", X_SWAP))
-    out = pltpu.VMEM((rows, HALVES * width), jnp.float32)
-    mine_grad = grad_rows(blocks, x, cots[0] + cots[1], wide_gain, out, SHORT)
+        last = sent_grad(*loaded, cots[half])
+        theirs.append(lax.ppermute(last, "fsdp", X_SWAP))
+    mine_grad = kept_grad(blocks, wide_gain, x, cots, last)
     weight_grad = add_half(0, mine_grad, theirs[0], None)
     weight_grad = add_half(1, mine_grad, theirs[1], weight_grad, fresh_frag)
     return (new_params, new_moment, fresh_frag, weight_grad[None])

time: 149 us -> 143 us (0.960)
  waiting for transfers between devices: 38.9 us -> 49.8 us
  Pallas kernels: 55.6 us -> 49.3 us
  local copies, waits for them, and re-layouts: 7.73 us -> 2.67 us
  starting transfers between devices: 43.7 us -> 39.1 us
    ppermute x1, waiting for transfers between devices: 3.66 us -> 17.9 us  [per_device(): other = lax.ppermute(weight, 'fsdp', X_SWAP)]
    all_to_all x1, waiting for transfers between devices: 20.2 us -> 13.1 us  [per_device(): frags = lax.all_to_all(fragment, 'rep', 0, 0, tiled=True)]
    pallas_call x11 -> x10, Pallas kernels: 31.2 us -> 24.6 us  [the longest x2 8.09 us: key_parts(): pl.pallas_call(functools.partial(part_kernel, count), in_specs=[HBM] * co...]
    unnamed x42 -> x20, local copies, waits for them, and re-layouts: 6.69 us -> 1.63 us
    ppermute x12, starting transfers between devices: 20.9 us -> 16.9 us  [send_y(): return lax.ppermute(block, 'fsdp', y_shift(step))]
    ppermute x2, waiting for transfers between devices: 4.99 us -> 8.32 us  [per_device(): theirs.append(lax.ppermute(last, 'fsdp', X_SWAP))]
    all_to_all x1, starting transfers between devices: 7.74 us -> 6.1 us  [per_device(): lax.all_to_all(many.reshape(chips * own_rows, cols), 'rep', 0, 0, axis_in...]
  transfers between devices with their start and end apart: 18 -> 18, of which waited for: 9 -> 9; matrix products, arithmetic and copies ran while one was open for 1% -> 1% of each run, Pallas kernels for 37% -> 32%
where the time goes in v3:
time: 143 us; the launch traced here: 142 us
  waiting for transfers between devices  49.8 us (35%)
  Pallas kernels  49.3 us (34%)
  starting transfers between devices  39.1 us (27%)
  local copies, waits for them, and re-layouts  2.67 us (2%)
    ppermute x1, waiting for transfers between devices, per_device(): other = lax.ppermute(weight, 'fsdp', X_SWAP)  17.9 us
    ppermute x12, starting transfers between devices, send_y(): return lax.ppermute(block, 'fsdp', y_shift(step))  16.9 us
    all_to_all x1, waiting for transfers between devices, per_device(): frags = lax.all_to_all(fragment, 'rep', 0, 0, tiled=True)  13.1 us
    ppermute x12, waiting for transfers between devices, send_y(): return lax.ppermute(block, 'fsdp', y_shift(step))  10.5 us
    all_to_all x1, starting transfers between devices, per_device(): frags = lax.all_to_all(fragment, 'rep', 0, 0, tiled=True)  8.81 us
    ppermute x2, waiting for transfers between devices, per_device(): theirs.append(lax.ppermute(last, 'fsdp', X_SWAP))  8.32 us
    pallas_call x2, Pallas kernels, key_parts(): pl.pallas_call(functools.partial(part_kernel, count), in_specs=[HBM] * co...  8.09 us
    pallas_call x1, Pallas kernels, outer_step(): pl.pallas_call(functools.partial(outer_kernel, replicas), grid=(replicas...  7.67 us
  transfers between devices with their start and end apart: 18, of which 9 were waited for; matrix products, arithmetic and copies ran while one was open for 1% of the time, Pallas kernels for 32%

profile of v3, /device:TPU:32, one launch (start us, length us, event | category | flops | bytes accessed | tf_op | source)
XLA Modules:
  0.0 142.1 jit_solution(5692728767624635043)
XLA Ops:
  0.7 2.3 %cut.2.refs_2_ = bf16[2,384,1024]{2,1,0:T(8,128)(2,1)} custom-call(s32[1]{0:T(128)} %bitcast.2.at_ref, bf16[384,8192]{1,0:T(8,128)(2,1)} %bitcast.17), custom_call_target="tpu_custom_call" | custom-call | flops 999999995904 | bytes 1000000000 | tf_op jit(solution)/shard_map/cut/pallas_call | solution.py:216
  3.0 3.3 %collective-permute-start = (bf16[2,384,1024]{2,1,0:T(8,128)(2,1)}, bf16[2,384,1024]{2,1,0:T(8,128)(2,1)}, u32[]{:S(2)}, u32[]{:S(2)}) collective-permute-start(bf16[2,384,1024]{2,1,0:T(8,128)(2,1)} %cut.2.refs_2_), channel_id=1, source_target_pairs={{0,4},{1,5},{2,6},{3,7},{4,0},{5,1},{6,2},{7,3},{8,12},{9,13},{10,... | collective-permute-start | bytes 4718600 | tf_op jit(solution)/shard_map/ppermute | solution.py:38
  6.3 2.8 %behind.1 = (bf16[1024,1024]{1,0:T(8,128)(2,1)}, bf16[1024,512]{1,0:T(8,128)(2,1)}) custom-call(bf16[1024,1024]{1,0:T(8,128)(2,1)} %bitcast.20, bf16[1024,512]{1,0:T(8,128)(2,1)} %bitcast.21, bf16[2,384,1024]{2,1,0:T(8,128)(2,1)} %cut.2.refs_2_), custom_call_target="tpu_custom_call" | custom-call | flops 999999995904 | bytes 1000000000 | tf_op jit(solution)/shard_map/behind/pallas_call | solution.py:255
  9.1 3.1 %collective-permute-start.1 = (bf16[1024,512]{1,0:T(8,128)(2,1)}, bf16[1024,512]{1,0:T(8,128)(2,1)}, u32[]{:S(2)}, u32[]{:S(2)}) collective-permute-start(bf16[1024,512]{1,0:T(8,128)(2,1)} %get-tuple-element.21.weight_ref), channel_id=1, source_target_pairs={{0,1},{1,0},{2,3},{3,2},{4,5},{5,4},{6,7},{7,6},{8,9},{9,8},{10,11... | collective-permute-start | bytes 3145736 | tf_op jit(solution)/shard_map/ppermute | solution.py:559
  12.2 8.8 %all-to-all-start = ((bf16[32,32,1024]{2,1,0:T(8,128)(2,1)}), bf16[32,32,1024]{2,1,0:T(8,128)(2,1)}, u32[]{:S(2)}, u32[]{:S(2)}) async-start(bf16[32,32,1024]{2,1,0:T(8,128)(2,1)} %bitcast.4), calls=%async_computation | async-start | bytes 4194304 | tf_op jit(solution)/shard_map/all_to_all | solution.py:552
  21.0 0.1 pad_add_fusion.at_ref
  21.1 3.8 %cut.3 = (bf16[2,384,1024]{2,1,0:T(8,128)(2,1)}, bf16[2,384,1024]{2,1,0:T(8,128)(2,1)}, bf16[2,384,1024]{2,1,0:T(8,128)(2,1)S(1)}) custom-call(s32[3]{0:T(128)S(1)} %pad_add_fusion.at_ref, bf16[384,8192]{1,0:T(8,128)(2,1)} %bitcast.18, bf16[1024,1024]{1,0:T(8,128)(2,1)} %get-tuple-element.20.refs_0_), custom_call_target="tpu_custom_call" | custom-call | flops 999999995904 | bytes 1000000000 | tf_op jit(solution)/shard_map/cut/pallas_call | solution.py:216
  24.9 0.8 collective-permute-start.2
  25.7 2.6 %collective-permute-start.3 = (bf16[2,384,1024]{2,1,0:T(8,128)(2,1)}, bf16[2,384,1024]{2,1,0:T(8,128)(2,1)}, u32[]{:S(2)}, u32[]{:S(2)}) collective-permute-start(bf16[2,384,1024]{2,1,0:T(8,128)(2,1)} %get-tuple-element.28), channel_id=1, source_target_pairs={{0,6},{1,7},{2,0},{3,1},{4,2},{5,3},{6,4},{7,5},{8,14},{9,15},{10,... | collective-permute-start | bytes 4718600 | tf_op jit(solution)/shard_map/ppermute | solution.py:38
  28.2 0.7 dynamic_slice.3
  28.9 17.9 %collective-permute-done.1.other_ref = bf16[1024,512]{1,0:T(8,128)(2,1)} collective-permute-done((bf16[1024,512]{1,0:T(8,128)(2,1)}, bf16[1024,512]{1,0:T(8,128)(2,1)}, u32[]{:S(2)}, u32[]{:S(2)}) %collective-permute-start.1) | collective-permute-done | bytes 1048608 | tf_op jit(solution)/shard_map/ppermute | solution.py:559
  46.9 0.3 broadcast_in_dim.11.gain_ref.refs_4_
  47.2 2.3 %pair.1.weight_ref.refs_1_.refs_2_ = bf16[2,1024,512]{2,1,0:T(8,128)(2,1)S(1)} custom-call(s32[1]{0:T(128)} %bitcast.5.x_ref.half_ref, bf16[1024,512]{1,0:T(8,128)(2,1)} %get-tuple-element.21.weight_ref, bf16[1024,512]{1,0:T(8,128)(2,1)} %collective-permute-done.1.other_ref, f32[2,1024,128]{2,1,0:T(8,128)S(1)} %broadcast_in_dim.11.gain_ref.refs_4_), custom_call_target="tpu_custom_call" | custom-call | flops 999999995904 | bytes 1000000000 | tf_op jit(solution)/shard_map/pair/pallas_call | solution.py:278
  49.6 5.7 %own.1 = (f32[384,512]{1,0:T(8,128)S(1)}, f32[384,128]{1,0:T(8,128)S(1)}) custom-call(bf16[384,8192]{1,0:T(8,128)(2,1)} %bitcast.19, bf16[2,384,1024]{2,1,0:T(8,128)(2,1)S(1)} %get-tuple-element.22.block_ref.refs_0_, bf16[2,1024,512]{2,1,0:T(8,128)(2,1)S(1)} %pair.1.weight_ref.refs_1_.refs_2_, bf16[384,512]{1,0:T(8,128)(2,1)} %bitcast.22), custom_call_target="tpu_custom_call" | custom-call | flops 999999995904 | bytes 1000000000 | tf_op jit(solution)/shard_map/own/pallas_call | solution.py:307
  55.4 0.0 copy-start.4
  55.4 3.6 %part.2.refs_0_ = bf16[384,512]{1,0:T(8,128)(2,1)} custom-call(bf16[2,384,1024]{2,1,0:T(8,128)(2,1)} %collective-permute-done.refs_0_.refs_1_, bf16[2,1024,512]{2,1,0:T(8,128)(2,1)S(1)} %pair.1.weight_ref.refs_1_.refs_2_, f32[384,512]{1,0:T(8,128)S(1)} %get-tuple-element.23.refs_2_.refs_0_), custom_call_target="tpu_custom_call" | custom-call | flops 999999995904 | bytes 1000000000 | tf_op jit(solution)/shard_map/part/pallas_call | solution.py:357
  59.0 0.4 collective-permute-start.5
  59.4 13.1 %all-to-all-done.frag_ref = bf16[32,32,1024]{2,1,0:T(8,128)(2,1)} async-done(((bf16[32,32,1024]{2,1,0:T(8,128)(2,1)}), bf16[32,32,1024]{2,1,0:T(8,128)(2,1)}, u32[]{:S(2)}, u32[]{:S(2)}) %all-to-all-start) | async-done | bytes 2097184 | tf_op jit(solution)/shard_map/all_to_all | solution.py:552
  72.5 7.7 %outer.1 = (f32[32,1024]{1,0:T(8,128)}, f32[32,1024]{1,0:T(8,128)}, bf16[32,1024]{1,0:T(8,128)(2,1)S(1)}) custom-call(bf16[32,32,1024]{2,1,0:T(8,128)(2,1)} %all-to-all-done.frag_ref, f32[32,1024]{1,0:T(8,128)S(1)} %copy-done.4, f32[32,1024]{1,0:T(8,128)S(1)} %copy-done.5, bf16[384,512]{1,0:T(8,128)(2,1)} %part.2.refs_0_), custom_call_target="tpu_custom_call" | custom-call | flops 999999995904 | bytes 1000000000 | tf_op jit(solution)/shard_map/outer/pallas_call | solution.py:112
  80.2 4.5 %part.3 = (bf16[384,512]{1,0:T(8,128)(2,1)}, bf16[384,512]{1,0:T(8,128)(2,1)}) custom-call(bf16[2,384,1024]{2,1,0:T(8,128)(2,1)} %collective-permute-done.2.refs_0_.refs_2_, bf16[2,384,1024]{2,1,0:T(8,128)(2,1)} %collective-permute-done.3.refs_1_.refs_3_, bf16[2,1024,512]{2,1,0:T(8,128)(2,1)S(1)} %copy-done.7, ...), custom_call_target="tpu_custom_call" | custom-call | flops 999999995904 | bytes 1000000000 | tf_op jit(solution)/shard_map/part/pallas_call | solution.py:357
  84.7 1.1 collective-permute-start.6
  85.9 1.0 collective-permute-start.7
  86.8 1.0 spread.1.refs_5_
  87.9 6.1 %all-to-all-start.1 = ((bf16[16,32,1024]{2,1,0:T(8,128)(2,1)}), bf16[16,32,1024]{2,1,0:T(8,128)(2,1)}, u32[]{:S(2)}, u32[]{:S(2)}) async-start(bf16[16,32,1024]{2,1,0:T(8,128)(2,1)} %spread.1.refs_5_), calls=%async_computation.1 | async-start | bytes 2097152 | tf_op jit(solution)/shard_map/all_to_all | solution.py:577
  94.0 1.8 %collective-permute-done.6.refs_3_ = bf16[384,512]{1,0:T(8,128)(2,1)} collective-permute-done((bf16[384,512]{1,0:T(8,128)(2,1)}, bf16[384,512]{1,0:T(8,128)(2,1)}, u32[]{:S(2)}, u32[]{:S(2)}) %collective-permute-start.6) | collective-permute-done | bytes 393248 | tf_op jit(solution)/shard_map/ppermute | solution.py:38
  95.8 2.0 %collective-permute-done.7.refs_4_ = bf16[384,512]{1,0:T(8,128)(2,1)} collective-permute-done((bf16[384,512]{1,0:T(8,128)(2,1)}, bf16[384,512]{1,0:T(8,128)(2,1)}, u32[]{:S(2)}, u32[]{:S(2)}) %collective-permute-start.7) | collective-permute-done | bytes 393248 | tf_op jit(solution)/shard_map/ppermute | solution.py:38
  97.8 1.8 %cot.1 = (bf16[256,384]{1,0:T(8,128)(2,1)S(1)}, bf16[256,384]{1,0:T(8,128)(2,1)S(1)}) custom-call(f32[384,512]{1,0:T(8,128)} %copy-done.8, f32[384,128]{1,0:T(8,128)} %copy-done.9, bf16[384,512]{1,0:T(8,128)(2,1)} %collective-permute-done.5.refs_2_, bf16[384,512]{1,0:T(8,128)(2,1)} %collective-permute-done.6.refs_3_, ...), custom_call_target="tpu_custom_call" | custom-call | flops 999999995904 | bytes 1000000000 | tf_op jit(solution)/shard_map/cot/pallas_call | solution.py:398
  99.6 0.4 collective-permute-start.10
  100.0 1.5 %collective-permute-start.8 = (bf16[256,384]{1,0:T(8,128)(2,1)S(1)}, bf16[256,384]{1,0:T(8,128)(2,1)S(1)}, u32[]{:S(2)}, u32[]{:S(2)}) collective-permute-start(bf16[256,384]{1,0:T(8,128)(2,1)S(1)} %get-tuple-element.32.refs_5_.refs_0_), channel_id=1, source_target_pairs={{0,4},{1,5},{2,6},{3,7},{4,0},{5,1},{6,2},{7,3},{8,12},{9,13},{10,... | collective-permute-start | bytes 589832 | tf_op jit(solution)/shard_map/ppermute | solution.py:38
  101.5 0.2 collective-permute-start.9
  101.7 4.1 %collective-permute-start.11 = (bf16[256,384]{1,0:T(8,128)(2,1)S(1)}, bf16[256,384]{1,0:T(8,128)(2,1)S(1)}, u32[]{:S(2)}, u32[]{:S(2)}) collective-permute-start(bf16[256,384]{1,0:T(8,128)(2,1)S(1)} %get-tuple-element.33.refs_0_.refs_9_), channel_id=1, source_target_pairs={{0,4},{1,5},{2,6},{3,7},{4,0},{5,1},{6,2},{7,3},{8,12},{9,13},{10,... | collective-permute-start | bytes 589832 | tf_op jit(solution)/shard_map/ppermute | solution.py:38
  105.9 1.7 %collective-permute-done.10.refs_8_.refs_3_ = bf16[256,384]{1,0:T(8,128)(2,1)S(1)} collective-permute-done((bf16[256,384]{1,0:T(8,128)(2,1)S(1)}, bf16[256,384]{1,0:T(8,128)(2,1)S(1)}, u32[]{:S(2)}, u32[]{:S(2)}) %collective-permute-start.10) | collective-permute-done | bytes 196640 | tf_op jit(solution)/shard_map/ppermute | solution.py:38
  107.5 1.6 %collective-permute-start.13 = (bf16[256,384]{1,0:T(8,128)(2,1)S(1)}, bf16[256,384]{1,0:T(8,128)(2,1)S(1)}, u32[]{:S(2)}, u32[]{:S(2)}) collective-permute-start(bf16[256,384]{1,0:T(8,128)(2,1)S(1)} %get-tuple-element.33.refs_0_.refs_9_), channel_id=1, source_target_pairs={{0,6},{1,7},{2,0},{3,1},{4,2},{5,3},{6,4},{7,5},{8,14},{9,15},{10,... | collective-permute-start | bytes 589832 | tf_op jit(solution)/shard_map/ppermute | solution.py:38
  109.1 2.0 %load.1 = (bf16[1536,1024]{1,0:T(8,128)(2,1)S(1)}, f32[1024,128]{1,0:T(8,128)S(1)}) custom-call(s32[1]{0:T(128)} %bitcast.12.half_ref, bf16[2,384,1024]{2,1,0:T(8,128)(2,1)} %copy-done.1, bf16[2,384,1024]{2,1,0:T(8,128)(2,1)} %collective-permute-done.refs_0_.refs_1_, bf16[2,384,1024]{2,1,0:T(8,128)(2,1)} %collective-permute-done.2.refs_0_.refs_2_, ...), custom_call_target="tpu_custom_call" | custom-call | tf_op jit(solution)/shard_map/load/pallas_call | solution.py:470
  111.2 3.7 %collective-permute-done.9.refs_7_.refs_2_ = bf16[256,384]{1,0:T(8,128)(2,1)S(1)} collective-permute-done((bf16[256,384]{1,0:T(8,128)(2,1)S(1)}, bf16[256,384]{1,0:T(8,128)(2,1)S(1)}, u32[]{:S(2)}, u32[]{:S(2)}) %collective-permute-start.9) | collective-permute-done | bytes 196640 | tf_op jit(solution)/shard_map/ppermute | solution.py:38
  114.8 1.1 grad.3
  116.0 2.1 %collective-permute-start.15 = (bf16[1024,256]{1,0:T(8,128)(2,1)S(1)}, bf16[1024,256]{1,0:T(8,128)(2,1)S(1)}, u32[]{:S(2)}, u32[]{:S(2)}) collective-permute-start(bf16[1024,256]{1,0:T(8,128)(2,1)S(1)} %grad.3), channel_id=1, source_target_pairs={{0,1},{1,0},{2,3},{3,2},{4,5},{5,4},{6,7},{7,6},{8,9},{9,8},{10,11... | collective-permute-start | bytes 1572872 | tf_op jit(solution)/shard_map/ppermute | solution.py:593
  118.1 1.3 collective-permute-done.12.refs_2_.refs_11_
  119.4 1.1 grad.2.refs_13_
  120.5 0.7 copy-done.2
  121.2 2.0 %collective-permute-start.14 = (bf16[1024,256]{1,0:T(8,128)(2,1)S(1)}, bf16[1024,256]{1,0:T(8,128)(2,1)S(1)}, u32[]{:S(2)}, u32[]{:S(2)}) collective-permute-start(bf16[1024,256]{1,0:T(8,128)(2,1)S(1)} %grad.2.refs_13_), channel_id=1, source_target_pairs={{0,1},{1,0},{2,3},{3,2},{4,5},{5,4},{6,7},{7,6},{8,9},{9,8},{10,11... | collective-permute-start | bytes 1572872 | tf_op jit(solution)/shard_map/ppermute | solution.py:593
  123.2 0.9 copy-done.3
  124.1 4.0 %kept.1.own_ref = f32[1024,512]{1,0:T(8,128)S(1)} custom-call(s32[1]{0:T(128)} %bitcast.5.x_ref.half_ref, bf16[2,384,1024]{2,1,0:T(8,128)(2,1)} %copy-done.1, bf16[2,384,1024]{2,1,0:T(8,128)(2,1)} %collective-permute-done.refs_0_.refs_1_, bf16[2,384,1024]{2,1,0:T(8,128)(2,1)} %collective-permute-done.2.refs_0_.refs_2_, ...), custom_call_target="tpu_custom_call" | custom-call | flops 20000000000 | bytes 1000000 | tf_op jit(solution)/shard_map/kept/pallas_call | solution.py:519
  128.1 4.4 %collective-permute-done.15.theirs_ref = bf16[1024,256]{1,0:T(8,128)(2,1)S(1)} collective-permute-done((bf16[1024,256]{1,0:T(8,128)(2,1)S(1)}, bf16[1024,256]{1,0:T(8,128)(2,1)S(1)}, u32[]{:S(2)}, u32[]{:S(2)}) %collective-permute-start.15) | collective-permute-done | bytes 524320 | tf_op jit(solution)/shard_map/ppermute | solution.py:593
  132.6 1.5 %add.32.refs_0_ = bf16[1024,512]{1,0:T(8,128)(2,1)} custom-call(f32[1024,512]{1,0:T(8,128)S(1)} %kept.1.own_ref, bf16[1024,256]{1,0:T(8,128)(2,1)S(1)} %collective-permute-done.15.theirs_ref), custom_call_target="tpu_custom_call" | custom-call | tf_op jit(solution)/shard_map/add/pallas_call | solution.py:433
  134.1 2.4 %merge.1 = bf16[16,2,32,1024]{3,2,1,0:T(8,128)(2,1)} custom-call(s32[1]{0:T(128)} %bitcast.10.core_ref, bf16[16,32,1024]{2,1,0:T(8,128)(2,1)} %all-to-all-done.1.mine_ref, bf16[16,32,1024]{2,1,0:T(8,128)(2,1)S(1)} %collective-permute-done.4.theirs_ref), custom_call_target="tpu_custom_call" | custom-call | tf_op jit(solution)/shard_map/merge/pallas_call | solution.py:174
  136.5 3.9 %collective-permute-done.14.theirs_ref = bf16[1024,256]{1,0:T(8,128)(2,1)S(1)} collective-permute-done((bf16[1024,256]{1,0:T(8,128)(2,1)S(1)}, bf16[1024,256]{1,0:T(8,128)(2,1)S(1)}, u32[]{:S(2)}, u32[]{:S(2)}) %collective-permute-start.14) | collective-permute-done | bytes 524320 | tf_op jit(solution)/shard_map/ppermute | solution.py:593
  140.4 1.5 %add.33 = bf16[1024,512]{1,0:T(8,128)(2,1)} custom-call(f32[1024,512]{1,0:T(8,128)S(1)} %kept.1.own_ref, bf16[1024,256]{1,0:T(8,128)(2,1)S(1)} %collective-permute-done.14.theirs_ref, bf16[1024,512]{1,0:T(8,128)(2,1)} %add.32.refs_0_, bf16[1024,1024]{1,0:T(8,128)(2,1)} %bitcast.14), custom_call_target="tpu_custom_call", output_to_operand_aliasing={{}: (2, {})} | custom-call | tf_op jit(solution)/shard_map/add/pallas_call | solution.py:433
  (29 shorter events, 0.1 us)
Async XLA Ops:
  3.0 52.4 %collective-permute-start = (bf16[2,384,1024]{2,1,0:T(8,128)(2,1)}, bf16[2,384,1024]{2,1,0:T(8,128)(2,1)}, u32[]{:S(2)}, u32[]{:S(2)}) collective-permute-start(bf16[2,384,1024]{2,1,0:T(8,128)(2,1)} %cut.2.refs_2_), channel_id=1, source_target_pairs={{0,4},{1,5},{2,6},{3,7},{4,0},{5,1},{6,2},{7,3},{8,12},{9,13},{10,... | collective-permute-start | bytes 4718600 | tf_op jit(solution)/shard_map/ppermute | solution.py:38
  9.1 37.8 %collective-permute-start.1 = (bf16[1024,512]{1,0:T(8,128)(2,1)}, bf16[1024,512]{1,0:T(8,128)(2,1)}, u32[]{:S(2)}, u32[]{:S(2)}) collective-permute-start(bf16[1024,512]{1,0:T(8,128)(2,1)} %get-tuple-element.21.weight_ref), channel_id=1, source_target_pairs={{0,1},{1,0},{2,3},{3,2},{4,5},{5,4},{6,7},{7,6},{8,9},{9,8},{10,11... | collective-permute-start | bytes 3145736 | tf_op jit(solution)/shard_map/ppermute | solution.py:559
  12.2 60.3 %all-to-all-start = ((bf16[32,32,1024]{2,1,0:T(8,128)(2,1)}), bf16[32,32,1024]{2,1,0:T(8,128)(2,1)}, u32[]{:S(2)}, u32[]{:S(2)}) async-start(bf16[32,32,1024]{2,1,0:T(8,128)(2,1)} %bitcast.4), calls=%async_computation | async-start | bytes 4194304 | tf_op jit(solution)/shard_map/all_to_all | solution.py:552
  24.9 24.7 %copy-start.1 = (bf16[2,384,1024]{2,1,0:T(8,128)(2,1)}, bf16[2,384,1024]{2,1,0:T(8,128)(2,1)S(1)}, u32[]{:S(2)}) copy-start(bf16[2,384,1024]{2,1,0:T(8,128)(2,1)S(1)} %get-tuple-element.22.block_ref.refs_0_) | copy-start | bytes 4718596
  24.9 55.3 %collective-permute-start.2 = (bf16[2,384,1024]{2,1,0:T(8,128)(2,1)}, bf16[2,384,1024]{2,1,0:T(8,128)(2,1)}, u32[]{:S(2)}, u32[]{:S(2)}) collective-permute-start(bf16[2,384,1024]{2,1,0:T(8,128)(2,1)} %get-tuple-element.27), channel_id=1, source_target_pairs={{0,2},{1,3},{2,4},{3,5},{4,6},{5,7},{6,0},{7,1},{8,10},{9,11},{10,... | collective-permute-start | bytes 4718600 | tf_op jit(solution)/shard_map/ppermute | solution.py:38
  25.7 54.6 %collective-permute-start.3 = (bf16[2,384,1024]{2,1,0:T(8,128)(2,1)}, bf16[2,384,1024]{2,1,0:T(8,128)(2,1)}, u32[]{:S(2)}, u32[]{:S(2)}) collective-permute-start(bf16[2,384,1024]{2,1,0:T(8,128)(2,1)} %get-tuple-element.28), channel_id=1, source_target_pairs={{0,6},{1,7},{2,0},{3,1},{4,2},{5,3},{6,4},{7,5},{8,14},{9,15},{10,... | collective-permute-start | bytes 4718600 | tf_op jit(solution)/shard_map/ppermute | solution.py:38
  47.2 2.3 %copy-start = (f32[2,1024,128]{2,1,0:T(8,128)}, f32[2,1024,128]{2,1,0:T(8,128)S(1)}, u32[]{:S(2)}) copy-start(f32[2,1024,128]{2,1,0:T(8,128)S(1)} %broadcast_in_dim.11.gain_ref.refs_4_) | copy-start | bytes 3145732
  49.5 5.8 %copy-start.6 = (bf16[2,1024,512]{2,1,0:T(8,128)(2,1)}, bf16[2,1024,512]{2,1,0:T(8,128)(2,1)S(1)}, u32[]{:S(2)}) copy-start(bf16[2,1024,512]{2,1,0:T(8,128)(2,1)S(1)} %pair.1.weight_ref.refs_1_.refs_2_) | copy-start | bytes 6291460
  55.3 3.7 %copy-start.8 = (f32[384,512]{1,0:T(8,128)}, f32[384,512]{1,0:T(8,128)S(1)}, u32[]{:S(2)}) copy-start(f32[384,512]{1,0:T(8,128)S(1)} %get-tuple-element.23.refs_2_.refs_0_) | copy-start | bytes 2359300
  55.3 3.7 %copy-start.9 = (f32[384,128]{1,0:T(8,128)}, f32[384,128]{1,0:T(8,128)S(1)}, u32[]{:S(2)}) copy-start(f32[384,128]{1,0:T(8,128)S(1)} %get-tuple-element.30.refs_1_) | copy-start | bytes 589828
  55.4 17.2 %copy-start.4 = (f32[32,1024]{1,0:T(8,128)S(1)}, f32[32,1024]{1,0:T(8,128)}, u32[]{:S(2)}) copy-start(f32[32,1024]{1,0:T(8,128)} %params_ref.1) | copy-start | bytes 393220
  55.4 17.2 %copy-start.5 = (f32[32,1024]{1,0:T(8,128)S(1)}, f32[32,1024]{1,0:T(8,128)}, u32[]{:S(2)}) copy-start(f32[32,1024]{1,0:T(8,128)} %moment_ref.1) | copy-start | bytes 393220
  59.0 35.0 %collective-permute-start.5 = (bf16[384,512]{1,0:T(8,128)(2,1)}, bf16[384,512]{1,0:T(8,128)(2,1)}, u32[]{:S(2)}, u32[]{:S(2)}) collective-permute-start(bf16[384,512]{1,0:T(8,128)(2,1)} %part.2.refs_0_), channel_id=1, source_target_pairs={{0,4},{1,5},{2,6},{3,7},{4,0},{5,1},{6,2},{7,3},{8,12},{9,13},{10,... | collective-permute-start | bytes 1179656 | tf_op jit(solution)/shard_map/ppermute | solution.py:38
  72.5 7.7 %copy-start.7 = (bf16[2,1024,512]{2,1,0:T(8,128)(2,1)S(1)}, bf16[2,1024,512]{2,1,0:T(8,128)(2,1)}, u32[]{:S(2)}) copy-start(bf16[2,1024,512]{2,1,0:T(8,128)(2,1)} %copy-done.6) | copy-start | bytes 6291460
  84.7 11.1 %collective-permute-start.6 = (bf16[384,512]{1,0:T(8,128)(2,1)}, bf16[384,512]{1,0:T(8,128)(2,1)}, u32[]{:S(2)}, u32[]{:S(2)}) collective-permute-start(bf16[384,512]{1,0:T(8,128)(2,1)} %get-tuple-element.31), channel_id=1, source_target_pairs={{0,6},{1,7},{2,0},{3,1},{4,2},{5,3},{6,4},{7,5},{8,14},{9,15},{10,... | collective-permute-start | bytes 1179656 | tf_op jit(solution)/shard_map/ppermute | solution.py:38
  85.9 11.9 %collective-permute-start.7 = (bf16[384,512]{1,0:T(8,128)(2,1)}, bf16[384,512]{1,0:T(8,128)(2,1)}, u32[]{:S(2)}, u32[]{:S(2)}) collective-permute-start(bf16[384,512]{1,0:T(8,128)(2,1)} %get-tuple-element.29.refs_0_), channel_id=1, source_target_pairs={{0,2},{1,3},{2,4},{3,5},{4,6},{5,7},{6,0},{7,1},{8,10},{9,11},{10,... | collective-permute-start | bytes 1179656 | tf_op jit(solution)/shard_map/ppermute | solution.py:38
  87.9 35.3 %all-to-all-start.1 = ((bf16[16,32,1024]{2,1,0:T(8,128)(2,1)}), bf16[16,32,1024]{2,1,0:T(8,128)(2,1)}, u32[]{:S(2)}, u32[]{:S(2)}) async-start(bf16[16,32,1024]{2,1,0:T(8,128)(2,1)} %spread.1.refs_5_), calls=%async_computation.1 | async-start | bytes 2097152 | tf_op jit(solution)/shard_map/all_to_all | solution.py:577
  99.6 7.9 %collective-permute-start.10 = (bf16[256,384]{1,0:T(8,128)(2,1)S(1)}, bf16[256,384]{1,0:T(8,128)(2,1)S(1)}, u32[]{:S(2)}, u32[]{:S(2)}) collective-permute-start(bf16[256,384]{1,0:T(8,128)(2,1)S(1)} %get-tuple-element.32.refs_5_.refs_0_), channel_id=1, source_target_pairs={{0,6},{1,7},{2,0},{3,1},{4,2},{5,3},{6,4},{7,5},{8,14},{9,15},{10,... | collective-permute-start | bytes 589832 | tf_op jit(solution)/shard_map/ppermute | solution.py:38
  100.0 11.2 %collective-permute-start.8 = (bf16[256,384]{1,0:T(8,128)(2,1)S(1)}, bf16[256,384]{1,0:T(8,128)(2,1)S(1)}, u32[]{:S(2)}, u32[]{:S(2)}) collective-permute-start(bf16[256,384]{1,0:T(8,128)(2,1)S(1)} %get-tuple-element.32.refs_5_.refs_0_), channel_id=1, source_target_pairs={{0,4},{1,5},{2,6},{3,7},{4,0},{5,1},{6,2},{7,3},{8,12},{9,13},{10,... | collective-permute-start | bytes 589832 | tf_op jit(solution)/shard_map/ppermute | solution.py:38
  101.5 13.3 %collective-permute-start.9 = (bf16[256,384]{1,0:T(8,128)(2,1)S(1)}, bf16[256,384]{1,0:T(8,128)(2,1)S(1)}, u32[]{:S(2)}, u32[]{:S(2)}) collective-permute-start(bf16[256,384]{1,0:T(8,128)(2,1)S(1)} %get-tuple-element.32.refs_5_.refs_0_), channel_id=1, source_target_pairs={{0,2},{1,3},{2,4},{3,5},{4,6},{5,7},{6,0},{7,1},{8,10},{9,11},{10,... | collective-permute-start | bytes 589832 | tf_op jit(solution)/shard_map/ppermute | solution.py:38
  101.7 16.3 %collective-permute-start.11 = (bf16[256,384]{1,0:T(8,128)(2,1)S(1)}, bf16[256,384]{1,0:T(8,128)(2,1)S(1)}, u32[]{:S(2)}, u32[]{:S(2)}) collective-permute-start(bf16[256,384]{1,0:T(8,128)(2,1)S(1)} %get-tuple-element.33.refs_0_.refs_9_), channel_id=1, source_target_pairs={{0,4},{1,5},{2,6},{3,7},{4,0},{5,1},{6,2},{7,3},{8,12},{9,13},{10,... | collective-permute-start | bytes 589832 | tf_op jit(solution)/shard_map/ppermute | solution.py:38
  105.9 13.5 %collective-permute-start.12 = (bf16[256,384]{1,0:T(8,128)(2,1)S(1)}, bf16[256,384]{1,0:T(8,128)(2,1)S(1)}, u32[]{:S(2)}, u32[]{:S(2)}) collective-permute-start(bf16[256,384]{1,0:T(8,128)(2,1)S(1)} %get-tuple-element.33.refs_0_.refs_9_), channel_id=1, source_target_pairs={{0,2},{1,3},{2,4},{3,5},{4,6},{5,7},{6,0},{7,1},{8,10},{9,11},{10,... | collective-permute-start | bytes 589832 | tf_op jit(solution)/shard_map/ppermute | solution.py:38
  107.5 11.9 %collective-permute-start.13 = (bf16[256,384]{1,0:T(8,128)(2,1)S(1)}, bf16[256,384]{1,0:T(8,128)(2,1)S(1)}, u32[]{:S(2)}, u32[]{:S(2)}) collective-permute-start(bf16[256,384]{1,0:T(8,128)(2,1)S(1)} %get-tuple-element.33.refs_0_.refs_9_), channel_id=1, source_target_pairs={{0,6},{1,7},{2,0},{3,1},{4,2},{5,3},{6,4},{7,5},{8,14},{9,15},{10,... | collective-permute-start | bytes 589832 | tf_op jit(solution)/shard_map/ppermute | solution.py:38
  116.0 16.6 %collective-permute-start.15 = (bf16[1024,256]{1,0:T(8,128)(2,1)S(1)}, bf16[1024,256]{1,0:T(8,128)(2,1)S(1)}, u32[]{:S(2)}, u32[]{:S(2)}) collective-permute-start(bf16[1024,256]{1,0:T(8,128)(2,1)S(1)} %grad.3), channel_id=1, source_target_pairs={{0,1},{1,0},{2,3},{3,2},{4,5},{5,4},{6,7},{7,6},{8,9},{9,8},{10,11... | collective-permute-start | bytes 1572872 | tf_op jit(solution)/shard_map/ppermute | solution.py:593
  120.5 0.7 copy-start.2
  121.2 19.2 %collective-permute-start.14 = (bf16[1024,256]{1,0:T(8,128)(2,1)S(1)}, bf16[1024,256]{1,0:T(8,128)(2,1)S(1)}, u32[]{:S(2)}, u32[]{:S(2)}) collective-permute-start(bf16[1024,256]{1,0:T(8,128)(2,1)S(1)} %grad.2.refs_13_), channel_id=1, source_target_pairs={{0,1},{1,0},{2,3},{3,2},{4,5},{5,4},{6,7},{7,6},{8,9},{9,8},{10,11... | collective-permute-start | bytes 1572872 | tf_op jit(solution)/shard_map/ppermute | solution.py:593
  123.2 10.9 %collective-permute-start.4 = (bf16[16,32,1024]{2,1,0:T(8,128)(2,1)}, bf16[16,32,1024]{2,1,0:T(8,128)(2,1)S(1)}, u32[]{:S(2)}, u32[]{:S(2)}) collective-permute-start(bf16[16,32,1024]{2,1,0:T(8,128)(2,1)} %all-to-all-done.1.mine_ref), channel_id=1, source_target_pairs={{0,8},{8,0},{16,24},{24,16},{32,40},{40,32},{48,56},{56,48},{64,72... | collective-permute-start | bytes 3145736 | tf_op jit(solution)/shard_map/ppermute | solution.py:585
  123.2 0.9 copy-start.3

commit v4 on v3

--- a/solution.py
+++ b/solution.py
@@ -10,7 +10,7 @@
 BLOCK = 128
 N_Y = 4
 N_X = 2
-PER_STEP = 8
+PER_STEP = 16
 N_CORE = 2
 ANY = pl.BlockSpec(memory_space=pl.ANY)
 HBM = pl.BlockSpec(memory_space=pltpu.HBM)
@@ -50,13 +50,11 @@
     return scale, inverse
 
 
-def grid_spacing(magnitude):
-    whole = jnp.maximum((magnitude * 64.0).astype(jnp.int32), 1)
-    power = 31 - lax.clz(whole)
-    one = jnp.ones_like(whole)
-    spacing = lax.shift_left(one, power).astype(jnp.float32)
-    inverse = lax.shift_left(one, 15 - power).astype(jnp.float32) * 2.0**-15
-    return spacing, inverse
+def grid_steps(scaled):
+    zeros = lax.clz(jnp.maximum(scaled.astype(jnp.int32), 2))
+    spacing = lax.shift_right_logical(jnp.full_like(zeros, 2**30), zeros).astype(jnp.float32)
+    inverse = lax.shift_left(jnp.ones_like(zeros), zeros).astype(jnp.float32) * 2.0**-28
+    return spacing, scaled * inverse
 
 
 def outer_kernel(
@@ -83,16 +81,15 @@
             peak = jnp.max(jnp.abs(delta(replica, block)), axis=1, keepdims=True)
             largest = jnp.where(lane == replica * blocks + block, peak, largest)
     scales, inverses = power_not_below((largest + 1e-06) / 448.0)
+    scales, inverses = scales * 2.0**-9, inverses * 128.0
     for block in range(blocks):
         at = pl.ds(block * BLOCK, BLOCK)
         term = total[:, at]
         for replica in range(PER_STEP):
             slot = replica * blocks + block
             diff = delta(replica, block)
-            magnitude = jnp.abs(diff) * inverses[:, slot : slot + 1]
-            spacing, inverse = grid_spacing(magnitude)
-            level = jnp.floor(magnitude * (inverse * 512.0) + 0.5)
-            decoded = level * (spacing * (scales[:, slot : slot + 1] * 2.0**-9))
+            spacing, steps = grid_steps(jnp.abs(diff) * inverses[:, slot : slot + 1])
+            decoded = jnp.floor(steps + 0.5) * (spacing * scales[:, slot : slot + 1])
             term = term + jnp.where(diff < 0, -decoded, decoded)
         total[:, at] = term
 
@@ -326,7 +323,7 @@
 
 def part_kernel(count, *refs):
     blocks, weight_ref = refs[:count], refs[count]
-    parts, (held, sems) = refs[-2 - count : -2], refs[-2:]
+    parts, (held, result, sems, out_sems) = refs[-4 - count : -4], refs[-4:]
     rows = held.shape[2] // SPLIT
     reads = []
     for which in range(count):
@@ -348,7 +345,10 @@
                 read.wait()
             term = jnp.dot(held[which, half], weight_ref[half], preferred_element_type=jnp.float32)
             total = term if total is None else total + term
-        parts[which][...] = total.astype(jnp.bfloat16)
+        result[which] = total.astype(jnp.bfloat16)
+        pltpu.make_async_copy(result.at[which], parts[which], out_sems.at[which]).start()
+    for which in range(count):
+        pltpu.make_async_copy(result.at[which], parts[which], out_sems.at[which]).wait()
 
 
 def key_parts(blocks, weight, *after):
@@ -357,11 +357,13 @@
     return pl.pallas_call(
         functools.partial(part_kernel, count),
         in_specs=[HBM] * count + [VMEM] + [ANY] * len(after),
-        out_specs=[VMEM] * count,
+        out_specs=[HBM] * count,
         out_shape=[jax.ShapeDtypeStruct((rows, weight.shape[2]), jnp.bfloat16)] * count,
         scratch_shapes=[
             pltpu.VMEM((count,) + blocks[0].shape, jnp.bfloat16),
+            pltpu.VMEM((count, rows, weight.shape[2]), jnp.bfloat16),
             pltpu.SemaphoreType.DMA((count * N_X * SPLIT,)),
+            pltpu.SemaphoreType.DMA((count,)),
         ],
         compiler_params=PARAMS,
         cost_estimate=COST,
@@ -500,6 +502,7 @@
         out_specs=VMEM,
         out_shape=jax.ShapeDtypeStruct((block.shape[1], cots[0].shape[0]), jnp.bfloat16),
         compiler_params=PARAMS,
+        cost_estimate=pl.CostEstimate(flops=5 * 10**9, bytes_accessed=10**6, transcendentals=0),
         name="grad",
     )(block, gain, *cots)
 
@@ -570,7 +573,7 @@
     many = spread(fresh, chips, parts[3])
     others = [send_y(parts[step], N_Y - step) for step in (2, 1, 3)]
     cot = cotangent(base, factor, others, many)
-    cots = [[part] + [send_y(part, step) for step in (2, 1, 3)] for part in cot]
+    cots = [[part] + [send_y(part, step) for step in (1, 3, 2)] for part in cot]
 
     cores = [[chip * N_CORE + core for chip in range(chips)] for core in range(N_CORE)]
     own_rows, cols = fresh.shape
@@ -585,7 +588,7 @@
     theirs = lax.ppermute(mine, "rep", [(i, i ^ 1) for i in range(chips * N_CORE)])
     fresh_frag = merge_cores(lax.axis_index("rep") % N_CORE, mine, theirs).reshape(-1, cols)
 
-    blocks = [own, held[2], held[1], held[3]]
+    blocks = [own, held[1], held[3], held[2]]
     theirs, last = [], None
     loaded = load_half(blocks, wide_gain, 1 - x, cot[0])
     for half in range(HALVES):

time: 143 us -> 142 us (level)
  transfers between devices with their start and end apart: 18 -> 18, of which waited for: 9 -> 10; matrix products, arithmetic and copies ran while one was open for 1% -> 1% of each run, Pallas kernels for 32% -> 32%
where the time goes in v4:
time: 142 us; the launch traced here: 141 us
  waiting for transfers between devices  49.4 us (35%)
  Pallas kernels  48.8 us (34%)
  starting transfers between devices  39.4 us (28%)
  local copies, waits for them, and re-layouts  2.67 us (2%)
    ppermute x1, waiting for transfers between devices, per_device(): other = lax.ppermute(weight, 'fsdp', X_SWAP)  17.9 us
    ppermute x12, starting transfers between devices, send_y(): return lax.ppermute(block, 'fsdp', y_shift(step))  16.6 us
    all_to_all x1, waiting for transfers between devices, per_device(): frags = lax.all_to_all(fragment, 'rep', 0, 0, tiled=True)  13.1 us
    ppermute x12, waiting for transfers between devices, send_y(): return lax.ppermute(block, 'fsdp', y_shift(step))  9.91 us
    all_to_all x1, starting transfers between devices, per_device(): frags = lax.all_to_all(fragment, 'rep', 0, 0, tiled=True)  8.81 us
    ppermute x2, waiting for transfers between devices, per_device(): theirs.append(lax.ppermute(last, 'fsdp', X_SWAP))  8.52 us
    pallas_call x2, Pallas kernels, key_parts(): pl.pallas_call(functools.partial(part_kernel, count), in_specs=[HBM] * co...  8.12 us
    pallas_call x1, Pallas kernels, outer_step(): pl.pallas_call(functools.partial(outer_kernel, replicas), grid=(replicas...  7.12 us
  transfers between devices with their start and end apart: 18, of which 10 were waited for; matrix products, arithmetic and copies ran while one was open for 1% of the time, Pallas kernels for 32%

profile of v4, /device:TPU:32, one launch (start us, length us, event | category | flops | bytes accessed | tf_op | source)
XLA Modules:
  0.0 141.5 jit_solution(6215888408276589228)
XLA Ops:
  0.7 2.3 %cut.2.refs_2_ = bf16[2,384,1024]{2,1,0:T(8,128)(2,1)} custom-call(s32[1]{0:T(128)} %bitcast.2.at_ref, bf16[384,8192]{1,0:T(8,128)(2,1)} %bitcast.17), custom_call_target="tpu_custom_call" | custom-call | flops 999999995904 | bytes 1000000000 | tf_op jit(solution)/shard_map/cut/pallas_call | solution.py:213
  3.0 3.3 %collective-permute-start = (bf16[2,384,1024]{2,1,0:T(8,128)(2,1)}, bf16[2,384,1024]{2,1,0:T(8,128)(2,1)}, u32[]{:S(2)}, u32[]{:S(2)}) collective-permute-start(bf16[2,384,1024]{2,1,0:T(8,128)(2,1)} %cut.2.refs_2_), channel_id=1, source_target_pairs={{0,4},{1,5},{2,6},{3,7},{4,0},{5,1},{6,2},{7,3},{8,12},{9,13},{10,... | collective-permute-start | bytes 4718600 | tf_op jit(solution)/shard_map/ppermute | solution.py:38
  6.3 2.8 %behind.1 = (bf16[1024,1024]{1,0:T(8,128)(2,1)}, bf16[1024,512]{1,0:T(8,128)(2,1)}) custom-call(bf16[1024,1024]{1,0:T(8,128)(2,1)} %bitcast.20, bf16[1024,512]{1,0:T(8,128)(2,1)} %bitcast.21, bf16[2,384,1024]{2,1,0:T(8,128)(2,1)} %cut.2.refs_2_), custom_call_target="tpu_custom_call" | custom-call | flops 999999995904 | bytes 1000000000 | tf_op jit(solution)/shard_map/behind/pallas_call | solution.py:252
  9.1 3.1 %collective-permute-start.1 = (bf16[1024,512]{1,0:T(8,128)(2,1)}, bf16[1024,512]{1,0:T(8,128)(2,1)}, u32[]{:S(2)}, u32[]{:S(2)}) collective-permute-start(bf16[1024,512]{1,0:T(8,128)(2,1)} %get-tuple-element.21.weight_ref), channel_id=1, source_target_pairs={{0,1},{1,0},{2,3},{3,2},{4,5},{5,4},{6,7},{7,6},{8,9},{9,8},{10,11... | collective-permute-start | bytes 3145736 | tf_op jit(solution)/shard_map/ppermute | solution.py:562
  12.2 8.8 %all-to-all-start = ((bf16[32,32,1024]{2,1,0:T(8,128)(2,1)}), bf16[32,32,1024]{2,1,0:T(8,128)(2,1)}, u32[]{:S(2)}, u32[]{:S(2)}) async-start(bf16[32,32,1024]{2,1,0:T(8,128)(2,1)} %bitcast.4), calls=%async_computation | async-start | bytes 4194304 | tf_op jit(solution)/shard_map/all_to_all | solution.py:555
  21.0 0.1 pad_add_fusion.at_ref
  21.1 3.8 %cut.3 = (bf16[2,384,1024]{2,1,0:T(8,128)(2,1)}, bf16[2,384,1024]{2,1,0:T(8,128)(2,1)}, bf16[2,384,1024]{2,1,0:T(8,128)(2,1)S(1)}) custom-call(s32[3]{0:T(128)S(1)} %pad_add_fusion.at_ref, bf16[384,8192]{1,0:T(8,128)(2,1)} %bitcast.18, bf16[1024,1024]{1,0:T(8,128)(2,1)} %get-tuple-element.20.refs_0_), custom_call_target="tpu_custom_call" | custom-call | flops 999999995904 | bytes 1000000000 | tf_op jit(solution)/shard_map/cut/pallas_call | solution.py:213
  24.9 0.8 collective-permute-start.2
  25.7 2.6 %collective-permute-start.3 = (bf16[2,384,1024]{2,1,0:T(8,128)(2,1)}, bf16[2,384,1024]{2,1,0:T(8,128)(2,1)}, u32[]{:S(2)}, u32[]{:S(2)}) collective-permute-start(bf16[2,384,1024]{2,1,0:T(8,128)(2,1)} %get-tuple-element.28), channel_id=1, source_target_pairs={{0,6},{1,7},{2,0},{3,1},{4,2},{5,3},{6,4},{7,5},{8,14},{9,15},{10,... | collective-permute-start | bytes 4718600 | tf_op jit(solution)/shard_map/ppermute | solution.py:38
  28.2 0.7 dynamic_slice.3
  28.9 17.9 %collective-permute-done.1.other_ref = bf16[1024,512]{1,0:T(8,128)(2,1)} collective-permute-done((bf16[1024,512]{1,0:T(8,128)(2,1)}, bf16[1024,512]{1,0:T(8,128)(2,1)}, u32[]{:S(2)}, u32[]{:S(2)}) %collective-permute-start.1) | collective-permute-done | bytes 1048608 | tf_op jit(solution)/shard_map/ppermute | solution.py:562
  46.9 0.3 broadcast_in_dim.11.gain_ref.refs_4_
  47.2 2.3 %pair.1.weight_ref.refs_1_.refs_2_ = bf16[2,1024,512]{2,1,0:T(8,128)(2,1)S(1)} custom-call(s32[1]{0:T(128)} %bitcast.5.x_ref.half_ref, bf16[1024,512]{1,0:T(8,128)(2,1)} %get-tuple-element.21.weight_ref, bf16[1024,512]{1,0:T(8,128)(2,1)} %collective-permute-done.1.other_ref, f32[2,1024,128]{2,1,0:T(8,128)S(1)} %broadcast_in_dim.11.gain_ref.refs_4_), custom_call_target="tpu_custom_call" | custom-call | flops 999999995904 | bytes 1000000000 | tf_op jit(solution)/shard_map/pair/pallas_call | solution.py:275
  49.6 5.7 %own.1 = (f32[384,512]{1,0:T(8,128)S(1)}, f32[384,128]{1,0:T(8,128)S(1)}) custom-call(bf16[384,8192]{1,0:T(8,128)(2,1)} %bitcast.19, bf16[2,384,1024]{2,1,0:T(8,128)(2,1)S(1)} %get-tuple-element.22.block_ref.refs_0_, bf16[2,1024,512]{2,1,0:T(8,128)(2,1)S(1)} %pair.1.weight_ref.refs_1_.refs_2_, bf16[384,512]{1,0:T(8,128)(2,1)} %bitcast.22), custom_call_target="tpu_custom_call" | custom-call | flops 999999995904 | bytes 1000000000 | tf_op jit(solution)/shard_map/own/pallas_call | solution.py:304
  55.4 3.6 %part.2.refs_0_ = bf16[384,512]{1,0:T(8,128)(2,1)} custom-call(bf16[2,384,1024]{2,1,0:T(8,128)(2,1)} %collective-permute-done.refs_0_.refs_3_, bf16[2,1024,512]{2,1,0:T(8,128)(2,1)S(1)} %pair.1.weight_ref.refs_1_.refs_2_, f32[384,512]{1,0:T(8,128)S(1)} %get-tuple-element.23.refs_2_.refs_0_), custom_call_target="tpu_custom_call" | custom-call | flops 999999995904 | bytes 1000000000 | tf_op jit(solution)/shard_map/part/pallas_call | solution.py:357
  59.0 0.4 collective-permute-start.5
  59.5 13.1 %all-to-all-done.frag_ref = bf16[32,32,1024]{2,1,0:T(8,128)(2,1)} async-done(((bf16[32,32,1024]{2,1,0:T(8,128)(2,1)}), bf16[32,32,1024]{2,1,0:T(8,128)(2,1)}, u32[]{:S(2)}, u32[]{:S(2)}) %all-to-all-start) | async-done | bytes 2097184 | tf_op jit(solution)/shard_map/all_to_all | solution.py:555
  72.5 7.1 %outer.1 = (f32[32,1024]{1,0:T(8,128)}, f32[32,1024]{1,0:T(8,128)}, bf16[32,1024]{1,0:T(8,128)(2,1)S(1)}) custom-call(bf16[32,32,1024]{2,1,0:T(8,128)(2,1)} %all-to-all-done.frag_ref, f32[32,1024]{1,0:T(8,128)S(1)} %copy-done.4, f32[32,1024]{1,0:T(8,128)S(1)} %copy-done.5, bf16[384,512]{1,0:T(8,128)(2,1)} %part.2.refs_0_), custom_call_target="tpu_custom_call" | custom-call | flops 999999995904 | bytes 1000000000 | tf_op jit(solution)/shard_map/outer/pallas_call | solution.py:109
  79.7 4.5 %part.3 = (bf16[384,512]{1,0:T(8,128)(2,1)}, bf16[384,512]{1,0:T(8,128)(2,1)}) custom-call(bf16[2,384,1024]{2,1,0:T(8,128)(2,1)} %collective-permute-done.2.refs_0_.refs_1_, bf16[2,384,1024]{2,1,0:T(8,128)(2,1)} %collective-permute-done.3.refs_1_.refs_2_, bf16[2,1024,512]{2,1,0:T(8,128)(2,1)S(1)} %copy-done.7, ...), custom_call_target="tpu_custom_call" | custom-call | flops 999999995904 | bytes 1000000000 | tf_op jit(solution)/shard_map/part/pallas_call | solution.py:357
  84.2 1.1 collective-permute-start.6
  85.3 1.0 collective-permute-start.7
  86.3 1.0 spread.1.refs_5_
  87.3 6.7 %all-to-all-start.1 = ((bf16[16,32,1024]{2,1,0:T(8,128)(2,1)}), bf16[16,32,1024]{2,1,0:T(8,128)(2,1)}, u32[]{:S(2)}, u32[]{:S(2)}) async-start(bf16[16,32,1024]{2,1,0:T(8,128)(2,1)} %spread.1.refs_5_), calls=%async_computation.1 | async-start | bytes 2097152 | tf_op jit(solution)/shard_map/all_to_all | solution.py:580
  94.0 1.2 collective-permute-done.6.refs_3_
  95.2 2.0 %collective-permute-done.7.refs_4_ = bf16[384,512]{1,0:T(8,128)(2,1)} collective-permute-done((bf16[384,512]{1,0:T(8,128)(2,1)}, bf16[384,512]{1,0:T(8,128)(2,1)}, u32[]{:S(2)}, u32[]{:S(2)}) %collective-permute-start.7) | collective-permute-done | bytes 393248 | tf_op jit(solution)/shard_map/ppermute | solution.py:38
  97.2 1.8 %cot.1 = (bf16[256,384]{1,0:T(8,128)(2,1)S(1)}, bf16[256,384]{1,0:T(8,128)(2,1)S(1)}) custom-call(f32[384,512]{1,0:T(8,128)} %copy-done.8, f32[384,128]{1,0:T(8,128)} %copy-done.9, bf16[384,512]{1,0:T(8,128)(2,1)} %collective-permute-done.5.refs_2_, bf16[384,512]{1,0:T(8,128)(2,1)} %collective-permute-done.6.refs_3_, ...), custom_call_target="tpu_custom_call" | custom-call | flops 999999995904 | bytes 1000000000 | tf_op jit(solution)/shard_map/cot/pallas_call | solution.py:400
  99.1 0.6 collective-permute-start.10
  99.6 0.7 collective-permute-start.8
  100.3 2.6 %collective-permute-start.9 = (bf16[256,384]{1,0:T(8,128)(2,1)S(1)}, bf16[256,384]{1,0:T(8,128)(2,1)S(1)}, u32[]{:S(2)}, u32[]{:S(2)}) collective-permute-start(bf16[256,384]{1,0:T(8,128)(2,1)S(1)} %get-tuple-element.32.refs_5_.refs_0_), channel_id=1, source_target_pairs={{0,6},{1,7},{2,0},{3,1},{4,2},{5,3},{6,4},{7,5},{8,14},{9,15},{10,... | collective-permute-start | bytes 589832 | tf_op jit(solution)/shard_map/ppermute | solution.py:38
  102.9 3.2 %collective-permute-start.12 = (bf16[256,384]{1,0:T(8,128)(2,1)S(1)}, bf16[256,384]{1,0:T(8,128)(2,1)S(1)}, u32[]{:S(2)}, u32[]{:S(2)}) collective-permute-start(bf16[256,384]{1,0:T(8,128)(2,1)S(1)} %get-tuple-element.33.refs_0_.refs_9_), channel_id=1, source_target_pairs={{0,6},{1,7},{2,0},{3,1},{4,2},{5,3},{6,4},{7,5},{8,14},{9,15},{10,... | collective-permute-start | bytes 589832 | tf_op jit(solution)/shard_map/ppermute | solution.py:38
  106.1 2.0 %load.1 = (bf16[1536,1024]{1,0:T(8,128)(2,1)S(1)}, f32[1024,128]{1,0:T(8,128)S(1)}) custom-call(s32[1]{0:T(128)} %bitcast.12.half_ref, bf16[2,384,1024]{2,1,0:T(8,128)(2,1)} %copy-done.1, bf16[2,384,1024]{2,1,0:T(8,128)(2,1)} %collective-permute-done.2.refs_0_.refs_1_, bf16[2,384,1024]{2,1,0:T(8,128)(2,1)} %collective-permute-done.3.refs_1_.refs_2_, ...), custom_call_target="tpu_custom_call" | custom-call | tf_op jit(solution)/shard_map/load/pallas_call | solution.py:472
  108.2 0.3 collective-permute-done.10.refs_8_.refs_3_
  108.5 0.5 collective-permute-start.13
  109.0 1.8 %collective-permute-done.8.refs_6_.refs_1_ = bf16[256,384]{1,0:T(8,128)(2,1)S(1)} collective-permute-done((bf16[256,384]{1,0:T(8,128)(2,1)S(1)}, bf16[256,384]{1,0:T(8,128)(2,1)S(1)}, u32[]{:S(2)}, u32[]{:S(2)}) %collective-permute-start.8) | collective-permute-done | bytes 196640 | tf_op jit(solution)/shard_map/ppermute | solution.py:38
  110.7 1.1 grad.3
  111.9 2.1 %collective-permute-start.15 = (bf16[1024,256]{1,0:T(8,128)(2,1)S(1)}, bf16[1024,256]{1,0:T(8,128)(2,1)S(1)}, u32[]{:S(2)}, u32[]{:S(2)}) collective-permute-start(bf16[1024,256]{1,0:T(8,128)(2,1)S(1)} %grad.3), channel_id=1, source_target_pairs={{0,1},{1,0},{2,3},{3,2},{4,5},{5,4},{6,7},{7,6},{8,9},{9,8},{10,11... | collective-permute-start | bytes 1572872 | tf_op jit(solution)/shard_map/ppermute | solution.py:596
  114.0 2.3 %collective-permute-done.11.refs_1_.refs_10_ = bf16[256,384]{1,0:T(8,128)(2,1)S(1)} collective-permute-done((bf16[256,384]{1,0:T(8,128)(2,1)S(1)}, bf16[256,384]{1,0:T(8,128)(2,1)S(1)}, u32[]{:S(2)}, u32[]{:S(2)}) %collective-permute-start.11) | collective-permute-done | bytes 196640 | tf_op jit(solution)/shard_map/ppermute | solution.py:38
  116.4 2.2 %collective-permute-done.13.refs_3_.refs_12_ = bf16[256,384]{1,0:T(8,128)(2,1)S(1)} collective-permute-done((bf16[256,384]{1,0:T(8,128)(2,1)S(1)}, bf16[256,384]{1,0:T(8,128)(2,1)S(1)}, u32[]{:S(2)}, u32[]{:S(2)}) %collective-permute-start.13) | collective-permute-done | bytes 196640 | tf_op jit(solution)/shard_map/ppermute | solution.py:38
  118.6 1.1 grad.2.refs_13_
  119.7 0.7 copy-done.2
  120.4 2.0 %collective-permute-start.14 = (bf16[1024,256]{1,0:T(8,128)(2,1)S(1)}, bf16[1024,256]{1,0:T(8,128)(2,1)S(1)}, u32[]{:S(2)}, u32[]{:S(2)}) collective-permute-start(bf16[1024,256]{1,0:T(8,128)(2,1)S(1)} %grad.2.refs_13_), channel_id=1, source_target_pairs={{0,1},{1,0},{2,3},{3,2},{4,5},{5,4},{6,7},{7,6},{8,9},{9,8},{10,11... | collective-permute-start | bytes 1572872 | tf_op jit(solution)/shard_map/ppermute | solution.py:596
  122.4 0.9 copy-done.3
  123.3 4.0 %kept.1.own_ref = f32[1024,512]{1,0:T(8,128)S(1)} custom-call(s32[1]{0:T(128)} %bitcast.5.x_ref.half_ref, bf16[2,384,1024]{2,1,0:T(8,128)(2,1)} %copy-done.1, bf16[2,384,1024]{2,1,0:T(8,128)(2,1)} %collective-permute-done.2.refs_0_.refs_1_, bf16[2,384,1024]{2,1,0:T(8,128)(2,1)} %collective-permute-done.3.refs_1_.refs_2_, ...), custom_call_target="tpu_custom_call" | custom-call | flops 20000000000 | bytes 1000000 | tf_op jit(solution)/shard_map/kept/pallas_call | solution.py:522
  127.3 2.0 %collective-permute-done.15.theirs_ref = bf16[1024,256]{1,0:T(8,128)(2,1)S(1)} collective-permute-done((bf16[1024,256]{1,0:T(8,128)(2,1)S(1)}, bf16[1024,256]{1,0:T(8,128)(2,1)S(1)}, u32[]{:S(2)}, u32[]{:S(2)}) %collective-permute-start.15) | collective-permute-done | bytes 524320 | tf_op jit(solution)/shard_map/ppermute | solution.py:596
  129.4 1.5 %add.32.refs_0_ = bf16[1024,512]{1,0:T(8,128)(2,1)} custom-call(f32[1024,512]{1,0:T(8,128)S(1)} %kept.1.own_ref, bf16[1024,256]{1,0:T(8,128)(2,1)S(1)} %collective-permute-done.15.theirs_ref), custom_call_target="tpu_custom_call" | custom-call | tf_op jit(solution)/shard_map/add/pallas_call | solution.py:435
  130.9 2.4 %merge.1 = bf16[16,2,32,1024]{3,2,1,0:T(8,128)(2,1)} custom-call(s32[1]{0:T(128)} %bitcast.10.core_ref, bf16[16,32,1024]{2,1,0:T(8,128)(2,1)} %all-to-all-done.1.mine_ref, bf16[16,32,1024]{2,1,0:T(8,128)(2,1)S(1)} %collective-permute-done.4.theirs_ref), custom_call_target="tpu_custom_call" | custom-call | tf_op jit(solution)/shard_map/merge/pallas_call | solution.py:171
  133.3 6.5 %collective-permute-done.14.theirs_ref = bf16[1024,256]{1,0:T(8,128)(2,1)S(1)} collective-permute-done((bf16[1024,256]{1,0:T(8,128)(2,1)S(1)}, bf16[1024,256]{1,0:T(8,128)(2,1)S(1)}, u32[]{:S(2)}, u32[]{:S(2)}) %collective-permute-start.14) | collective-permute-done | bytes 524320 | tf_op jit(solution)/shard_map/ppermute | solution.py:596
  139.8 1.5 %add.33 = bf16[1024,512]{1,0:T(8,128)(2,1)} custom-call(f32[1024,512]{1,0:T(8,128)S(1)} %kept.1.own_ref, bf16[1024,256]{1,0:T(8,128)(2,1)S(1)} %collective-permute-done.14.theirs_ref, bf16[1024,512]{1,0:T(8,128)(2,1)} %add.32.refs_0_, bf16[1024,1024]{1,0:T(8,128)(2,1)} %bitcast.14), custom_call_target="tpu_custom_call", output_to_operand_aliasing={{}: (2, {})} | custom-call | tf_op jit(solution)/shard_map/add/pallas_call | solution.py:435
  (29 shorter events, 0.1 us)
Async XLA Ops:
  3.0 52.4 %collective-permute-start = (bf16[2,384,1024]{2,1,0:T(8,128)(2,1)}, bf16[2,384,1024]{2,1,0:T(8,128)(2,1)}, u32[]{:S(2)}, u32[]{:S(2)}) collective-permute-start(bf16[2,384,1024]{2,1,0:T(8,128)(2,1)} %cut.2.refs_2_), channel_id=1, source_target_pairs={{0,4},{1,5},{2,6},{3,7},{4,0},{5,1},{6,2},{7,3},{8,12},{9,13},{10,... | collective-permute-start | bytes 4718600 | tf_op jit(solution)/shard_map/ppermute | solution.py:38
  9.1 37.8 %collective-permute-start.1 = (bf16[1024,512]{1,0:T(8,128)(2,1)}, bf16[1024,512]{1,0:T(8,128)(2,1)}, u32[]{:S(2)}, u32[]{:S(2)}) collective-permute-start(bf16[1024,512]{1,0:T(8,128)(2,1)} %get-tuple-element.21.weight_ref), channel_id=1, source_target_pairs={{0,1},{1,0},{2,3},{3,2},{4,5},{5,4},{6,7},{7,6},{8,9},{9,8},{10,11... | collective-permute-start | bytes 3145736 | tf_op jit(solution)/shard_map/ppermute | solution.py:562
  12.2 60.3 %all-to-all-start = ((bf16[32,32,1024]{2,1,0:T(8,128)(2,1)}), bf16[32,32,1024]{2,1,0:T(8,128)(2,1)}, u32[]{:S(2)}, u32[]{:S(2)}) async-start(bf16[32,32,1024]{2,1,0:T(8,128)(2,1)} %bitcast.4), calls=%async_computation | async-start | bytes 4194304 | tf_op jit(solution)/shard_map/all_to_all | solution.py:555
  24.9 24.7 %copy-start.1 = (bf16[2,384,1024]{2,1,0:T(8,128)(2,1)}, bf16[2,384,1024]{2,1,0:T(8,128)(2,1)S(1)}, u32[]{:S(2)}) copy-start(bf16[2,384,1024]{2,1,0:T(8,128)(2,1)S(1)} %get-tuple-element.22.block_ref.refs_0_) | copy-start | bytes 4718596
  24.9 54.8 %collective-permute-start.2 = (bf16[2,384,1024]{2,1,0:T(8,128)(2,1)}, bf16[2,384,1024]{2,1,0:T(8,128)(2,1)}, u32[]{:S(2)}, u32[]{:S(2)}) collective-permute-start(bf16[2,384,1024]{2,1,0:T(8,128)(2,1)} %get-tuple-element.27), channel_id=1, source_target_pairs={{0,2},{1,3},{2,4},{3,5},{4,6},{5,7},{6,0},{7,1},{8,10},{9,11},{10,... | collective-permute-start | bytes 4718600 | tf_op jit(solution)/shard_map/ppermute | solution.py:38
  25.7 54.0 %collective-permute-start.3 = (bf16[2,384,1024]{2,1,0:T(8,128)(2,1)}, bf16[2,384,1024]{2,1,0:T(8,128)(2,1)}, u32[]{:S(2)}, u32[]{:S(2)}) collective-permute-start(bf16[2,384,1024]{2,1,0:T(8,128)(2,1)} %get-tuple-element.28), channel_id=1, source_target_pairs={{0,6},{1,7},{2,0},{3,1},{4,2},{5,3},{6,4},{7,5},{8,14},{9,15},{10,... | collective-permute-start | bytes 4718600 | tf_op jit(solution)/shard_map/ppermute | solution.py:38
  47.2 2.3 %copy-start = (f32[2,1024,128]{2,1,0:T(8,128)}, f32[2,1024,128]{2,1,0:T(8,128)S(1)}, u32[]{:S(2)}) copy-start(f32[2,1024,128]{2,1,0:T(8,128)S(1)} %broadcast_in_dim.11.gain_ref.refs_4_) | copy-start | bytes 3145732
  49.5 5.8 %copy-start.6 = (bf16[2,1024,512]{2,1,0:T(8,128)(2,1)}, bf16[2,1024,512]{2,1,0:T(8,128)(2,1)S(1)}, u32[]{:S(2)}) copy-start(bf16[2,1024,512]{2,1,0:T(8,128)(2,1)S(1)} %pair.1.weight_ref.refs_1_.refs_2_) | copy-start | bytes 6291460
  55.3 3.7 %copy-start.8 = (f32[384,512]{1,0:T(8,128)}, f32[384,512]{1,0:T(8,128)S(1)}, u32[]{:S(2)}) copy-start(f32[384,512]{1,0:T(8,128)S(1)} %get-tuple-element.23.refs_2_.refs_0_) | copy-start | bytes 2359300
  55.3 3.7 %copy-start.9 = (f32[384,128]{1,0:T(8,128)}, f32[384,128]{1,0:T(8,128)S(1)}, u32[]{:S(2)}) copy-start(f32[384,128]{1,0:T(8,128)S(1)} %get-tuple-element.30.refs_1_) | copy-start | bytes 589828
  55.4 17.2 %copy-start.4 = (f32[32,1024]{1,0:T(8,128)S(1)}, f32[32,1024]{1,0:T(8,128)}, u32[]{:S(2)}) copy-start(f32[32,1024]{1,0:T(8,128)} %params_ref.1) | copy-start | bytes 393220
  55.4 17.2 %copy-start.5 = (f32[32,1024]{1,0:T(8,128)S(1)}, f32[32,1024]{1,0:T(8,128)}, u32[]{:S(2)}) copy-start(f32[32,1024]{1,0:T(8,128)} %moment_ref.1) | copy-start | bytes 393220
  59.0 35.0 %collective-permute-start.5 = (bf16[384,512]{1,0:T(8,128)(2,1)}, bf16[384,512]{1,0:T(8,128)(2,1)}, u32[]{:S(2)}, u32[]{:S(2)}) collective-permute-start(bf16[384,512]{1,0:T(8,128)(2,1)} %part.2.refs_0_), channel_id=1, source_target_pairs={{0,4},{1,5},{2,6},{3,7},{4,0},{5,1},{6,2},{7,3},{8,12},{9,13},{10,... | collective-permute-start | bytes 1179656 | tf_op jit(solution)/shard_map/ppermute | solution.py:38
  72.5 7.1 %copy-start.7 = (bf16[2,1024,512]{2,1,0:T(8,128)(2,1)S(1)}, bf16[2,1024,512]{2,1,0:T(8,128)(2,1)}, u32[]{:S(2)}) copy-start(bf16[2,1024,512]{2,1,0:T(8,128)(2,1)} %copy-done.6) | copy-start | bytes 6291460
  84.2 11.1 %collective-permute-start.6 = (bf16[384,512]{1,0:T(8,128)(2,1)}, bf16[384,512]{1,0:T(8,128)(2,1)}, u32[]{:S(2)}, u32[]{:S(2)}) collective-permute-start(bf16[384,512]{1,0:T(8,128)(2,1)} %get-tuple-element.31), channel_id=1, source_target_pairs={{0,6},{1,7},{2,0},{3,1},{4,2},{5,3},{6,4},{7,5},{8,14},{9,15},{10,... | collective-permute-start | bytes 1179656 | tf_op jit(solution)/shard_map/ppermute | solution.py:38
  85.3 11.9 %collective-permute-start.7 = (bf16[384,512]{1,0:T(8,128)(2,1)}, bf16[384,512]{1,0:T(8,128)(2,1)}, u32[]{:S(2)}, u32[]{:S(2)}) collective-permute-start(bf16[384,512]{1,0:T(8,128)(2,1)} %get-tuple-element.29.refs_0_), channel_id=1, source_target_pairs={{0,2},{1,3},{2,4},{3,5},{4,6},{5,7},{6,0},{7,1},{8,10},{9,11},{10,... | collective-permute-start | bytes 1179656 | tf_op jit(solution)/shard_map/ppermute | solution.py:38
  87.3 35.1 %all-to-all-start.1 = ((bf16[16,32,1024]{2,1,0:T(8,128)(2,1)}), bf16[16,32,1024]{2,1,0:T(8,128)(2,1)}, u32[]{:S(2)}, u32[]{:S(2)}) async-start(bf16[16,32,1024]{2,1,0:T(8,128)(2,1)} %spread.1.refs_5_), calls=%async_computation.1 | async-start | bytes 2097152 | tf_op jit(solution)/shard_map/all_to_all | solution.py:580
  99.1 9.4 %collective-permute-start.10 = (bf16[256,384]{1,0:T(8,128)(2,1)S(1)}, bf16[256,384]{1,0:T(8,128)(2,1)S(1)}, u32[]{:S(2)}, u32[]{:S(2)}) collective-permute-start(bf16[256,384]{1,0:T(8,128)(2,1)S(1)} %get-tuple-element.32.refs_5_.refs_0_), channel_id=1, source_target_pairs={{0,4},{1,5},{2,6},{3,7},{4,0},{5,1},{6,2},{7,3},{8,12},{9,13},{10,... | collective-permute-start | bytes 589832 | tf_op jit(solution)/shard_map/ppermute | solution.py:38
  99.6 11.1 %collective-permute-start.8 = (bf16[256,384]{1,0:T(8,128)(2,1)S(1)}, bf16[256,384]{1,0:T(8,128)(2,1)S(1)}, u32[]{:S(2)}, u32[]{:S(2)}) collective-permute-start(bf16[256,384]{1,0:T(8,128)(2,1)S(1)} %get-tuple-element.32.refs_5_.refs_0_), channel_id=1, source_target_pairs={{0,2},{1,3},{2,4},{3,5},{4,6},{5,7},{6,0},{7,1},{8,10},{9,11},{10,... | collective-permute-start | bytes 589832 | tf_op jit(solution)/shard_map/ppermute | solution.py:38
  100.3 10.4 %collective-permute-start.9 = (bf16[256,384]{1,0:T(8,128)(2,1)S(1)}, bf16[256,384]{1,0:T(8,128)(2,1)S(1)}, u32[]{:S(2)}, u32[]{:S(2)}) collective-permute-start(bf16[256,384]{1,0:T(8,128)(2,1)S(1)} %get-tuple-element.32.refs_5_.refs_0_), channel_id=1, source_target_pairs={{0,6},{1,7},{2,0},{3,1},{4,2},{5,3},{6,4},{7,5},{8,14},{9,15},{10,... | collective-permute-start | bytes 589832 | tf_op jit(solution)/shard_map/ppermute | solution.py:38
  102.9 13.5 %collective-permute-start.11 = (bf16[256,384]{1,0:T(8,128)(2,1)S(1)}, bf16[256,384]{1,0:T(8,128)(2,1)S(1)}, u32[]{:S(2)}, u32[]{:S(2)}) collective-permute-start(bf16[256,384]{1,0:T(8,128)(2,1)S(1)} %get-tuple-element.33.refs_0_.refs_9_), channel_id=1, source_target_pairs={{0,2},{1,3},{2,4},{3,5},{4,6},{5,7},{6,0},{7,1},{8,10},{9,11},{10,... | collective-permute-start | bytes 589832 | tf_op jit(solution)/shard_map/ppermute | solution.py:38
  102.9 13.5 %collective-permute-start.12 = (bf16[256,384]{1,0:T(8,128)(2,1)S(1)}, bf16[256,384]{1,0:T(8,128)(2,1)S(1)}, u32[]{:S(2)}, u32[]{:S(2)}) collective-permute-start(bf16[256,384]{1,0:T(8,128)(2,1)S(1)} %get-tuple-element.33.refs_0_.refs_9_), channel_id=1, source_target_pairs={{0,6},{1,7},{2,0},{3,1},{4,2},{5,3},{6,4},{7,5},{8,14},{9,15},{10,... | collective-permute-start | bytes 589832 | tf_op jit(solution)/shard_map/ppermute | solution.py:38
  108.5 10.1 %collective-permute-start.13 = (bf16[256,384]{1,0:T(8,128)(2,1)S(1)}, bf16[256,384]{1,0:T(8,128)(2,1)S(1)}, u32[]{:S(2)}, u32[]{:S(2)}) collective-permute-start(bf16[256,384]{1,0:T(8,128)(2,1)S(1)} %get-tuple-element.33.refs_0_.refs_9_), channel_id=1, source_target_pairs={{0,4},{1,5},{2,6},{3,7},{4,0},{5,1},{6,2},{7,3},{8,12},{9,13},{10,... | collective-permute-start | bytes 589832 | tf_op jit(solution)/shard_map/ppermute | solution.py:38
  111.9 17.5 %collective-permute-start.15 = (bf16[1024,256]{1,0:T(8,128)(2,1)S(1)}, bf16[1024,256]{1,0:T(8,128)(2,1)S(1)}, u32[]{:S(2)}, u32[]{:S(2)}) collective-permute-start(bf16[1024,256]{1,0:T(8,128)(2,1)S(1)} %grad.3), channel_id=1, source_target_pairs={{0,1},{1,0},{2,3},{3,2},{4,5},{5,4},{6,7},{7,6},{8,9},{9,8},{10,11... | collective-permute-start | bytes 1572872 | tf_op jit(solution)/shard_map/ppermute | solution.py:596
  119.7 0.7 copy-start.2
  120.4 19.4 %collective-permute-start.14 = (bf16[1024,256]{1,0:T(8,128)(2,1)S(1)}, bf16[1024,256]{1,0:T(8,128)(2,1)S(1)}, u32[]{:S(2)}, u32[]{:S(2)}) collective-permute-start(bf16[1024,256]{1,0:T(8,128)(2,1)S(1)} %grad.2.refs_13_), channel_id=1, source_target_pairs={{0,1},{1,0},{2,3},{3,2},{4,5},{5,4},{6,7},{7,6},{8,9},{9,8},{10,11... | collective-permute-start | bytes 1572872 | tf_op jit(solution)/shard_map/ppermute | solution.py:596
  122.4 8.5 %collective-permute-start.4 = (bf16[16,32,1024]{2,1,0:T(8,128)(2,1)}, bf16[16,32,1024]{2,1,0:T(8,128)(2,1)S(1)}, u32[]{:S(2)}, u32[]{:S(2)}) collective-permute-start(bf16[16,32,1024]{2,1,0:T(8,128)(2,1)} %all-to-all-done.1.mine_ref), channel_id=1, source_target_pairs={{0,8},{8,0},{16,24},{24,16},{32,40},{40,32},{48,56},{56,48},{64,72... | collective-permute-start | bytes 3145736 | tf_op jit(solution)/shard_map/ppermute | solution.py:588
  122.4 0.9 copy-start.3

commit v5 on v4

--- a/solution.py
+++ b/solution.py
@@ -491,20 +491,20 @@
         out_ref[at, pl.ds(group * width, width)] = total.astype(out_ref.dtype)
 
 
-def grad_kernel(block_ref, gain_ref, *refs):
-    grad_tiles(block_ref, gain_ref, refs[:-1], refs[-1], 0)
-
-
-def sent_grad(block, gain, cots):
-    return pl.pallas_call(
-        grad_kernel,
+def grad_kernel(order, block_ref, gain_ref, *refs):
+    grad_tiles(block_ref, gain_ref, [refs[order.index(which)] for which in range(len(order))], refs[-1], 0)
+
+
+def sent_grad(block, gain, cots, order):
+    return pl.pallas_call(
+        functools.partial(grad_kernel, order),
         in_specs=[VMEM] * (2 + len(cots)),
         out_specs=VMEM,
         out_shape=jax.ShapeDtypeStruct((block.shape[1], cots[0].shape[0]), jnp.bfloat16),
         compiler_params=PARAMS,
         cost_estimate=pl.CostEstimate(flops=5 * 10**9, bytes_accessed=10**6, transcendentals=0),
         name="grad",
-    )(block, gain, *cots)
+    )(block, gain, *(cots[which] for which in order))
 
 
 def kept_kernel(count, half_ref, *refs):
@@ -592,7 +592,7 @@
     theirs, last = [], None
     loaded = load_half(blocks, wide_gain, 1 - x, cot[0])
     for half in range(HALVES):
-        last = sent_grad(*loaded, cots[half])
+        last = sent_grad(*loaded, cots[half], ((0, 1, 2, 3), (0, 3, 1, 2))[half])
         theirs.append(lax.ppermute(last, "fsdp", X_SWAP))
     mine_grad = kept_grad(blocks, wide_gain, x, cots, last)
     weight_grad = add_half(0, mine_grad, theirs[0], None)

time: 142 us -> 142 us (level)
  no operation moved by 1% of the time
where the time goes in v5:
time: 142 us; the launch traced here: 141 us
  waiting for transfers between devices  50 us (35%)
  Pallas kernels  48.8 us (34%)
  starting transfers between devices  39.5 us (28%)
  local copies, waits for them, and re-layouts  2 us (1%)
    ppermute x1, waiting for transfers between devices, per_device(): other = lax.ppermute(weight, 'fsdp', X_SWAP)  17.9 us
    ppermute x12, starting transfers between devices, send_y(): return lax.ppermute(block, 'fsdp', y_shift(step))  16.6 us
    all_to_all x1, waiting for transfers between devices, per_device(): frags = lax.all_to_all(fragment, 'rep', 0, 0, tiled=True)  13.1 us
    ppermute x12, waiting for transfers between devices, send_y(): return lax.ppermute(block, 'fsdp', y_shift(step))  9.91 us
    ppermute x2, waiting for transfers between devices, per_device(): theirs.append(lax.ppermute(last, 'fsdp', X_SWAP))  9.1 us
    all_to_all x1, starting transfers between devices, per_device(): frags = lax.all_to_all(fragment, 'rep', 0, 0, tiled=True)  8.81 us
    pallas_call x2, Pallas kernels, key_parts(): pl.pallas_call(functools.partial(part_kernel, count), in_specs=[HBM] * co...  8.12 us
    pallas_call x1, Pallas kernels, outer_step(): pl.pallas_call(functools.partial(outer_kernel, replicas), grid=(replicas...  7.12 us
  transfers between devices with their start and end apart: 18, of which 10 were waited for; matrix products, arithmetic and copies ran while one was open for 1% of the time, Pallas kernels for 32%

profile of v5, /device:TPU:32, one launch (start us, length us, event | category | flops | bytes accessed | tf_op | source)
XLA Modules:
  0.0 141.5 jit_solution(14897451038311933720)
XLA Ops:
  0.7 2.3 %cut.2.refs_2_ = bf16[2,384,1024]{2,1,0:T(8,128)(2,1)} custom-call(s32[1]{0:T(128)} %bitcast.2.at_ref, bf16[384,8192]{1,0:T(8,128)(2,1)} %bitcast.17), custom_call_target="tpu_custom_call" | custom-call | flops 999999995904 | bytes 1000000000 | tf_op jit(solution)/shard_map/cut/pallas_call | solution.py:213
  3.0 3.3 %collective-permute-start = (bf16[2,384,1024]{2,1,0:T(8,128)(2,1)}, bf16[2,384,1024]{2,1,0:T(8,128)(2,1)}, u32[]{:S(2)}, u32[]{:S(2)}) collective-permute-start(bf16[2,384,1024]{2,1,0:T(8,128)(2,1)} %cut.2.refs_2_), channel_id=1, source_target_pairs={{0,4},{1,5},{2,6},{3,7},{4,0},{5,1},{6,2},{7,3},{8,12},{9,13},{10,... | collective-permute-start | bytes 4718600 | tf_op jit(solution)/shard_map/ppermute | solution.py:38
  6.3 2.8 %behind.1 = (bf16[1024,1024]{1,0:T(8,128)(2,1)}, bf16[1024,512]{1,0:T(8,128)(2,1)}) custom-call(bf16[1024,1024]{1,0:T(8,128)(2,1)} %bitcast.20, bf16[1024,512]{1,0:T(8,128)(2,1)} %bitcast.21, bf16[2,384,1024]{2,1,0:T(8,128)(2,1)} %cut.2.refs_2_), custom_call_target="tpu_custom_call" | custom-call | flops 999999995904 | bytes 1000000000 | tf_op jit(solution)/shard_map/behind/pallas_call | solution.py:252
  9.1 3.1 %collective-permute-start.1 = (bf16[1024,512]{1,0:T(8,128)(2,1)}, bf16[1024,512]{1,0:T(8,128)(2,1)}, u32[]{:S(2)}, u32[]{:S(2)}) collective-permute-start(bf16[1024,512]{1,0:T(8,128)(2,1)} %get-tuple-element.21.weight_ref), channel_id=1, source_target_pairs={{0,1},{1,0},{2,3},{3,2},{4,5},{5,4},{6,7},{7,6},{8,9},{9,8},{10,11... | collective-permute-start | bytes 3145736 | tf_op jit(solution)/shard_map/ppermute | solution.py:562
  12.2 8.8 %all-to-all-start = ((bf16[32,32,1024]{2,1,0:T(8,128)(2,1)}), bf16[32,32,1024]{2,1,0:T(8,128)(2,1)}, u32[]{:S(2)}, u32[]{:S(2)}) async-start(bf16[32,32,1024]{2,1,0:T(8,128)(2,1)} %bitcast.4), calls=%async_computation | async-start | bytes 4194304 | tf_op jit(solution)/shard_map/all_to_all | solution.py:555
  21.0 0.1 pad_add_fusion.at_ref
  21.1 3.8 %cut.3 = (bf16[2,384,1024]{2,1,0:T(8,128)(2,1)}, bf16[2,384,1024]{2,1,0:T(8,128)(2,1)}, bf16[2,384,1024]{2,1,0:T(8,128)(2,1)S(1)}) custom-call(s32[3]{0:T(128)S(1)} %pad_add_fusion.at_ref, bf16[384,8192]{1,0:T(8,128)(2,1)} %bitcast.18, bf16[1024,1024]{1,0:T(8,128)(2,1)} %get-tuple-element.20.refs_0_), custom_call_target="tpu_custom_call" | custom-call | flops 999999995904 | bytes 1000000000 | tf_op jit(solution)/shard_map/cut/pallas_call | solution.py:213
  24.9 0.8 collective-permute-start.2
  25.7 2.6 %collective-permute-start.3 = (bf16[2,384,1024]{2,1,0:T(8,128)(2,1)}, bf16[2,384,1024]{2,1,0:T(8,128)(2,1)}, u32[]{:S(2)}, u32[]{:S(2)}) collective-permute-start(bf16[2,384,1024]{2,1,0:T(8,128)(2,1)} %get-tuple-element.28), channel_id=1, source_target_pairs={{0,6},{1,7},{2,0},{3,1},{4,2},{5,3},{6,4},{7,5},{8,14},{9,15},{10,... | collective-permute-start | bytes 4718600 | tf_op jit(solution)/shard_map/ppermute | solution.py:38
  28.2 0.7 dynamic_slice.3
  28.9 17.9 %collective-permute-done.1.other_ref = bf16[1024,512]{1,0:T(8,128)(2,1)} collective-permute-done((bf16[1024,512]{1,0:T(8,128)(2,1)}, bf16[1024,512]{1,0:T(8,128)(2,1)}, u32[]{:S(2)}, u32[]{:S(2)}) %collective-permute-start.1) | collective-permute-done | bytes 1048608 | tf_op jit(solution)/shard_map/ppermute | solution.py:562
  46.9 0.3 broadcast_in_dim.11.gain_ref.refs_4_
  47.2 2.3 %pair.1.weight_ref.refs_1_.refs_2_ = bf16[2,1024,512]{2,1,0:T(8,128)(2,1)S(1)} custom-call(s32[1]{0:T(128)} %bitcast.5.x_ref.half_ref, bf16[1024,512]{1,0:T(8,128)(2,1)} %get-tuple-element.21.weight_ref, bf16[1024,512]{1,0:T(8,128)(2,1)} %collective-permute-done.1.other_ref, f32[2,1024,128]{2,1,0:T(8,128)S(1)} %broadcast_in_dim.11.gain_ref.refs_4_), custom_call_target="tpu_custom_call" | custom-call | flops 999999995904 | bytes 1000000000 | tf_op jit(solution)/shard_map/pair/pallas_call | solution.py:275
  49.6 5.7 %own.1 = (f32[384,512]{1,0:T(8,128)S(1)}, f32[384,128]{1,0:T(8,128)S(1)}) custom-call(bf16[384,8192]{1,0:T(8,128)(2,1)} %bitcast.19, bf16[2,384,1024]{2,1,0:T(8,128)(2,1)S(1)} %get-tuple-element.22.block_ref.refs_0_, bf16[2,1024,512]{2,1,0:T(8,128)(2,1)S(1)} %pair.1.weight_ref.refs_1_.refs_2_, bf16[384,512]{1,0:T(8,128)(2,1)} %bitcast.22), custom_call_target="tpu_custom_call" | custom-call | flops 999999995904 | bytes 1000000000 | tf_op jit(solution)/shard_map/own/pallas_call | solution.py:304
  55.4 0.0 copy-start.5
  55.4 3.6 %part.2.refs_0_ = bf16[384,512]{1,0:T(8,128)(2,1)} custom-call(bf16[2,384,1024]{2,1,0:T(8,128)(2,1)} %collective-permute-done.refs_0_.refs_3_, bf16[2,1024,512]{2,1,0:T(8,128)(2,1)S(1)} %pair.1.weight_ref.refs_1_.refs_2_, f32[384,512]{1,0:T(8,128)S(1)} %get-tuple-element.23.refs_2_.refs_0_), custom_call_target="tpu_custom_call" | custom-call | flops 999999995904 | bytes 1000000000 | tf_op jit(solution)/shard_map/part/pallas_call | solution.py:357
  59.0 0.4 collective-permute-start.5
  59.5 13.1 %all-to-all-done.frag_ref = bf16[32,32,1024]{2,1,0:T(8,128)(2,1)} async-done(((bf16[32,32,1024]{2,1,0:T(8,128)(2,1)}), bf16[32,32,1024]{2,1,0:T(8,128)(2,1)}, u32[]{:S(2)}, u32[]{:S(2)}) %all-to-all-start) | async-done | bytes 2097184 | tf_op jit(solution)/shard_map/all_to_all | solution.py:555
  72.5 7.1 %outer.1 = (f32[32,1024]{1,0:T(8,128)}, f32[32,1024]{1,0:T(8,128)}, bf16[32,1024]{1,0:T(8,128)(2,1)S(1)}) custom-call(bf16[32,32,1024]{2,1,0:T(8,128)(2,1)} %all-to-all-done.frag_ref, f32[32,1024]{1,0:T(8,128)S(1)} %copy-done.4, f32[32,1024]{1,0:T(8,128)S(1)} %copy-done.5, bf16[384,512]{1,0:T(8,128)(2,1)} %part.2.refs_0_), custom_call_target="tpu_custom_call" | custom-call | flops 999999995904 | bytes 1000000000 | tf_op jit(solution)/shard_map/outer/pallas_call | solution.py:109
  79.7 4.5 %part.3 = (bf16[384,512]{1,0:T(8,128)(2,1)}, bf16[384,512]{1,0:T(8,128)(2,1)}) custom-call(bf16[2,384,1024]{2,1,0:T(8,128)(2,1)} %collective-permute-done.2.refs_0_.refs_1_, bf16[2,384,1024]{2,1,0:T(8,128)(2,1)} %collective-permute-done.3.refs_1_.refs_2_, bf16[2,1024,512]{2,1,0:T(8,128)(2,1)S(1)} %copy-done.7, ...), custom_call_target="tpu_custom_call" | custom-call | flops 999999995904 | bytes 1000000000 | tf_op jit(solution)/shard_map/part/pallas_call | solution.py:357
  84.2 1.1 collective-permute-start.6
  85.3 1.0 collective-permute-start.7
  86.3 1.0 spread.1.refs_5_
  87.3 6.7 %all-to-all-start.1 = ((bf16[16,32,1024]{2,1,0:T(8,128)(2,1)}), bf16[16,32,1024]{2,1,0:T(8,128)(2,1)}, u32[]{:S(2)}, u32[]{:S(2)}) async-start(bf16[16,32,1024]{2,1,0:T(8,128)(2,1)} %spread.1.refs_5_), calls=%async_computation.1 | async-start | bytes 2097152 | tf_op jit(solution)/shard_map/all_to_all | solution.py:580
  94.0 1.2 collective-permute-done.6.refs_3_
  95.2 2.0 %collective-permute-done.7.refs_4_ = bf16[384,512]{1,0:T(8,128)(2,1)} collective-permute-done((bf16[384,512]{1,0:T(8,128)(2,1)}, bf16[384,512]{1,0:T(8,128)(2,1)}, u32[]{:S(2)}, u32[]{:S(2)}) %collective-permute-start.7) | collective-permute-done | bytes 393248 | tf_op jit(solution)/shard_map/ppermute | solution.py:38
  97.2 1.8 %cot.1 = (bf16[256,384]{1,0:T(8,128)(2,1)S(1)}, bf16[256,384]{1,0:T(8,128)(2,1)S(1)}) custom-call(f32[384,512]{1,0:T(8,128)} %copy-done.8, f32[384,128]{1,0:T(8,128)} %copy-done.9, bf16[384,512]{1,0:T(8,128)(2,1)} %collective-permute-done.5.refs_2_, bf16[384,512]{1,0:T(8,128)(2,1)} %collective-permute-done.6.refs_3_, ...), custom_call_target="tpu_custom_call" | custom-call | flops 999999995904 | bytes 1000000000 | tf_op jit(solution)/shard_map/cot/pallas_call | solution.py:400
  99.1 0.6 collective-permute-start.10
  99.6 0.7 collective-permute-start.8
  100.3 2.6 %collective-permute-start.9 = (bf16[256,384]{1,0:T(8,128)(2,1)S(1)}, bf16[256,384]{1,0:T(8,128)(2,1)S(1)}, u32[]{:S(2)}, u32[]{:S(2)}) collective-permute-start(bf16[256,384]{1,0:T(8,128)(2,1)S(1)} %get-tuple-element.32.refs_5_.refs_0_), channel_id=1, source_target_pairs={{0,6},{1,7},{2,0},{3,1},{4,2},{5,3},{6,4},{7,5},{8,14},{9,15},{10,... | collective-permute-start | bytes 589832 | tf_op jit(solution)/shard_map/ppermute | solution.py:38
  102.9 3.2 %collective-permute-start.12 = (bf16[256,384]{1,0:T(8,128)(2,1)S(1)}, bf16[256,384]{1,0:T(8,128)(2,1)S(1)}, u32[]{:S(2)}, u32[]{:S(2)}) collective-permute-start(bf16[256,384]{1,0:T(8,128)(2,1)S(1)} %get-tuple-element.33.refs_0_.refs_9_), channel_id=1, source_target_pairs={{0,6},{1,7},{2,0},{3,1},{4,2},{5,3},{6,4},{7,5},{8,14},{9,15},{10,... | collective-permute-start | bytes 589832 | tf_op jit(solution)/shard_map/ppermute | solution.py:38
  106.1 2.0 %load.1 = (bf16[1536,1024]{1,0:T(8,128)(2,1)S(1)}, f32[1024,128]{1,0:T(8,128)S(1)}) custom-call(s32[1]{0:T(128)} %bitcast.12.half_ref, bf16[2,384,1024]{2,1,0:T(8,128)(2,1)} %copy-done.1, bf16[2,384,1024]{2,1,0:T(8,128)(2,1)} %collective-permute-done.2.refs_0_.refs_1_, bf16[2,384,1024]{2,1,0:T(8,128)(2,1)} %collective-permute-done.3.refs_1_.refs_2_, ...), custom_call_target="tpu_custom_call" | custom-call | tf_op jit(solution)/shard_map/load/pallas_call | solution.py:472
  108.2 0.3 collective-permute-done.10.refs_8_.refs_3_
  108.5 0.5 collective-permute-start.13
  109.0 1.8 %collective-permute-done.8.refs_6_.refs_1_ = bf16[256,384]{1,0:T(8,128)(2,1)S(1)} collective-permute-done((bf16[256,384]{1,0:T(8,128)(2,1)S(1)}, bf16[256,384]{1,0:T(8,128)(2,1)S(1)}, u32[]{:S(2)}, u32[]{:S(2)}) %collective-permute-start.8) | collective-permute-done | bytes 196640 | tf_op jit(solution)/shard_map/ppermute | solution.py:38
  110.7 1.1 grad.3
  111.9 2.1 %collective-permute-start.15 = (bf16[1024,256]{1,0:T(8,128)(2,1)S(1)}, bf16[1024,256]{1,0:T(8,128)(2,1)S(1)}, u32[]{:S(2)}, u32[]{:S(2)}) collective-permute-start(bf16[1024,256]{1,0:T(8,128)(2,1)S(1)} %grad.3), channel_id=1, source_target_pairs={{0,1},{1,0},{2,3},{3,2},{4,5},{5,4},{6,7},{7,6},{8,9},{9,8},{10,11... | collective-permute-start | bytes 1572872 | tf_op jit(solution)/shard_map/ppermute | solution.py:596
  114.0 2.3 %collective-permute-done.11.refs_2_.refs_10_ = bf16[256,384]{1,0:T(8,128)(2,1)S(1)} collective-permute-done((bf16[256,384]{1,0:T(8,128)(2,1)S(1)}, bf16[256,384]{1,0:T(8,128)(2,1)S(1)}, u32[]{:S(2)}, u32[]{:S(2)}) %collective-permute-start.11) | collective-permute-done | bytes 196640 | tf_op jit(solution)/shard_map/ppermute | solution.py:38
  116.4 2.2 %collective-permute-done.13.refs_1_.refs_12_ = bf16[256,384]{1,0:T(8,128)(2,1)S(1)} collective-permute-done((bf16[256,384]{1,0:T(8,128)(2,1)S(1)}, bf16[256,384]{1,0:T(8,128)(2,1)S(1)}, u32[]{:S(2)}, u32[]{:S(2)}) %collective-permute-start.13) | collective-permute-done | bytes 196640 | tf_op jit(solution)/shard_map/ppermute | solution.py:38
  118.6 1.1 grad.2.refs_13_
  119.7 2.1 %collective-permute-start.14 = (bf16[1024,256]{1,0:T(8,128)(2,1)S(1)}, bf16[1024,256]{1,0:T(8,128)(2,1)S(1)}, u32[]{:S(2)}, u32[]{:S(2)}) collective-permute-start(bf16[1024,256]{1,0:T(8,128)(2,1)S(1)} %grad.2.refs_13_), channel_id=1, source_target_pairs={{0,1},{1,0},{2,3},{3,2},{4,5},{5,4},{6,7},{7,6},{8,9},{9,8},{10,11... | collective-permute-start | bytes 1572872 | tf_op jit(solution)/shard_map/ppermute | solution.py:596
  121.8 0.9 copy-done.3
  122.8 4.0 %kept.1.own_ref = f32[1024,512]{1,0:T(8,128)S(1)} custom-call(s32[1]{0:T(128)} %bitcast.5.x_ref.half_ref, bf16[2,384,1024]{2,1,0:T(8,128)(2,1)} %copy-done.1, bf16[2,384,1024]{2,1,0:T(8,128)(2,1)} %collective-permute-done.2.refs_0_.refs_1_, bf16[2,384,1024]{2,1,0:T(8,128)(2,1)} %collective-permute-done.3.refs_1_.refs_2_, ...), custom_call_target="tpu_custom_call" | custom-call | flops 20000000000 | bytes 1000000 | tf_op jit(solution)/shard_map/kept/pallas_call | solution.py:522
  126.7 2.6 %collective-permute-done.15.theirs_ref = bf16[1024,256]{1,0:T(8,128)(2,1)S(1)} collective-permute-done((bf16[1024,256]{1,0:T(8,128)(2,1)S(1)}, bf16[1024,256]{1,0:T(8,128)(2,1)S(1)}, u32[]{:S(2)}, u32[]{:S(2)}) %collective-permute-start.15) | collective-permute-done | bytes 524320 | tf_op jit(solution)/shard_map/ppermute | solution.py:596
  129.4 1.5 %add.32.refs_0_ = bf16[1024,512]{1,0:T(8,128)(2,1)} custom-call(f32[1024,512]{1,0:T(8,128)S(1)} %kept.1.own_ref, bf16[1024,256]{1,0:T(8,128)(2,1)S(1)} %collective-permute-done.15.theirs_ref), custom_call_target="tpu_custom_call" | custom-call | tf_op jit(solution)/shard_map/add/pallas_call | solution.py:435
  130.9 2.4 %merge.1 = bf16[16,2,32,1024]{3,2,1,0:T(8,128)(2,1)} custom-call(s32[1]{0:T(128)} %bitcast.10.core_ref, bf16[16,32,1024]{2,1,0:T(8,128)(2,1)} %all-to-all-done.1.mine_ref, bf16[16,32,1024]{2,1,0:T(8,128)(2,1)S(1)} %collective-permute-done.4.theirs_ref), custom_call_target="tpu_custom_call" | custom-call | tf_op jit(solution)/shard_map/merge/pallas_call | solution.py:171
  133.3 6.5 %collective-permute-done.14.theirs_ref = bf16[1024,256]{1,0:T(8,128)(2,1)S(1)} collective-permute-done((bf16[1024,256]{1,0:T(8,128)(2,1)S(1)}, bf16[1024,256]{1,0:T(8,128)(2,1)S(1)}, u32[]{:S(2)}, u32[]{:S(2)}) %collective-permute-start.14) | collective-permute-done | bytes 524320 | tf_op jit(solution)/shard_map/ppermute | solution.py:596
  139.8 1.5 %add.33 = bf16[1024,512]{1,0:T(8,128)(2,1)} custom-call(f32[1024,512]{1,0:T(8,128)S(1)} %kept.1.own_ref, bf16[1024,256]{1,0:T(8,128)(2,1)S(1)} %collective-permute-done.14.theirs_ref, bf16[1024,512]{1,0:T(8,128)(2,1)} %add.32.refs_0_, bf16[1024,1024]{1,0:T(8,128)(2,1)} %bitcast.14), custom_call_target="tpu_custom_call", output_to_operand_aliasing={{}: (2, {})} | custom-call | tf_op jit(solution)/shard_map/add/pallas_call | solution.py:435
  (29 shorter events, 0.1 us)
Async XLA Ops:
  3.0 52.4 %collective-permute-start = (bf16[2,384,1024]{2,1,0:T(8,128)(2,1)}, bf16[2,384,1024]{2,1,0:T(8,128)(2,1)}, u32[]{:S(2)}, u32[]{:S(2)}) collective-permute-start(bf16[2,384,1024]{2,1,0:T(8,128)(2,1)} %cut.2.refs_2_), channel_id=1, source_target_pairs={{0,4},{1,5},{2,6},{3,7},{4,0},{5,1},{6,2},{7,3},{8,12},{9,13},{10,... | collective-permute-start | bytes 4718600 | tf_op jit(solution)/shard_map/ppermute | solution.py:38
  9.1 37.8 %collective-permute-start.1 = (bf16[1024,512]{1,0:T(8,128)(2,1)}, bf16[1024,512]{1,0:T(8,128)(2,1)}, u32[]{:S(2)}, u32[]{:S(2)}) collective-permute-start(bf16[1024,512]{1,0:T(8,128)(2,1)} %get-tuple-element.21.weight_ref), channel_id=1, source_target_pairs={{0,1},{1,0},{2,3},{3,2},{4,5},{5,4},{6,7},{7,6},{8,9},{9,8},{10,11... | collective-permute-start | bytes 3145736 | tf_op jit(solution)/shard_map/ppermute | solution.py:562
  12.2 60.3 %all-to-all-start = ((bf16[32,32,1024]{2,1,0:T(8,128)(2,1)}), bf16[32,32,1024]{2,1,0:T(8,128)(2,1)}, u32[]{:S(2)}, u32[]{:S(2)}) async-start(bf16[32,32,1024]{2,1,0:T(8,128)(2,1)} %bitcast.4), calls=%async_computation | async-start | bytes 4194304 | tf_op jit(solution)/shard_map/all_to_all | solution.py:555
  24.9 24.7 %copy-start.1 = (bf16[2,384,1024]{2,1,0:T(8,128)(2,1)}, bf16[2,384,1024]{2,1,0:T(8,128)(2,1)S(1)}, u32[]{:S(2)}) copy-start(bf16[2,384,1024]{2,1,0:T(8,128)(2,1)S(1)} %get-tuple-element.22.block_ref.refs_0_) | copy-start | bytes 4718596
  24.9 54.8 %collective-permute-start.2 = (bf16[2,384,1024]{2,1,0:T(8,128)(2,1)}, bf16[2,384,1024]{2,1,0:T(8,128)(2,1)}, u32[]{:S(2)}, u32[]{:S(2)}) collective-permute-start(bf16[2,384,1024]{2,1,0:T(8,128)(2,1)} %get-tuple-element.27), channel_id=1, source_target_pairs={{0,2},{1,3},{2,4},{3,5},{4,6},{5,7},{6,0},{7,1},{8,10},{9,11},{10,... | collective-permute-start | bytes 4718600 | tf_op jit(solution)/shard_map/ppermute | solution.py:38
  25.7 54.0 %collective-permute-start.3 = (bf16[2,384,1024]{2,1,0:T(8,128)(2,1)}, bf16[2,384,1024]{2,1,0:T(8,128)(2,1)}, u32[]{:S(2)}, u32[]{:S(2)}) collective-permute-start(bf16[2,384,1024]{2,1,0:T(8,128)(2,1)} %get-tuple-element.28), channel_id=1, source_target_pairs={{0,6},{1,7},{2,0},{3,1},{4,2},{5,3},{6,4},{7,5},{8,14},{9,15},{10,... | collective-permute-start | bytes 4718600 | tf_op jit(solution)/shard_map/ppermute | solution.py:38
  47.2 2.3 %copy-start = (f32[2,1024,128]{2,1,0:T(8,128)}, f32[2,1024,128]{2,1,0:T(8,128)S(1)}, u32[]{:S(2)}) copy-start(f32[2,1024,128]{2,1,0:T(8,128)S(1)} %broadcast_in_dim.11.gain_ref.refs_4_) | copy-start | bytes 3145732
  49.5 5.8 %copy-start.6 = (bf16[2,1024,512]{2,1,0:T(8,128)(2,1)}, bf16[2,1024,512]{2,1,0:T(8,128)(2,1)S(1)}, u32[]{:S(2)}) copy-start(bf16[2,1024,512]{2,1,0:T(8,128)(2,1)S(1)} %pair.1.weight_ref.refs_1_.refs_2_) | copy-start | bytes 6291460
  55.3 3.7 %copy-start.8 = (f32[384,512]{1,0:T(8,128)}, f32[384,512]{1,0:T(8,128)S(1)}, u32[]{:S(2)}) copy-start(f32[384,512]{1,0:T(8,128)S(1)} %get-tuple-element.23.refs_2_.refs_0_) | copy-start | bytes 2359300
  55.3 3.7 %copy-start.9 = (f32[384,128]{1,0:T(8,128)}, f32[384,128]{1,0:T(8,128)S(1)}, u32[]{:S(2)}) copy-start(f32[384,128]{1,0:T(8,128)S(1)} %get-tuple-element.30.refs_1_) | copy-start | bytes 589828
  55.4 17.2 %copy-start.4 = (f32[32,1024]{1,0:T(8,128)S(1)}, f32[32,1024]{1,0:T(8,128)}, u32[]{:S(2)}) copy-start(f32[32,1024]{1,0:T(8,128)} %params_ref.1) | copy-start | bytes 393220
  55.4 17.2 %copy-start.5 = (f32[32,1024]{1,0:T(8,128)S(1)}, f32[32,1024]{1,0:T(8,128)}, u32[]{:S(2)}) copy-start(f32[32,1024]{1,0:T(8,128)} %moment_ref.1) | copy-start | bytes 393220
  59.0 35.0 %collective-permute-start.5 = (bf16[384,512]{1,0:T(8,128)(2,1)}, bf16[384,512]{1,0:T(8,128)(2,1)}, u32[]{:S(2)}, u32[]{:S(2)}) collective-permute-start(bf16[384,512]{1,0:T(8,128)(2,1)} %part.2.refs_0_), channel_id=1, source_target_pairs={{0,4},{1,5},{2,6},{3,7},{4,0},{5,1},{6,2},{7,3},{8,12},{9,13},{10,... | collective-permute-start | bytes 1179656 | tf_op jit(solution)/shard_map/ppermute | solution.py:38
  72.5 7.1 %copy-start.7 = (bf16[2,1024,512]{2,1,0:T(8,128)(2,1)S(1)}, bf16[2,1024,512]{2,1,0:T(8,128)(2,1)}, u32[]{:S(2)}) copy-start(bf16[2,1024,512]{2,1,0:T(8,128)(2,1)} %copy-done.6) | copy-start | bytes 6291460
  84.2 11.1 %collective-permute-start.6 = (bf16[384,512]{1,0:T(8,128)(2,1)}, bf16[384,512]{1,0:T(8,128)(2,1)}, u32[]{:S(2)}, u32[]{:S(2)}) collective-permute-start(bf16[384,512]{1,0:T(8,128)(2,1)} %get-tuple-element.31), channel_id=1, source_target_pairs={{0,6},{1,7},{2,0},{3,1},{4,2},{5,3},{6,4},{7,5},{8,14},{9,15},{10,... | collective-permute-start | bytes 1179656 | tf_op jit(solution)/shard_map/ppermute | solution.py:38
  85.3 11.9 %collective-permute-start.7 = (bf16[384,512]{1,0:T(8,128)(2,1)}, bf16[384,512]{1,0:T(8,128)(2,1)}, u32[]{:S(2)}, u32[]{:S(2)}) collective-permute-start(bf16[384,512]{1,0:T(8,128)(2,1)} %get-tuple-element.29.refs_0_), channel_id=1, source_target_pairs={{0,2},{1,3},{2,4},{3,5},{4,6},{5,7},{6,0},{7,1},{8,10},{9,11},{10,... | collective-permute-start | bytes 1179656 | tf_op jit(solution)/shard_map/ppermute | solution.py:38
  87.3 34.5 %all-to-all-start.1 = ((bf16[16,32,1024]{2,1,0:T(8,128)(2,1)}), bf16[16,32,1024]{2,1,0:T(8,128)(2,1)}, u32[]{:S(2)}, u32[]{:S(2)}) async-start(bf16[16,32,1024]{2,1,0:T(8,128)(2,1)} %spread.1.refs_5_), calls=%async_computation.1 | async-start | bytes 2097152 | tf_op jit(solution)/shard_map/all_to_all | solution.py:580
  99.1 9.4 %collective-permute-start.10 = (bf16[256,384]{1,0:T(8,128)(2,1)S(1)}, bf16[256,384]{1,0:T(8,128)(2,1)S(1)}, u32[]{:S(2)}, u32[]{:S(2)}) collective-permute-start(bf16[256,384]{1,0:T(8,128)(2,1)S(1)} %get-tuple-element.32.refs_5_.refs_0_), channel_id=1, source_target_pairs={{0,4},{1,5},{2,6},{3,7},{4,0},{5,1},{6,2},{7,3},{8,12},{9,13},{10,... | collective-permute-start | bytes 589832 | tf_op jit(solution)/shard_map/ppermute | solution.py:38
  99.6 11.1 %collective-permute-start.8 = (bf16[256,384]{1,0:T(8,128)(2,1)S(1)}, bf16[256,384]{1,0:T(8,128)(2,1)S(1)}, u32[]{:S(2)}, u32[]{:S(2)}) collective-permute-start(bf16[256,384]{1,0:T(8,128)(2,1)S(1)} %get-tuple-element.32.refs_5_.refs_0_), channel_id=1, source_target_pairs={{0,2},{1,3},{2,4},{3,5},{4,6},{5,7},{6,0},{7,1},{8,10},{9,11},{10,... | collective-permute-start | bytes 589832 | tf_op jit(solution)/shard_map/ppermute | solution.py:38
  100.3 10.4 %collective-permute-start.9 = (bf16[256,384]{1,0:T(8,128)(2,1)S(1)}, bf16[256,384]{1,0:T(8,128)(2,1)S(1)}, u32[]{:S(2)}, u32[]{:S(2)}) collective-permute-start(bf16[256,384]{1,0:T(8,128)(2,1)S(1)} %get-tuple-element.32.refs_5_.refs_0_), channel_id=1, source_target_pairs={{0,6},{1,7},{2,0},{3,1},{4,2},{5,3},{6,4},{7,5},{8,14},{9,15},{10,... | collective-permute-start | bytes 589832 | tf_op jit(solution)/shard_map/ppermute | solution.py:38
  102.9 13.5 %collective-permute-start.11 = (bf16[256,384]{1,0:T(8,128)(2,1)S(1)}, bf16[256,384]{1,0:T(8,128)(2,1)S(1)}, u32[]{:S(2)}, u32[]{:S(2)}) collective-permute-start(bf16[256,384]{1,0:T(8,128)(2,1)S(1)} %get-tuple-element.33.refs_0_.refs_9_), channel_id=1, source_target_pairs={{0,2},{1,3},{2,4},{3,5},{4,6},{5,7},{6,0},{7,1},{8,10},{9,11},{10,... | collective-permute-start | bytes 589832 | tf_op jit(solution)/shard_map/ppermute | solution.py:38
  102.9 13.5 %collective-permute-start.12 = (bf16[256,384]{1,0:T(8,128)(2,1)S(1)}, bf16[256,384]{1,0:T(8,128)(2,1)S(1)}, u32[]{:S(2)}, u32[]{:S(2)}) collective-permute-start(bf16[256,384]{1,0:T(8,128)(2,1)S(1)} %get-tuple-element.33.refs_0_.refs_9_), channel_id=1, source_target_pairs={{0,6},{1,7},{2,0},{3,1},{4,2},{5,3},{6,4},{7,5},{8,14},{9,15},{10,... | collective-permute-start | bytes 589832 | tf_op jit(solution)/shard_map/ppermute | solution.py:38
  108.5 10.1 %collective-permute-start.13 = (bf16[256,384]{1,0:T(8,128)(2,1)S(1)}, bf16[256,384]{1,0:T(8,128)(2,1)S(1)}, u32[]{:S(2)}, u32[]{:S(2)}) collective-permute-start(bf16[256,384]{1,0:T(8,128)(2,1)S(1)} %get-tuple-element.33.refs_0_.refs_9_), channel_id=1, source_target_pairs={{0,4},{1,5},{2,6},{3,7},{4,0},{5,1},{6,2},{7,3},{8,12},{9,13},{10,... | collective-permute-start | bytes 589832 | tf_op jit(solution)/shard_map/ppermute | solution.py:38
  111.9 17.5 %collective-permute-start.15 = (bf16[1024,256]{1,0:T(8,128)(2,1)S(1)}, bf16[1024,256]{1,0:T(8,128)(2,1)S(1)}, u32[]{:S(2)}, u32[]{:S(2)}) collective-permute-start(bf16[1024,256]{1,0:T(8,128)(2,1)S(1)} %grad.3), channel_id=1, source_target_pairs={{0,1},{1,0},{2,3},{3,2},{4,5},{5,4},{6,7},{7,6},{8,9},{9,8},{10,11... | collective-permute-start | bytes 1572872 | tf_op jit(solution)/shard_map/ppermute | solution.py:596
  118.6 1.1 copy-start.2
  119.7 20.1 %collective-permute-start.14 = (bf16[1024,256]{1,0:T(8,128)(2,1)S(1)}, bf16[1024,256]{1,0:T(8,128)(2,1)S(1)}, u32[]{:S(2)}, u32[]{:S(2)}) collective-permute-start(bf16[1024,256]{1,0:T(8,128)(2,1)S(1)} %grad.2.refs_13_), channel_id=1, source_target_pairs={{0,1},{1,0},{2,3},{3,2},{4,5},{5,4},{6,7},{7,6},{8,9},{9,8},{10,11... | collective-permute-start | bytes 1572872 | tf_op jit(solution)/shard_map/ppermute | solution.py:596
  121.8 9.1 %collective-permute-start.4 = (bf16[16,32,1024]{2,1,0:T(8,128)(2,1)}, bf16[16,32,1024]{2,1,0:T(8,128)(2,1)S(1)}, u32[]{:S(2)}, u32[]{:S(2)}) collective-permute-start(bf16[16,32,1024]{2,1,0:T(8,128)(2,1)} %all-to-all-done.1.mine_ref), channel_id=1, source_target_pairs={{0,8},{8,0},{16,24},{24,16},{32,40},{40,32},{48,56},{56,48},{64,72... | collective-permute-start | bytes 3145736 | tf_op jit(solution)/shard_map/ppermute | solution.py:588
  121.8 0.9 copy-start.3
